TPU v7x, 512 devices: a whole 4x8x8 slice. The times are simulated.
512 devices in a mesh: rep: 32 (over x, z), exp: 16 (over y, core).
Axes of the slice: x: 4, y: 8, z: 8, core: 2. Of those that a mesh axis runs over, the one named last changes fastest.
Arguments:
- tokens: bfloat16 [65536, 2048], P(('rep', 'exp')), may hold values from -6 to 6
- expert_ids: int32 [65536, 1], P(('rep', 'exp')), may hold values from 0 to 3; in each aligned block of 128 rows (0 to 127, 128 to 255, ...) at most 32 rows name the same one
- gate_prob: float32 [65536], P(('rep', 'exp')), may hold values from 0.05 to 1
- cotangent: bfloat16 [65536, 2048], P(('rep', 'exp')), may hold values from -6 to 6
- w_gate: bfloat16 [32, 2048, 4096], P('rep', None, 'exp'), may hold values from -0.125 to 0.125
- w_up: bfloat16 [32, 2048, 4096], P('rep', None, 'exp'), may hold values from -0.125 to 0.125
- w_down: bfloat16 [32, 4096, 2048], P('rep', 'exp'), may hold values from -0.1875 to 0.1875
- touched: int32 [32, 256], P('rep', 'exp'), may hold values 0 or 1
Outputs:
- mixed: bfloat16 [65536, 2048], P(('rep', 'exp'))
- averaged: bfloat16 [4096, 6144], P('exp', 'rep')
Inputs may be any that keep to these rules, and one draw needn't show every extreme that they name: `expert_ids`: the rows of one device name each of the 4 window experts exactly 32 times.
All inputs are finite; a program needn't handle non-finite values. No bound on the sum of `touched` on one device may be relied on, other than what follows from the above.
Results may differ from a plain program's by a relative error of at most 0.018.
Values may be sent and summed in bfloat16 or wider, within the bound.
No kernel may reach another device: no remote copies, remote signals or barrier semaphores. Data moves between devices by JAX's collectives and lax.ppermute only.
A program may use at most 64 MiB of HBM per device.

v0:
```python
import jax
import jax.numpy as jnp
from jax import lax
from jax.sharding import PartitionSpec as P

EW = 4
TILE = 16


def swish_slope(h):
    s = jax.nn.sigmoid(h)
    return s * (1.0 + h * (1.0 - s))


def body(tokens, expert_ids, gate_prob, cotangent, w_gate, w_up, w_down, touched):
    rows = tokens.shape[0]
    width = tokens.shape[1]
    n_exp = lax.axis_size("exp")
    n_rep = lax.axis_size("rep")
    shards = n_exp // EW
    cap = rows // EW
    onehot = (expert_ids == jnp.arange(EW)[None, :]).astype(jnp.float32)
    lower = (
        lax.broadcasted_iota(jnp.int32, (rows, rows), 0)
        > lax.broadcasted_iota(jnp.int32, (rows, rows), 1)
    ).astype(jnp.float32)
    earlier = jnp.dot(lower, onehot, precision=lax.Precision.HIGHEST)
    slot_of = jnp.sum(onehot * earlier, axis=1).astype(jnp.int32)
    target = expert_ids[:, 0] * cap + slot_of
    placer = (target[None, :] == jnp.arange(EW * cap)[:, None]).astype(jnp.bfloat16)
    dy = (gate_prob[:, None] * cotangent.astype(jnp.float32)).astype(jnp.bfloat16)
    x_buf = (
        jnp.dot(placer, tokens, preferred_element_type=jnp.float32)
        .astype(jnp.bfloat16)
        .reshape(EW, cap, width)
    )
    d_buf = (
        jnp.dot(placer, dy, preferred_element_type=jnp.float32)
        .astype(jnp.bfloat16)
        .reshape(EW, cap, width)
    )
    x_recv, d_recv = (
        lax.all_to_all(
            jnp.repeat(x_buf, shards, axis=0), "exp", split_axis=0, concat_axis=0, tiled=True
        ),
        lax.all_to_all(
            jnp.repeat(d_buf, shards, axis=0), "exp", split_axis=0, concat_axis=0, tiled=True
        ),
    )
    x_rows = x_recv.reshape(n_exp * cap, width)
    d_rows = d_recv.reshape(n_exp * cap, width)
    wg = w_gate[0]
    wu = w_up[0]
    wd = w_down[0]
    h = jnp.dot(x_rows, wg, preferred_element_type=jnp.float32)
    u = jnp.dot(x_rows, wu, preferred_element_type=jnp.float32)
    act = (h * jax.nn.sigmoid(h) * u).astype(jnp.bfloat16)
    partial_out = jnp.dot(act, wd, preferred_element_type=jnp.float32).astype(jnp.bfloat16)
    returned = lax.all_to_all(
        partial_out.reshape(n_exp, cap, width), "exp", split_axis=0, concat_axis=0, tiled=True
    )
    summed = returned.astype(jnp.float32).reshape(EW, shards, cap, width).sum(axis=1)
    row_out = jnp.take(summed.reshape(EW * cap, width), target, axis=0)
    mixed = (gate_prob[:, None] * row_out).astype(jnp.bfloat16)
    grad_a = lax.dot_general(
        d_rows, wd, (((1,), (1,)), ((), ())), preferred_element_type=jnp.float32
    )
    d_down = lax.dot_general(
        act, d_rows, (((0,), (0,)), ((), ())), preferred_element_type=jnp.float32
    )
    d_h = (grad_a * u * swish_slope(h)).astype(jnp.bfloat16)
    d_u = (grad_a * h * jax.nn.sigmoid(h)).astype(jnp.bfloat16)
    d_gate = lax.dot_general(
        d_h, x_rows, (((0,), (0,)), ((), ())), preferred_element_type=jnp.float32
    )
    d_upper = lax.dot_general(
        d_u, x_rows, (((0,), (0,)), ((), ())), preferred_element_type=jnp.float32
    )
    delta = jnp.concatenate([d_gate, d_upper, d_down], axis=1)
    weight_rows = jnp.repeat(touched[0].astype(jnp.float32), TILE)
    masked = delta * weight_rows[:, None]
    columns = delta.shape[1] // n_rep
    total = lax.psum(masked.astype(jnp.bfloat16), "rep").astype(jnp.float32)
    share = lax.dynamic_slice_in_dim(total, lax.axis_index("rep") * columns, columns, 1)
    averaged = (share / n_rep).astype(jnp.bfloat16)
    return (mixed, averaged)


def solution(mesh):
    return jax.shard_map(
        body,
        mesh=mesh,
        in_specs=(
            P(("rep", "exp"), None),
            P(("rep", "exp"), None),
            P(("rep", "exp")),
            P(("rep", "exp"), None),
            P("rep", None, "exp"),
            P("rep", None, "exp"),
            P("rep", "exp", None),
            P("rep", "exp"),
        ),
        out_specs=(P(("rep", "exp"), None), P("exp", "rep")),
        check_vma=False,
    )
```

profile of v0, /device:TPU:1, one launch (start us, length us, event | category | flops | bytes accessed | tf_op | source)
XLA Modules:
  0.0 330.9 jit_solution(8879640322844170862)
XLA Ops:
  7.2 0.0 copy-start
  7.2 0.9 fusion.1
  8.1 0.7 multiply_add_fusion
  8.8 1.3 convolution_convert_fusion.2
  10.1 1.6 broadcast_in_dim.25
  11.7 10.5 %all-to-all-start = ((bf16[16,32,2048]{2,1,0:T(8,128)(2,1)}), bf16[16,32,2048]{2,1,0:T(8,128)(2,1)S(1)}, u32[]{:S(2)}, u32[]{:S(2)}) async-start(bf16[16,32,2048]{2,1,0:T(8,128)(2,1)} %bitcast.51), calls=%async_computation | async-start | bytes 4194304 | tf_op jit(solution)/shard_map/all_to_all | solution.py:43
  22.2 2.2 convolution_convert_fusion.1
  24.4 46.8 %all-to-all-done = bf16[16,32,2048]{2,1,0:T(8,128)(2,1)S(1)} async-done(((bf16[16,32,2048]{2,1,0:T(8,128)(2,1)}), bf16[16,32,2048]{2,1,0:T(8,128)(2,1)S(1)}, u32[]{:S(2)}, u32[]{:S(2)}) %all-to-all-start) | async-done | bytes 2097184 | tf_op jit(solution)/shard_map/all_to_all | solution.py:43
  71.2 2.6 broadcast_in_dim.27
  73.8 5.1 %all-to-all-start.2 = ((bf16[16,32,2048]{2,1,0:T(8,128)(2,1)}), bf16[16,32,2048]{2,1,0:T(8,128)(2,1)}, u32[]{:S(2)}, u32[]{:S(2)}) async-start(bf16[16,32,2048]{2,1,0:T(8,128)(2,1)} %bitcast.50), calls=%async_computation.2 | async-start | bytes 4194304 | tf_op jit(solution)/shard_map/all_to_all | solution.py:46
  79.0 0.1 broadcast_in_dim.28
  79.0 0.1 mul.86
  79.1 2.0 fusion.7
  81.2 0.8 copy-done.2
  82.0 1.5 multiply_convert_fusion.5
  83.5 44.5 %all-to-all-done.2 = bf16[16,32,2048]{2,1,0:T(8,128)(2,1)} async-done(((bf16[16,32,2048]{2,1,0:T(8,128)(2,1)}), bf16[16,32,2048]{2,1,0:T(8,128)(2,1)}, u32[]{:S(2)}, u32[]{:S(2)}) %all-to-all-start.2) | async-done | bytes 2097184 | tf_op jit(solution)/shard_map/all_to_all | solution.py:46
  128.0 2.3 fusion.2
  130.4 3.7 %fusion.19 = f32[256,2048]{1,0:T(8,128)} fusion(bf16[512,256]{1,0:T(8,128)(2,1)S(1)} %get-tuple-element.6, bf16[512,2048]{1,0:T(8,128)(2,1)} %bitcast.15), kind=kOutput, calls=%fused_computation.42 | convolution fusion | flops 536870912 | bytes 4456448 | tf_op jit(solution)/shard_map/dot_general | solution.py:68
  134.0 2.1 convolution_convert_fusion
  136.1 2.1 fusion.11
  138.2 2.2 fusion.10
  140.4 5.1 %all-to-all-start.1 = ((bf16[16,32,2048]{2,1,0:T(8,128)(2,1)}), bf16[16,32,2048]{2,1,0:T(8,128)(2,1)}, u32[]{:S(2)}, u32[]{:S(2)}) async-start(bf16[16,32,2048]{2,1,0:T(8,128)(2,1)} %bitcast.52), calls=%async_computation.1 | async-start | bytes 4194304 | tf_op jit(solution)/shard_map/all_to_all | solution.py:59
  145.5 0.0 all-reduce.2.cloned.1.call-start
  145.6 3.6 %fusion = bf16[256,6144]{1,0:T(8,128)(2,1)} fusion(f32[256,2048]{1,0:T(8,128)S(1)} %copy-done.1, f32[256,2048]{1,0:T(8,128)} %fusion.11, f32[256,2048]{1,0:T(8,128)} %fusion.10, f32[256]{0:T(256)S(1)} %mul.86), kind=kLoop, calls=%fused_computation.2 | loop fusion | flops 6291456 | bytes 9438208 | tf_op jit(solution)/shard_map/convert_element_type | solution.py:83
  149.2 0.0 all-reduce.2.cloned.1.call-update
  149.2 0.6 copy-done.6
  149.9 168.3 %all-reduce.2.cloned.1.call-done = bf16[256,6144]{1,0:T(8,128)(2,1)} async-done(((bf16[256,6144]{1,0:T(8,128)(2,1)}), bf16[256,6144]{1,0:T(8,128)(2,1)}) %all-reduce.2.cloned.1.call-update) | async-done | bytes 3145744 | tf_op jit(solution)/shard_map/psum | solution.py:83
  318.2 1.0 multiply_convert_fusion.8
  319.2 0.7 copy.10
  320.0 2.1 convert_reduce_fusion
  322.1 1.0 gather_fusion
  323.1 1.0 multiply_convert_fusion.1
  (19 shorter events, 0.1 us)
Async XLA Ops:
  7.2 120.8 %copy-start = (bf16[1,256,2048]{2,1,0:T(8,128)(2,1)S(1)}, bf16[1,256,2048]{2,1,0:T(8,128)(2,1)}, u32[]{:S(2)}) copy-start(bf16[1,256,2048]{2,1,0:T(8,128)(2,1)} %param.14) | copy-start | bytes 3145732
  11.7 10.5 %copy-start.5 = (f32[128]{0:T(128)S(1)}, f32[128]{0:T(128)}, u32[]{:S(2)}) copy-start(f32[128]{0:T(128)} %param.10) | copy-start | bytes 1540
  11.7 59.5 %all-to-all-start = ((bf16[16,32,2048]{2,1,0:T(8,128)(2,1)}), bf16[16,32,2048]{2,1,0:T(8,128)(2,1)S(1)}, u32[]{:S(2)}, u32[]{:S(2)}) async-start(bf16[16,32,2048]{2,1,0:T(8,128)(2,1)} %bitcast.51), calls=%async_computation | async-start | bytes 4194304 | tf_op jit(solution)/shard_map/all_to_all | solution.py:43
  73.8 5.1 %copy-start.8 = (s32[1,16]{1,0:T(1,128)S(1)}, s32[1,16]{1,0:T(1,128)}, u32[]{:S(2)}) copy-start(s32[1,16]{1,0:T(1,128)} %param.15) | copy-start | bytes 196
  73.8 54.2 %all-to-all-start.2 = ((bf16[16,32,2048]{2,1,0:T(8,128)(2,1)}), bf16[16,32,2048]{2,1,0:T(8,128)(2,1)}, u32[]{:S(2)}, u32[]{:S(2)}) async-start(bf16[16,32,2048]{2,1,0:T(8,128)(2,1)} %bitcast.50), calls=%async_computation.2 | async-start | bytes 4194304 | tf_op jit(solution)/shard_map/all_to_all | solution.py:46
  79.1 2.8 copy-start.7
  81.2 0.8 copy-start.2
  134.0 2.1 copy-start.3
  136.1 2.2 copy-start.4
  140.4 5.2 %copy-start.1 = (f32[256,2048]{1,0:T(8,128)S(1)}, f32[256,2048]{1,0:T(8,128)}, u32[]{:S(2)}) copy-start(f32[256,2048]{1,0:T(8,128)} %fusion.19) | copy-start | bytes 6291460
  140.4 179.5 %all-to-all-start.1 = ((bf16[16,32,2048]{2,1,0:T(8,128)(2,1)}), bf16[16,32,2048]{2,1,0:T(8,128)(2,1)}, u32[]{:S(2)}, u32[]{:S(2)}) async-start(bf16[16,32,2048]{2,1,0:T(8,128)(2,1)} %bitcast.52), calls=%async_computation.1 | async-start | bytes 4194304 | tf_op jit(solution)/shard_map/all_to_all | solution.py:59
  145.5 172.6 %all-reduce.2.cloned.1.call-start = ((), (), s32[]{:S(2)}) async-start(), calls=%async_computation.3 | async-start | bytes 6291456 | tf_op jit(solution)/shard_map/psum | solution.py:83
  149.2 0.7 copy-start.6
Sparse Core Ops, SparseCore 0:
  149.9 168.2 all-reduce.1
where the time goes:
time: 334 us; the launch traced here: 331 us
  waiting for transfers between devices  260 us (78%)
  starting transfers between devices  20.8 us (6%)
  matrix products  20.4 us (6%)
  between operations  14.1 us (4%)
  other arithmetic  8.42 us (3%)
  local copies, waits for them, and re-layouts  7.54 us (2%)
    psum x1, waiting for transfers between devices, body(): total = lax.psum(masked.astype(jnp.bfloat16), 'rep').astype(jnp.float32)  168 us
    all_to_all x1, waiting for transfers between devices, body(): lax.all_to_all(jnp.repeat(x_buf, shards, axis=0), 'exp', split_axis=0, co...  46.8 us
    all_to_all x1, waiting for transfers between devices, body(): lax.all_to_all(jnp.repeat(d_buf, shards, axis=0), 'exp', split_axis=0, co...  44.5 us
    all_to_all x1, starting transfers between devices, body(): lax.all_to_all(jnp.repeat(x_buf, shards, axis=0), 'exp', split_axis=0, co...  10.5 us
  transfers between devices with their start and end apart: 4, of which 3 were waited for; matrix products, arithmetic and copies ran while one was open for 3% of the time, Pallas kernels for 0%

commit v1 on v0

v1 whole, which is shorter than its diff:
```python
import jax
import jax.numpy as jnp
from jax import lax
from jax.sharding import Mesh, PartitionSpec as P

EW = 4
TILE = 16
X, Z, Y, C = 4, 8, 8, 2
AXES = ("x", "z", "y", "c")
bf16 = jnp.bfloat16
f32 = jnp.float32

PERM1 = [(i, (i - 1) % Y if i % 2 == 0 else (i + 1) % Y) for i in range(Y)]
PERM2 = [(i, (i + 2) % Y if i % 2 == 0 else (i - 2) % Y) for i in range(Y)]
PERM3 = [(i, ((i + 4) ^ 1) % Y) for i in range(Y)]
PAIR = [(i, i ^ 1) for i in range(Y)]
SWAP = [(0, 1), (1, 0)]


def swish_slope(h):
    s = jax.nn.sigmoid(h)
    return s * (1.0 + h * (1.0 - s))


def share(buf):
    parts = [
        buf[0],
        lax.ppermute(buf[1], "y", PERM1),
        lax.ppermute(buf[2], "y", PERM2),
        lax.ppermute(buf[3], "y", PERM3),
    ]
    mine = jnp.concatenate(parts, axis=0)
    both = jnp.concatenate([mine, lax.ppermute(mine, "y", PAIR)], axis=0)
    return jnp.concatenate([both, lax.ppermute(both, "c", SWAP)], axis=0)


def reduce_rep(part):
    n = part.shape[1]
    over_x = lax.all_to_all(part, "x", split_axis=0, concat_axis=0, tiled=True)
    sum_x = over_x.reshape(X, -1, n).astype(f32).sum(axis=0).astype(bf16)
    over_z = lax.all_to_all(sum_x, "z", split_axis=0, concat_axis=0, tiled=True)
    return over_z.reshape(Z, -1, n).astype(f32).sum(axis=0)


def body(tokens, expert_ids, gate_prob, cotangent, w_gate, w_up, w_down, touched):
    rows, width = tokens.shape
    cap = rows // EW
    y = lax.axis_index("y")
    odd = y % 2
    ids = expert_ids[:, 0]
    onehot = (expert_ids == jnp.arange(EW)[None, :]).astype(f32)
    lower = (
        lax.broadcasted_iota(jnp.int32, (rows, rows), 0)
        > lax.broadcasted_iota(jnp.int32, (rows, rows), 1)
    ).astype(f32)
    earlier = jnp.dot(lower, onehot)
    slot_of = jnp.sum(onehot * earlier, axis=1).astype(jnp.int32)
    away = (ids - y // 2) % EW
    place = jnp.where(away == 2, 3, jnp.where(away == 0, 0, jnp.where((away == 1) == (odd == 1), 1, 2)))
    target = place * cap + slot_of
    placer = (target[None, :] == jnp.arange(EW * cap)[:, None]).astype(bf16)
    dy = (gate_prob[:, None] * cotangent.astype(f32)).astype(bf16)
    x_buf = jnp.dot(placer, tokens, preferred_element_type=f32).astype(bf16).reshape(EW, cap, width)
    d_buf = jnp.dot(placer, dy, preferred_element_type=f32).astype(bf16).reshape(EW, cap, width)
    x_rows = share(x_buf)
    d_rows = share(d_buf)
    wg = w_gate[0]
    wu = w_up[0]
    wd = w_down[0]
    h = jnp.dot(x_rows, wg, preferred_element_type=f32)
    u = jnp.dot(x_rows, wu, preferred_element_type=f32)
    act = (h * jax.nn.sigmoid(h) * u).astype(bf16)
    partial_out = jnp.dot(act, wd, preferred_element_type=f32).astype(bf16)
    half = partial_out.shape[0] // 2
    core_sum = (
        partial_out[:half].astype(f32)
        + lax.ppermute(partial_out[half:], "c", SWAP).astype(f32)
    ).astype(bf16).reshape(Y, cap, width)

    grad_a = lax.dot_general(d_rows, wd, (((1,), (1,)), ((), ())), preferred_element_type=f32)
    mask = jnp.repeat(touched[0].astype(f32), TILE)[None, :]
    d_h = (grad_a * u * swish_slope(h) * mask).astype(bf16)
    d_u = (grad_a * h * jax.nn.sigmoid(h) * mask).astype(bf16)
    act_m = act * mask.astype(bf16)
    tdot = lambda a, b: lax.dot_general(a, b, (((0,), (0,)), ((), ())), preferred_element_type=f32).astype(bf16)
    delta = jnp.concatenate([tdot(x_rows, d_h), tdot(x_rows, d_u), tdot(d_rows, act_m)], axis=0)
    hid = delta.shape[1] // 2
    parts = [reduce_rep(delta[:, :hid]), reduce_rep(delta[:, hid:])]
    averaged = (jnp.concatenate(parts, axis=1) / (X * Z)).astype(bf16).T

    offset = (jnp.arange(Y) - y) % Y
    at_even = jnp.array([0, 4, 5, 6, 7, 3, 2, 1], jnp.int32)
    at_odd = jnp.array([0, 1, 2, 3, 7, 6, 5, 4], jnp.int32)
    order = jnp.where(odd == 1, at_odd, at_even)[offset]
    send = jnp.take(core_sum, order, axis=0, mode="clip")
    back = lax.all_to_all(send, "y", split_axis=0, concat_axis=0, tiled=True).reshape(Y * cap, width)
    column = jnp.arange(Y * cap)[None, :]
    picker = ((column // (2 * cap) == ids[:, None]) & (column % cap == slot_of[:, None])).astype(bf16)
    row_out = jnp.dot(picker, back, preferred_element_type=f32)
    mixed = (gate_prob[:, None] * row_out).astype(bf16)
    return mixed, averaged


def solution(mesh):
    fine = Mesh(mesh.devices.reshape(X, Z, Y, C), AXES)
    rep, exp = ("x", "z"), ("y", "c")
    return jax.shard_map(
        body,
        mesh=fine,
        in_specs=(
            P(AXES, None),
            P(AXES, None),
            P(AXES),
            P(AXES, None),
            P(rep, None, exp),
            P(rep, None, exp),
            P(rep, exp, None),
            P(rep, exp),
        ),
        out_specs=(P(AXES, None), P(exp, rep)),
        check_vma=False,
    )
```

time: 334 us -> 194 us (0.58)
  waiting for transfers between devices: 260 us -> 54.7 us
  starting transfers between devices: 20.8 us -> 71.9 us
  blocking collectives: 0 us -> 24.3 us
  between operations: 14.1 us -> 1.06 us
  matrix products: 20.4 us -> 11.1 us
  local copies, waits for them, and re-layouts: 7.54 us -> 16.7 us
    psum x1 -> x0, waiting for transfers between devices: 168 us -> none  [body(): total = lax.psum(masked.astype(jnp.bfloat16), 'rep').astype(jnp.float32)]
    ppermute x0 -> x11, starting transfers between devices: none -> 48 us  [the longest x2 11.5 us: share(): lax.ppermute(buf[3], 'y', PERM3)]
    all_to_all x3 -> x4, waiting for transfers between devices: 91.3 us -> 49.8 us  [the longest x1 23.3 us: body(): lax.all_to_all(send, 'y', split_axis=0, concat_axis=0, tiled=True)]
    all_to_all x0 -> x1, blocking collectives: none -> 24.3 us  [reduce_rep(): over_x = lax.all_to_all(part, 'x', split_axis=0, concat_axis=0, tiled=True)]
    dot_general x9 -> x10, matrix products: 18 us -> 8.58 us  [the longest x3 2.63 us: body(): lax.dot_general(a, b, (((0,), (0,)), ((), ())), preferred_element_type=f32)]
    unnamed x19 -> x32, local copies, waits for them, and re-layouts: 2.19 us -> 7.75 us
    ppermute x0 -> x11, waiting for transfers between devices: none -> 4.93 us  [the longest x2 2.9 us: share(): lax.ppermute(buf[3], 'y', PERM3)]
    broadcast_in_dim x3 -> x1, local copies, waits for them, and re-layouts: 4.29 us -> 0.07 us  [body(): mask = jnp.repeat(touched[0].astype(f32), TILE)[None, :]]
  transfers between devices with their start and end apart: 4 -> 15, of which waited for: 3 -> 6; matrix products, arithmetic and copies ran while one was open for 3% -> 13% of each run, Pallas kernels for 0% -> 0%
where the time goes in v1:
time: 194 us; the launch traced here: 191 us
  starting transfers between devices  71.9 us (37%)
  waiting for transfers between devices  54.7 us (28%)
  blocking collectives  24.3 us (13%)
  local copies, waits for them, and re-layouts  16.7 us (9%)
  matrix products  11.1 us (6%)
  other arithmetic  10.7 us (6%)
    all_to_all x1, blocking collectives, reduce_rep(): over_x = lax.all_to_all(part, 'x', split_axis=0, concat_axis=0, tiled=True)  24.3 us
    all_to_all x1, waiting for transfers between devices, body(): lax.all_to_all(send, 'y', split_axis=0, concat_axis=0, tiled=True)  23.3 us
    all_to_all x2, starting transfers between devices, reduce_rep(): over_z = lax.all_to_all(sum_x, 'z', split_axis=0, concat_axis=0, tiled=True)  14.1 us
    all_to_all x2, waiting for transfers between devices, reduce_rep(): over_z = lax.all_to_all(sum_x, 'z', split_axis=0, concat_axis=0, tiled=True)  14.1 us
    all_to_all x1, waiting for transfers between devices, reduce_rep(): over_x = lax.all_to_all(part, 'x', split_axis=0, concat_axis=0, tiled=True)  12.4 us
    ppermute x2, starting transfers between devices, share(): lax.ppermute(buf[3], 'y', PERM3)  11.5 us
    ppermute x2, starting transfers between devices, share(): both = jnp.concatenate([mine, lax.ppermute(mine, 'y', PAIR)], axis=0)  11.3 us
    ppermute x2, starting transfers between devices, share(): return jnp.concatenate([both, lax.ppermute(both, 'c', SWAP)], axis=0)  10.2 us
  transfers between devices with their start and end apart: 15, of which 6 were waited for; matrix products, arithmetic and copies ran while one was open for 13% of the time, Pallas kernels for 0%

profile of v1, /device:TPU:1, one launch (start us, length us, event | category | flops | bytes accessed | tf_op | source)
XLA Modules:
  0.0 190.5 jit_solution(5700183844758937408)
XLA Ops:
  2.3 1.4 convolution_convert_fusion.4
  4.4 5.9 %collective-permute-start.6 = (bf16[32,2048]{1,0:T(8,128)(2,1)S(1)}, bf16[32,2048]{1,0:T(8,128)(2,1)S(1)}, u32[]{:S(2)}, u32[]{:S(2)}) collective-permute-start(bf16[32,2048]{1,0:T(8,128)(2,1)S(1)} %get-tuple-element.10), channel_id=1, source_target_pairs={{0,14},{2,4},{4,2},{6,8},{8,6},{10,12},{12,10},{14,0},{1,15},{3,5}... | collective-permute-start | bytes 393224 | tf_op jit(solution)/shard_map/ppermute | solution.py:28
  10.4 1.9 %collective-permute-start.7 = (bf16[32,2048]{1,0:T(8,128)(2,1)S(1)}, bf16[32,2048]{1,0:T(8,128)(2,1)S(1)}, u32[]{:S(2)}, u32[]{:S(2)}) collective-permute-start(bf16[32,2048]{1,0:T(8,128)(2,1)S(1)} %get-tuple-element.9), channel_id=1, source_target_pairs={{0,4},{2,14},{4,8},{6,2},{8,12},{10,6},{12,0},{14,10},{1,5},{3,15}... | collective-permute-start | bytes 393224 | tf_op jit(solution)/shard_map/ppermute | solution.py:29
  12.3 6.9 %collective-permute-start.8 = (bf16[32,2048]{1,0:T(8,128)(2,1)S(1)}, bf16[32,2048]{1,0:T(8,128)(2,1)S(1)}, u32[]{:S(2)}, u32[]{:S(2)}) collective-permute-start(bf16[32,2048]{1,0:T(8,128)(2,1)S(1)} %get-tuple-element.8), channel_id=1, source_target_pairs={{0,10},{2,8},{4,14},{6,12},{8,2},{10,0},{12,6},{14,4},{1,11},{3,9}... | collective-permute-start | bytes 393224 | tf_op jit(solution)/shard_map/ppermute | solution.py:30
  20.3 2.1 %collective-permute-start = (bf16[32,2048]{1,0:T(8,128)(2,1)S(1)}, bf16[32,2048]{1,0:T(8,128)(2,1)S(1)}, u32[]{:S(2)}, u32[]{:S(2)}) collective-permute-start(bf16[32,2048]{1,0:T(8,128)(2,1)S(1)} %get-tuple-element.18), channel_id=1, source_target_pairs={{0,14},{2,4},{4,2},{6,8},{8,6},{10,12},{12,10},{14,0},{1,15},{3,5}... | collective-permute-start | bytes 393224 | tf_op jit(solution)/shard_map/ppermute | solution.py:28
  22.4 2.1 %collective-permute-start.1 = (bf16[32,2048]{1,0:T(8,128)(2,1)S(1)}, bf16[32,2048]{1,0:T(8,128)(2,1)S(1)}, u32[]{:S(2)}, u32[]{:S(2)}) collective-permute-start(bf16[32,2048]{1,0:T(8,128)(2,1)S(1)} %get-tuple-element.17), channel_id=1, source_target_pairs={{0,4},{2,14},{4,8},{6,2},{8,12},{10,6},{12,0},{14,10},{1,5},{3,15}... | collective-permute-start | bytes 393224 | tf_op jit(solution)/shard_map/ppermute | solution.py:29
  24.5 4.6 %collective-permute-start.2 = (bf16[32,2048]{1,0:T(8,128)(2,1)S(1)}, bf16[32,2048]{1,0:T(8,128)(2,1)S(1)}, u32[]{:S(2)}, u32[]{:S(2)}) collective-permute-start(bf16[32,2048]{1,0:T(8,128)(2,1)S(1)} %get-tuple-element.16), channel_id=1, source_target_pairs={{0,10},{2,8},{4,14},{6,12},{8,2},{10,0},{12,6},{14,4},{1,11},{3,9}... | collective-permute-start | bytes 393224 | tf_op jit(solution)/shard_map/ppermute | solution.py:30
  29.1 2.7 %collective-permute-start.9 = (bf16[128,2048]{1,0:T(8,128)(2,1)S(1)}, bf16[128,2048]{1,0:T(8,128)(2,1)S(1)}, u32[]{:S(2)}, u32[]{:S(2)}) collective-permute-start(bf16[128,2048]{1,0:T(8,128)(2,1)S(1)} %pad_maximum_fusion.2), channel_id=1, source_target_pairs={{0,2},{2,0},{4,6},{6,4},{8,10},{10,8},{12,14},{14,12},{1,3},{3,1},... | collective-permute-start | bytes 1572872 | tf_op jit(solution)/shard_map/ppermute | solution.py:33
  31.9 2.9 %collective-permute-done.2 = bf16[32,2048]{1,0:T(8,128)(2,1)S(1)} collective-permute-done((bf16[32,2048]{1,0:T(8,128)(2,1)S(1)}, bf16[32,2048]{1,0:T(8,128)(2,1)S(1)}, u32[]{:S(2)}, u32[]{:S(2)}) %collective-permute-start.2) | collective-permute-done | bytes 131104 | tf_op jit(solution)/shard_map/ppermute | solution.py:30
  34.9 8.5 %collective-permute-start.3 = (bf16[128,2048]{1,0:T(8,128)(2,1)S(1)}, bf16[128,2048]{1,0:T(8,128)(2,1)S(1)}, u32[]{:S(2)}, u32[]{:S(2)}) collective-permute-start(bf16[128,2048]{1,0:T(8,128)(2,1)S(1)} %pad_maximum_fusion.1), channel_id=1, source_target_pairs={{0,2},{2,0},{4,6},{6,4},{8,10},{10,8},{12,14},{14,12},{1,3},{3,1},... | collective-permute-start | bytes 1572872 | tf_op jit(solution)/shard_map/ppermute | solution.py:33
  47.0 5.6 %collective-permute-start.10 = (bf16[256,2048]{1,0:T(8,128)(2,1)}, bf16[256,2048]{1,0:T(8,128)(2,1)S(1)}, u32[]{:S(2)}, u32[]{:S(2)}) collective-permute-start(bf16[256,2048]{1,0:T(8,128)(2,1)} %get-tuple-element.4), channel_id=1, source_target_pairs={{0,1},{1,0},{2,3},{3,2},{4,5},{5,4},{6,7},{7,6},{8,9},{9,8},{10,11... | collective-permute-start | bytes 3145736 | tf_op jit(solution)/shard_map/ppermute | solution.py:34
  53.9 2.0 %collective-permute-done.3 = bf16[128,2048]{1,0:T(8,128)(2,1)S(1)} collective-permute-done((bf16[128,2048]{1,0:T(8,128)(2,1)S(1)}, bf16[128,2048]{1,0:T(8,128)(2,1)S(1)}, u32[]{:S(2)}, u32[]{:S(2)}) %collective-permute-start.3) | collective-permute-done | bytes 524320 | tf_op jit(solution)/shard_map/ppermute | solution.py:33
  56.9 4.6 %collective-permute-start.4 = (bf16[256,2048]{1,0:T(8,128)(2,1)}, bf16[256,2048]{1,0:T(8,128)(2,1)S(1)}, u32[]{:S(2)}, u32[]{:S(2)}) collective-permute-start(bf16[256,2048]{1,0:T(8,128)(2,1)} %get-tuple-element.12), channel_id=1, source_target_pairs={{0,1},{1,0},{2,3},{3,2},{4,5},{5,4},{6,7},{7,6},{8,9},{9,8},{10,11... | collective-permute-start | bytes 3145736 | tf_op jit(solution)/shard_map/ppermute | solution.py:34
  62.7 2.5 %fusion.2 = f32[512,256]{1,0:T(8,128)S(1)} fusion(bf16[512,2048]{1,0:T(8,128)(2,1)} %constant_dynamic-update-slice_fusion.16, bf16[1,256,2048]{2,1,0:T(8,128)(2,1)S(1)} %copy-done), kind=kOutput, calls=%fused_computation.14 | convolution fusion | flops 536870912 | bytes 3670016 | tf_op jit(solution)/shard_map/dot_general | solution.py:80
  65.3 1.1 copy-done.9
  72.3 1.3 fusion.33
  73.6 24.3 %all_to_all.41 = bf16[4,1536,128]{2,1,0:T(8,128)(2,1)} all-to-all(bf16[4,1536,128]{2,1,0:T(8,128)(2,1)S(1)} %bitcast.36), channel_id=1, replica_groups=mesh['x'=4,'z'=8,'y'=8,'c'=2] {'x'}, dimensions={0} | all-to-all | bytes 3145728 | tf_op jit(solution)/shard_map/all_to_all | solution.py:39
  97.9 4.4 %all-to-all-start.1 = ((bf16[4,1536,128]{2,1,0:T(8,128)(2,1)}), bf16[4,1536,128]{2,1,0:T(8,128)(2,1)}, u32[]{:S(2)}, u32[]{:S(2)}) async-start(bf16[4,1536,128]{2,1,0:T(8,128)(2,1)} %bitcast.8), calls=%async_computation.1 | async-start | bytes 3145728 | tf_op jit(solution)/shard_map/all_to_all | solution.py:39
  103.0 1.1 slice.65
  104.1 3.0 %collective-permute-start.5 = (bf16[256,2048]{1,0:T(8,128)(2,1)}, bf16[256,2048]{1,0:T(8,128)(2,1)}, u32[]{:S(2)}, u32[]{:S(2)}) collective-permute-start(bf16[256,2048]{1,0:T(8,128)(2,1)} %slice.65), channel_id=1, source_target_pairs={{0,1},{1,0},{2,3},{3,2},{4,5},{5,4},{6,7},{7,6},{8,9},{9,8},{10,11... | collective-permute-start | bytes 3145736 | tf_op jit(solution)/shard_map/ppermute | solution.py:77
  107.1 2.5 %reduce_sum.54 = bf16[1536,128]{1,0:T(8,128)(2,1)} reduce(bf16[4,1536,128]{2,1,0:T(8,128)(2,1)} %all_to_all.41, bf16[]{:T(256)} %constant.110.clone.1), dimensions={0}, to_apply=%region_3.4 | reduce | flops 589824 | bytes 1966082 | tf_op jit(solution)/shard_map/reduce_sum | solution.py:40
  109.6 12.4 %all-to-all-done.1 = bf16[4,1536,128]{2,1,0:T(8,128)(2,1)} async-done(((bf16[4,1536,128]{2,1,0:T(8,128)(2,1)}), bf16[4,1536,128]{2,1,0:T(8,128)(2,1)}, u32[]{:S(2)}, u32[]{:S(2)}) %all-to-all-start.1) | async-done | bytes 1572896 | tf_op jit(solution)/shard_map/all_to_all | solution.py:39
  122.0 10.0 %all-to-all-start.4 = ((bf16[8,192,128]{2,1,0:T(8,128)(2,1)}), bf16[8,192,128]{2,1,0:T(8,128)(2,1)S(1)}, u32[]{:S(2)}, u32[]{:S(2)}) async-start(bf16[8,192,128]{2,1,0:T(8,128)(2,1)} %bitcast.40), calls=%async_computation.4 | async-start | bytes 786432 | tf_op jit(solution)/shard_map/all_to_all | solution.py:41
  132.1 2.5 %reduce_sum.52 = bf16[1536,128]{1,0:T(8,128)(2,1)} reduce(bf16[4,1536,128]{2,1,0:T(8,128)(2,1)} %all-to-all-done.1, bf16[]{:T(256)} %constant.110.clone.1), dimensions={0}, to_apply=%region_1.2 | reduce | flops 589824 | bytes 1966082 | tf_op jit(solution)/shard_map/reduce_sum | solution.py:40
  134.6 9.5 %all-to-all-done.4 = bf16[8,192,128]{2,1,0:T(8,128)(2,1)S(1)} async-done(((bf16[8,192,128]{2,1,0:T(8,128)(2,1)}), bf16[8,192,128]{2,1,0:T(8,128)(2,1)S(1)}, u32[]{:S(2)}, u32[]{:S(2)}) %all-to-all-start.4) | async-done | bytes 393248 | tf_op jit(solution)/shard_map/all_to_all | solution.py:41
  144.1 4.1 %all-to-all-start.2 = ((bf16[8,192,128]{2,1,0:T(8,128)(2,1)}), bf16[8,192,128]{2,1,0:T(8,128)(2,1)}, u32[]{:S(2)}, u32[]{:S(2)}) async-start(bf16[8,192,128]{2,1,0:T(8,128)(2,1)} %bitcast.39), calls=%async_computation.2 | async-start | bytes 786432 | tf_op jit(solution)/shard_map/all_to_all | solution.py:41
  148.9 2.6 %add_convert_fusion = bf16[256,2048]{1,0:T(8,128)(2,1)} fusion(bf16[256,2048]{1,0:T(8,128)(2,1)} %collective-permute-done.5, bf16[512,2048]{1,0:T(8,128)(2,1)S(1)} %convolution_convert_fusion), kind=kLoop, calls=%fused_computation.11 | loop fusion | flops 2097152 | bytes 3145728 | tf_op jit(solution)/shard_map/convert_element_type | solution.py:78
  151.4 2.8 %gather_fusion.1 = bf16[8,32,2048]{2,1,0:T(8,128)(2,1)} fusion(bf16[8,32,2048]{2,1,0:T(8,128)(2,1)} %bitcast.37, s32[1024]{0:T(1024)S(1)} %pad_clamp_fusion), kind=kCustom, calls=%fused_computation.1 | custom fusion | bytes 2097184 | tf_op jit(solution)/shard_map/jit(_take)/gather | solution.py:95
  154.3 4.5 %all-to-all-done.2 = bf16[8,192,128]{2,1,0:T(8,128)(2,1)} async-done(((bf16[8,192,128]{2,1,0:T(8,128)(2,1)}), bf16[8,192,128]{2,1,0:T(8,128)(2,1)}, u32[]{:S(2)}, u32[]{:S(2)}) %all-to-all-start.2) | async-done | bytes 393248 | tf_op jit(solution)/shard_map/all_to_all | solution.py:41
  158.8 5.4 %all-to-all-start = ((bf16[8,32,2048]{2,1,0:T(8,128)(2,1)}), bf16[8,32,2048]{2,1,0:T(8,128)(2,1)S(1)}, u32[]{:S(2)}, u32[]{:S(2)}) async-start(bf16[8,32,2048]{2,1,0:T(8,128)(2,1)} %gather_fusion.1), calls=%async_computation | async-start | bytes 2097152 | tf_op jit(solution)/shard_map/all_to_all | solution.py:96
  166.0 23.3 %all-to-all-done = bf16[8,32,2048]{2,1,0:T(8,128)(2,1)S(1)} async-done(((bf16[8,32,2048]{2,1,0:T(8,128)(2,1)}), bf16[8,32,2048]{2,1,0:T(8,128)(2,1)S(1)}, u32[]{:S(2)}, u32[]{:S(2)}) %all-to-all-start) | async-done | bytes 1048608 | tf_op jit(solution)/shard_map/all_to_all | solution.py:96
  189.4 1.1 fusion
  (70 shorter events, 19.6 us)
Async XLA Ops:
  0.6 62.1 %copy-start = (bf16[1,256,2048]{2,1,0:T(8,128)(2,1)S(1)}, bf16[1,256,2048]{2,1,0:T(8,128)(2,1)}, u32[]{:S(2)}) copy-start(bf16[1,256,2048]{2,1,0:T(8,128)(2,1)} %param.16) | copy-start | bytes 3145732
  0.6 18.6 %copy-start.1 = (bf16[128,2048]{1,0:T(8,128)(2,1)S(1)}, bf16[128,2048]{1,0:T(8,128)(2,1)}, u32[]{:S(2)}) copy-start(bf16[128,2048]{1,0:T(8,128)(2,1)} %param.10) | copy-start | bytes 1572868
  4.4 20.0 %collective-permute-start.6 = (bf16[32,2048]{1,0:T(8,128)(2,1)S(1)}, bf16[32,2048]{1,0:T(8,128)(2,1)S(1)}, u32[]{:S(2)}, u32[]{:S(2)}) collective-permute-start(bf16[32,2048]{1,0:T(8,128)(2,1)S(1)} %get-tuple-element.10), channel_id=1, source_target_pairs={{0,14},{2,4},{4,2},{6,8},{8,6},{10,12},{12,10},{14,0},{1,15},{3,5}... | collective-permute-start | bytes 393224 | tf_op jit(solution)/shard_map/ppermute | solution.py:28
  10.4 18.7 %collective-permute-start.7 = (bf16[32,2048]{1,0:T(8,128)(2,1)S(1)}, bf16[32,2048]{1,0:T(8,128)(2,1)S(1)}, u32[]{:S(2)}, u32[]{:S(2)}) collective-permute-start(bf16[32,2048]{1,0:T(8,128)(2,1)S(1)} %get-tuple-element.9), channel_id=1, source_target_pairs={{0,4},{2,14},{4,8},{6,2},{8,12},{10,6},{12,0},{14,10},{1,5},{3,15}... | collective-permute-start | bytes 393224 | tf_op jit(solution)/shard_map/ppermute | solution.py:29
  12.3 16.8 %collective-permute-start.8 = (bf16[32,2048]{1,0:T(8,128)(2,1)S(1)}, bf16[32,2048]{1,0:T(8,128)(2,1)S(1)}, u32[]{:S(2)}, u32[]{:S(2)}) collective-permute-start(bf16[32,2048]{1,0:T(8,128)(2,1)S(1)} %get-tuple-element.8), channel_id=1, source_target_pairs={{0,10},{2,8},{4,14},{6,12},{8,2},{10,0},{12,6},{14,4},{1,11},{3,9}... | collective-permute-start | bytes 393224 | tf_op jit(solution)/shard_map/ppermute | solution.py:30
  20.3 11.6 %collective-permute-start = (bf16[32,2048]{1,0:T(8,128)(2,1)S(1)}, bf16[32,2048]{1,0:T(8,128)(2,1)S(1)}, u32[]{:S(2)}, u32[]{:S(2)}) collective-permute-start(bf16[32,2048]{1,0:T(8,128)(2,1)S(1)} %get-tuple-element.18), channel_id=1, source_target_pairs={{0,14},{2,4},{4,2},{6,8},{8,6},{10,12},{12,10},{14,0},{1,15},{3,5}... | collective-permute-start | bytes 393224 | tf_op jit(solution)/shard_map/ppermute | solution.py:28
  22.4 9.5 %collective-permute-start.1 = (bf16[32,2048]{1,0:T(8,128)(2,1)S(1)}, bf16[32,2048]{1,0:T(8,128)(2,1)S(1)}, u32[]{:S(2)}, u32[]{:S(2)}) collective-permute-start(bf16[32,2048]{1,0:T(8,128)(2,1)S(1)} %get-tuple-element.17), channel_id=1, source_target_pairs={{0,4},{2,14},{4,8},{6,2},{8,12},{10,6},{12,0},{14,10},{1,5},{3,15}... | collective-permute-start | bytes 393224 | tf_op jit(solution)/shard_map/ppermute | solution.py:29
  24.5 10.3 %collective-permute-start.2 = (bf16[32,2048]{1,0:T(8,128)(2,1)S(1)}, bf16[32,2048]{1,0:T(8,128)(2,1)S(1)}, u32[]{:S(2)}, u32[]{:S(2)}) collective-permute-start(bf16[32,2048]{1,0:T(8,128)(2,1)S(1)} %get-tuple-element.16), channel_id=1, source_target_pairs={{0,10},{2,8},{4,14},{6,12},{8,2},{10,0},{12,6},{14,4},{1,11},{3,9}... | collective-permute-start | bytes 393224 | tf_op jit(solution)/shard_map/ppermute | solution.py:30
  29.1 16.9 %collective-permute-start.9 = (bf16[128,2048]{1,0:T(8,128)(2,1)S(1)}, bf16[128,2048]{1,0:T(8,128)(2,1)S(1)}, u32[]{:S(2)}, u32[]{:S(2)}) collective-permute-start(bf16[128,2048]{1,0:T(8,128)(2,1)S(1)} %pad_maximum_fusion.2), channel_id=1, source_target_pairs={{0,2},{2,0},{4,6},{6,4},{8,10},{10,8},{12,14},{14,12},{1,3},{3,1},... | collective-permute-start | bytes 1572872 | tf_op jit(solution)/shard_map/ppermute | solution.py:33
  34.9 21.1 %collective-permute-start.3 = (bf16[128,2048]{1,0:T(8,128)(2,1)S(1)}, bf16[128,2048]{1,0:T(8,128)(2,1)S(1)}, u32[]{:S(2)}, u32[]{:S(2)}) collective-permute-start(bf16[128,2048]{1,0:T(8,128)(2,1)S(1)} %pad_maximum_fusion.1), channel_id=1, source_target_pairs={{0,2},{2,0},{4,6},{6,4},{8,10},{10,8},{12,14},{14,12},{1,3},{3,1},... | collective-permute-start | bytes 1572872 | tf_op jit(solution)/shard_map/ppermute | solution.py:33
  45.4 16.1 %copy-start.11 = (s32[1,16]{1,0:T(1,128)S(1)}, s32[1,16]{1,0:T(1,128)}, u32[]{:S(2)}) copy-start(s32[1,16]{1,0:T(1,128)} %param.17) | copy-start | bytes 196
  47.0 14.5 %copy-start.2 = (bf16[512,2048]{1,0:T(8,128)(2,1)}, bf16[512,2048]{1,0:T(8,128)(2,1)S(1)}, u32[]{:S(2)}) copy-start(bf16[512,2048]{1,0:T(8,128)(2,1)S(1)} %get-tuple-element.5) | copy-start | bytes 6291460
  47.0 14.7 %collective-permute-start.10 = (bf16[256,2048]{1,0:T(8,128)(2,1)}, bf16[256,2048]{1,0:T(8,128)(2,1)S(1)}, u32[]{:S(2)}, u32[]{:S(2)}) collective-permute-start(bf16[256,2048]{1,0:T(8,128)(2,1)} %get-tuple-element.4), channel_id=1, source_target_pairs={{0,1},{1,0},{2,3},{3,2},{4,5},{5,4},{6,7},{7,6},{8,9},{9,8},{10,11... | collective-permute-start | bytes 3145736 | tf_op jit(solution)/shard_map/ppermute | solution.py:34
  56.9 4.7 %copy-start.4 = (bf16[512,2048]{1,0:T(8,128)(2,1)}, bf16[512,2048]{1,0:T(8,128)(2,1)S(1)}, u32[]{:S(2)}) copy-start(bf16[512,2048]{1,0:T(8,128)(2,1)S(1)} %get-tuple-element.13) | copy-start | bytes 6291460
  56.9 8.4 %collective-permute-start.4 = (bf16[256,2048]{1,0:T(8,128)(2,1)}, bf16[256,2048]{1,0:T(8,128)(2,1)S(1)}, u32[]{:S(2)}, u32[]{:S(2)}) collective-permute-start(bf16[256,2048]{1,0:T(8,128)(2,1)} %get-tuple-element.12), channel_id=1, source_target_pairs={{0,1},{1,0},{2,3},{3,2},{4,5},{5,4},{6,7},{7,6},{8,9},{9,8},{10,11... | collective-permute-start | bytes 3145736 | tf_op jit(solution)/shard_map/ppermute | solution.py:34
  62.7 2.5 %copy-start.5 = (bf16[512,2048]{1,0:T(8,128)(2,1)S(1)}, bf16[512,2048]{1,0:T(8,128)(2,1)}, u32[]{:S(2)}) copy-start(bf16[512,2048]{1,0:T(8,128)(2,1)} %copy-done.4) | copy-start | bytes 6291460
  65.2 1.2 copy-start.9
  66.5 1.2 copy-start.10
  69.3 1.6 copy-start.3
  97.9 24.1 %all-to-all-start.1 = ((bf16[4,1536,128]{2,1,0:T(8,128)(2,1)}), bf16[4,1536,128]{2,1,0:T(8,128)(2,1)}, u32[]{:S(2)}, u32[]{:S(2)}) async-start(bf16[4,1536,128]{2,1,0:T(8,128)(2,1)} %bitcast.8), calls=%async_computation.1 | async-start | bytes 3145728 | tf_op jit(solution)/shard_map/all_to_all | solution.py:39
  103.0 29.0 %copy-start.8 = (s32[8]{0:T(128)S(1)}, s32[8]{0:T(128)}, u32[]{:S(2)}) copy-start(s32[8]{0:T(128)} %constant.112.clone) | copy-start | bytes 100
  104.1 44.8 %collective-permute-start.5 = (bf16[256,2048]{1,0:T(8,128)(2,1)}, bf16[256,2048]{1,0:T(8,128)(2,1)}, u32[]{:S(2)}, u32[]{:S(2)}) collective-permute-start(bf16[256,2048]{1,0:T(8,128)(2,1)} %slice.65), channel_id=1, source_target_pairs={{0,1},{1,0},{2,3},{3,2},{4,5},{5,4},{6,7},{7,6},{8,9},{9,8},{10,11... | collective-permute-start | bytes 3145736 | tf_op jit(solution)/shard_map/ppermute | solution.py:77
  122.0 22.1 %all-to-all-start.4 = ((bf16[8,192,128]{2,1,0:T(8,128)(2,1)}), bf16[8,192,128]{2,1,0:T(8,128)(2,1)S(1)}, u32[]{:S(2)}, u32[]{:S(2)}) async-start(bf16[8,192,128]{2,1,0:T(8,128)(2,1)} %bitcast.40), calls=%async_computation.4 | async-start | bytes 786432 | tf_op jit(solution)/shard_map/all_to_all | solution.py:41
  144.1 14.7 %all-to-all-start.2 = ((bf16[8,192,128]{2,1,0:T(8,128)(2,1)}), bf16[8,192,128]{2,1,0:T(8,128)(2,1)}, u32[]{:S(2)}, u32[]{:S(2)}) async-start(bf16[8,192,128]{2,1,0:T(8,128)(2,1)} %bitcast.39), calls=%async_computation.2 | async-start | bytes 786432 | tf_op jit(solution)/shard_map/all_to_all | solution.py:41
  154.3 35.1 %copy-start.6 = (f32[128]{0:T(128)S(1)}, f32[128]{0:T(128)}, u32[]{:S(2)}) copy-start(f32[128]{0:T(128)} %param.12) | copy-start | bytes 1540
  154.3 35.1 %copy-start.7 = (s32[128,1]{0,1:T(1,128)S(1)}, s32[128,1]{0,1:T(1,128)}, u32[]{:S(2)}) copy-start(s32[128,1]{0,1:T(1,128)} %param.11) | copy-start | bytes 1540
  158.8 30.5 %all-to-all-start = ((bf16[8,32,2048]{2,1,0:T(8,128)(2,1)}), bf16[8,32,2048]{2,1,0:T(8,128)(2,1)S(1)}, u32[]{:S(2)}, u32[]{:S(2)}) async-start(bf16[8,32,2048]{2,1,0:T(8,128)(2,1)} %gather_fusion.1), calls=%async_computation | async-start | bytes 2097152 | tf_op jit(solution)/shard_map/all_to_all | solution.py:96

commit v2 on v1

v2 whole, which is shorter than its diff:
```python
import functools

import jax
import jax.numpy as jnp
from jax import lax
from jax.experimental import pallas as pl
from jax.experimental.pallas import tpu as pltpu
from jax.sharding import Mesh, PartitionSpec as P

EW = 4
TILE = 16
X, Z, Y, C = 4, 8, 8, 2
AXES = ("x", "z", "y", "c")
CAP = 32
D = 2048
HID = 256
PART = 64
bf16 = jnp.bfloat16
f32 = jnp.float32

PERM1 = [(i, (i - 1) % Y if i % 2 == 0 else (i + 1) % Y) for i in range(Y)]
PERM2 = [(i, (i + 2) % Y if i % 2 == 0 else (i - 2) % Y) for i in range(Y)]
PERM3 = [(i, ((i + 4) ^ 1) % Y) for i in range(Y)]
PAIR = [(i, i ^ 1) for i in range(Y)]
SWAP = [(0, 1), (1, 0)]
VMEM_LIMIT = 40 * 1024 * 1024

VM = pl.BlockSpec(memory_space=pltpu.VMEM)
SM = pl.BlockSpec(memory_space=pltpu.SMEM)
TN = (((0,), (0,)), ((), ()))
NT = (((1,), (1,)), ((), ()))
NN = (((1,), (0,)), ((), ()))


def mm(a, b, dims=NN):
    return lax.dot_general(a, b, dims, preferred_element_type=f32)


def call(kernel, outs, args, flops, moved, n_smem=0, scratch=()):
    return pl.pallas_call(
        kernel,
        out_shape=outs,
        in_specs=[SM] * n_smem + [VM] * (len(args) - n_smem),
        out_specs=jax.tree.map(lambda _: VM, outs),
        scratch_shapes=list(scratch),
        compiler_params=pltpu.CompilerParams(vmem_limit_bytes=VMEM_LIMIT),
        cost_estimate=pl.CostEstimate(flops=flops, bytes_accessed=moved, transcendentals=0),
    )(*args)


def shaped(*shape, dtype=bf16):
    return jax.ShapeDtypeStruct(shape, dtype)


def back_perm(perm):
    return [(b, a) for a, b in perm]


def place_kernel(at, ids, gate, tokens, cotangent, own, one, two, three, placer_out, gate_out):
    y = at[2]
    odd = y % 2
    pair = y // 2
    rows = ids.shape[1]
    e = ids[...]
    expert = lax.broadcasted_iota(jnp.int32, (8, rows), 0)
    onehot = (expert == e).astype(f32)
    before = (
        lax.broadcasted_iota(jnp.int32, (rows, rows), 0)
        < lax.broadcasted_iota(jnp.int32, (rows, rows), 1)
    ).astype(bf16)
    earlier = mm(onehot.astype(bf16), before)
    slot = jnp.sum(onehot * earlier, axis=0, keepdims=True).astype(jnp.int32)
    away = (e - pair + EW) & 3
    near = 1 + 2 * odd
    near = 4 - near
    place = jnp.where(away == 0, 0, jnp.where(away == 2, 3, jnp.where(away == near, 1, 2)))
    target = place * CAP + slot
    placer = (lax.broadcasted_iota(jnp.int32, (rows, rows), 0) == target).astype(f32)
    placed_gate = jnp.sum(placer * gate[...], axis=1, keepdims=True)
    gate_out[...] = jnp.broadcast_to(placed_gate, (rows, rows))
    placer = placer.astype(bf16)
    placer_out[...] = placer
    xs = mm(placer, tokens[...]).astype(bf16)
    ds = (mm(placer, cotangent[...]) * placed_gate).astype(bf16)
    for k, ref in enumerate((own, one, two, three)):
        ref[:, :D] = xs[k * CAP:(k + 1) * CAP]
        ref[:, D:] = ds[k * CAP:(k + 1) * CAP]


def join_kernel(a, b, c, d, out):
    for k, ref in enumerate((a, b, c, d)):
        out[k * CAP:(k + 1) * CAP, :] = ref[...]


def join(parts):
    return call(join_kernel, shaped(4 * CAP, 2 * D), parts, 0, 4 * CAP * 4 * D * 2)


def layer_kernel(touched, mine, mates, wg, wu, wd, out_mine, out_mates, grads):
    expand = (lax.broadcasted_iota(jnp.int32, (TILE, HID), 1) // TILE
              == lax.broadcasted_iota(jnp.int32, (TILE, HID), 0)).astype(f32)
    row = jnp.zeros((TILE, HID), f32)
    for k in range(HID // TILE):
        flag = touched[0, k].astype(f32)
        row = jnp.where(lax.broadcasted_iota(jnp.int32, (TILE, HID), 0) == k, flag, row)
    mask = jnp.sum(expand * row, axis=0, keepdims=True)
    for ref, out, base in ((mine, out_mine, 0), (mates, out_mates, 4 * CAP)):
        xs = ref[:, :D]
        ds = ref[:, D:]
        h = mm(xs, wg[...])
        u = mm(xs, wu[...])
        g = mm(ds, wd[...], NT)
        s = 1.0 / (1.0 + jnp.exp(-h))
        act = (h * s * u).astype(bf16)
        out[...] = mm(act, wd[...]).astype(bf16)
        end = base + 4 * CAP
        grads[base:end, :HID] = (g * u * (s * (1.0 + h * (1.0 - s))) * mask).astype(bf16)
        grads[base:end, HID:2 * HID] = (g * (h * s) * mask).astype(bf16)
        grads[base:end, 2 * HID:] = (act.astype(f32) * mask).astype(bf16)


def layer(touched, mine, mates, wg, wu, wd):
    rows = 8 * CAP
    return call(
        layer_kernel,
        (shaped(4 * CAP, D), shaped(4 * CAP, D), shaped(rows, 3 * HID)),
        (touched, mine, mates, wg, wu, wd),
        2 * 4 * rows * D * HID, 2 * (3 * D * HID + rows * 3 * D), n_smem=1,
    )


STEP = 512


def delta_kernel(at, xa, xb, xc, xd, ga, gb, first, *rest):
    second, held = rest[:Z], rest[Z]
    z = at[1]

    def put(piece, value):
        rep, part = piece // 3, piece % 3
        if part < 2:
            first[rep // Z, rep % Z, part * PART:(part + 1) * PART, :] = value
        else:
            held[lax.rem(rep % Z - z + Z, Z), rep // Z] = value

    grads = jnp.concatenate([ga[...], gb[...]], axis=0)
    for base, lo, n in ((0, 0, 2), (D, 2 * HID, 1)):
        right = grads[:, lo:lo + n * HID]
        for c0 in range(0, D, STEP):
            cols = slice(base + c0, base + c0 + STEP)
            left = jnp.concatenate([r[:, cols] for r in (xa, xb, xc, xd)], axis=0)
            out = mm(left, right, TN).astype(bf16)
            for k in range(n):
                start = ((k if n == 2 else 2) * D + c0) // PART
                for i in range(STEP // PART):
                    put(start + i, out[i * PART:(i + 1) * PART, k * HID:(k + 1) * HID])
    for j in range(Z):
        second[j][...] = held[j]


def delta(at, xs, ga, gb):
    return call(
        delta_kernel,
        (shaped(X, Z, 2 * PART, HID),) + (shaped(X, PART, HID),) * Z,
        (at, *xs, ga, gb),
        2 * 3 * 16 * CAP * D * HID, 2 * (16 * CAP * 2 * D + 3 * D * HID), n_smem=1,
        scratch=(pltpu.VMEM((Z, X, PART, HID), bf16),),
    )


def sum_x_kernel(got, out):
    out[...] = sum(got[k].astype(f32) for k in range(X)).astype(bf16)


def sum_z_kernel(at, *refs):
    x = at[0]
    for j in range(X):
        src = lax.rem(x + j, X)
        refs[Z + j][...] = sum(refs[k][src].astype(f32) for k in range(Z)).astype(bf16)


def last_kernel(got, a, b, c, d, out):
    out[:2 * PART, :] = (sum(got[k].astype(f32) for k in range(Z)) * (1.0 / (X * Z))).astype(bf16)
    out[2 * PART:, :] = (sum(r[...].astype(f32) for r in (a, b, c, d)) * (1.0 / (X * Z))).astype(bf16)


def add_kernel(a, b, out):
    out[...] = (a[...].astype(f32) + b[...].astype(f32)).astype(bf16)


def add_split_kernel(a, b, c, *outs):
    total = (a[...].astype(f32) + b[...].astype(f32) + c[...].astype(f32)).astype(bf16)
    for k in range(4):
        outs[k][...] = total[k * CAP:(k + 1) * CAP]


def mixed_kernel(a, b, c, d, gate, placer, out):
    parts = []
    for k, ref in enumerate((a, b, c, d)):
        parts.append((ref[...].astype(f32) * gate[k * CAP:(k + 1) * CAP, :1]).astype(bf16))
    out[...] = mm(placer[...], jnp.concatenate(parts, axis=0), TN).astype(bf16)


def body(tokens, expert_ids, gate_prob, cotangent, w_gate, w_up, w_down, touched):
    rows = tokens.shape[0]
    at = jnp.stack([lax.axis_index("x"), lax.axis_index("z"), lax.axis_index("y")]).astype(jnp.int32)
    wg, wu, wd = w_gate[0], w_up[0], w_down[0]
    own, one, two, three, placer, gate = call(
        place_kernel,
        (shaped(CAP, 2 * D),) * 4 + (shaped(rows, rows), shaped(rows, rows, dtype=f32)),
        (at, expert_ids.T, gate_prob[None, :], tokens, cotangent),
        2 * 2 * rows * rows * D, 2 * 4 * rows * D, n_smem=1,
    )
    near = [own, lax.ppermute(one, "y", PERM1), lax.ppermute(two, "y", PERM2), lax.ppermute(three, "y", PERM3)]
    far = [lax.ppermute(part, "y", PAIR) for part in near]
    mine = join(near)
    mates = lax.ppermute(mine, "c", SWAP)
    pair_mine = join(far)
    pair_mates = lax.ppermute(pair_mine, "c", SWAP)
    p_mine, p_mates, ga = layer(touched, mine, mates, wg, wu, wd)
    q_mine, q_mates, gb = layer(touched, pair_mine, pair_mates, wg, wu, wd)
    p_got = lax.ppermute(p_mates, "c", SWAP)
    q_got = lax.ppermute(q_mates, "c", SWAP)

    first, *second = delta(at, (mine, mates, pair_mine, pair_mates), ga, gb)
    over_x = lax.all_to_all(first, "x", split_axis=0, concat_axis=0, tiled=True)
    over_z = [second[0]] + [
        lax.ppermute(second[j], "z", [(i, (i + j) % Z) for i in range(Z)]) for j in range(1, Z)
    ]
    sum_x = call(sum_x_kernel, shaped(Z, 2 * PART, HID), (over_x,), 0, 2 * 5 * Z * 2 * PART * HID)
    got = lax.all_to_all(sum_x, "z", split_axis=0, concat_axis=0, tiled=True)
    sums = call(sum_z_kernel, (shaped(PART, HID),) * X, (at, *over_z), 0, 2 * 9 * X * PART * HID, n_smem=1)
    rest = [sums[0]] + [
        lax.ppermute(sums[j], "x", [(i, (i + j) % X) for i in range(X)]) for j in range(1, X)
    ]
    averaged = call(last_kernel, shaped(3 * PART, HID), (got, *rest), 0, 2 * 9 * 3 * PART * HID).T

    q_sum = call(add_kernel, shaped(4 * CAP, D), (q_mine, q_got), 0, 3 * 8 * CAP * D)
    from_pair = lax.ppermute(q_sum, "y", PAIR)
    blocks = call(add_split_kernel, (shaped(CAP, D),) * 4, (p_mine, p_got, from_pair), 0, 4 * 8 * CAP * D)
    back = [blocks[0]] + [
        lax.ppermute(block, "y", back_perm(perm)) for block, perm in zip(blocks[1:], (PERM1, PERM2, PERM3))
    ]
    mixed = call(mixed_kernel, shaped(rows, D), (*back, gate, placer), 2 * rows * rows * D, 2 * 2 * rows * D)
    return mixed, averaged


def solution(mesh):
    fine = Mesh(mesh.devices.reshape(X, Z, Y, C), AXES)
    rep, exp = ("x", "z"), ("y", "c")
    return jax.shard_map(
        body,
        mesh=fine,
        in_specs=(
            P(AXES, None),
            P(AXES, None),
            P(AXES),
            P(AXES, None),
            P(rep, None, exp),
            P(rep, None, exp),
            P(rep, exp, None),
            P(rep, exp),
        ),
        out_specs=(P(AXES, None), P(exp, rep)),
        check_vma=False,
    )
```

time: 194 us -> 171 us (0.88)
  starting transfers between devices: 71.9 us -> 107 us
  blocking collectives: 24.3 us -> 0 us
  waiting for transfers between devices: 54.7 us -> 38.1 us
  Pallas kernels: 0 us -> 13.9 us
  matrix products: 11.1 us -> 0 us
  other arithmetic: 10.7 us -> 0.08 us
  local copies, waits for them, and re-layouts: 16.7 us -> 8.18 us
    ppermute x11 -> x25, starting transfers between devices: 48 us -> 94.6 us  [the longest x7 28.5 us: body(): lax.ppermute(second[j], 'z', [(i, (i + j) % Z) for i in range(Z)])]
    all_to_all x4 -> x2, waiting for transfers between devices: 49.8 us -> 24.5 us  [the longest x1 24.5 us: body(): over_x = lax.all_to_all(first, 'x', split_axis=0, concat_axis=0, tiled=True)]
    all_to_all x1 -> x0, blocking collectives: 24.3 us -> none  [reduce_rep(): over_x = lax.all_to_all(part, 'x', split_axis=0, concat_axis=0, tiled=True)]
    pallas_call x0 -> x12, Pallas kernels: none -> 13.9 us  [call(): pl.pallas_call(kernel, out_shape=outs, in_specs=[SM] * n_smem + [VM] * (l...]
    all_to_all x4 -> x2, starting transfers between devices: 23.9 us -> 12.2 us  [the longest x1 8.62 us: body(): got = lax.all_to_all(sum_x, 'z', split_axis=0, concat_axis=0, tiled=True)]
    dot_general x11 -> x0, matrix products: 11.1 us -> none  [the longest x3 2.63 us: body(): lax.dot_general(a, b, (((0,), (0,)), ((), ())), preferred_element_type=f32)]
    ppermute x11 -> x25, waiting for transfers between devices: 4.93 us -> 13.5 us  [the longest x1 6.69 us: body(): lax.ppermute(three, 'y', PERM3)]
    reduce_sum x4 -> x0, other arithmetic: 6.1 us -> none  [the longest x2 4.98 us: reduce_rep(): sum_x = over_x.reshape(X, -1, n).astype(f32).sum(axis=0).astype(bf16)]
  transfers between devices with their start and end apart: 15 -> 27, of which waited for: 6 -> 5; matrix products, arithmetic and copies ran while one was open for 13% -> 0% of each run, Pallas kernels for 0% -> 4%
where the time goes in v2:
time: 171 us; the launch traced here: 168 us
  starting transfers between devices  107 us (63%)
  waiting for transfers between devices  38.1 us (22%)
  Pallas kernels  13.9 us (8%)
  local copies, waits for them, and re-layouts  8.18 us (5%)
    ppermute x7, starting transfers between devices, body(): lax.ppermute(second[j], 'z', [(i, (i + j) % Z) for i in range(Z)])  28.5 us
    all_to_all x1, waiting for transfers between devices, body(): over_x = lax.all_to_all(first, 'x', split_axis=0, concat_axis=0, tiled=True)  24.5 us
    pallas_call x12, Pallas kernels, call(): pl.pallas_call(kernel, out_shape=outs, in_specs=[SM] * n_smem + [VM] * (l...  13.9 us
    ppermute x4, starting transfers between devices, body(): far = [lax.ppermute(part, 'y', PAIR) for part in near]  11.5 us
    ppermute x3, starting transfers between devices, body(): lax.ppermute(block, 'y', back_perm(perm))  10.5 us
    all_to_all x1, starting transfers between devices, body(): got = lax.all_to_all(sum_x, 'z', split_axis=0, concat_axis=0, tiled=True)  8.62 us
    ppermute x3, starting transfers between devices, body(): lax.ppermute(sums[j], 'x', [(i, (i + j) % X) for i in range(X)])  8.41 us
    unnamed x32, local copies, waits for them, and re-layouts  8.18 us
  transfers between devices with their start and end apart: 27, of which 5 were waited for; matrix products, arithmetic and copies ran while one was open for 0% of the time, Pallas kernels for 4%

profile of v2, /device:TPU:1, one launch (start us, length us, event | category | flops | bytes accessed | tf_op | source)
XLA Modules:
  0.0 168.2 jit_solution(9916934149638570742)
XLA Ops:
  5.2 5.9 %collective-permute-start = (bf16[32,4096]{1,0:T(8,128)(2,1)S(1)}, bf16[32,4096]{1,0:T(8,128)(2,1)S(1)}, u32[]{:S(2)}, u32[]{:S(2)}) collective-permute-start(bf16[32,4096]{1,0:T(8,128)(2,1)S(1)} %get-tuple-element.32), channel_id=1, source_target_pairs={{0,14},{2,4},{4,2},{6,8},{8,6},{10,12},{12,10},{14,0},{1,15},{3,5}... | collective-permute-start | bytes 786440 | tf_op jit(solution)/shard_map/ppermute | solution.py:214
  11.1 1.9 %collective-permute-start.1 = (bf16[32,4096]{1,0:T(8,128)(2,1)S(1)}, bf16[32,4096]{1,0:T(8,128)(2,1)S(1)}, u32[]{:S(2)}, u32[]{:S(2)}) collective-permute-start(bf16[32,4096]{1,0:T(8,128)(2,1)S(1)} %get-tuple-element.33), channel_id=1, source_target_pairs={{0,4},{2,14},{4,8},{6,2},{8,12},{10,6},{12,0},{14,10},{1,5},{3,15}... | collective-permute-start | bytes 786440 | tf_op jit(solution)/shard_map/ppermute | solution.py:214
  13.1 6.9 %collective-permute-start.2 = (bf16[32,4096]{1,0:T(8,128)(2,1)S(1)}, bf16[32,4096]{1,0:T(8,128)(2,1)S(1)}, u32[]{:S(2)}, u32[]{:S(2)}) collective-permute-start(bf16[32,4096]{1,0:T(8,128)(2,1)S(1)} %get-tuple-element.34), channel_id=1, source_target_pairs={{0,10},{2,8},{4,14},{6,12},{8,2},{10,0},{12,6},{14,4},{1,11},{3,9}... | collective-permute-start | bytes 786440 | tf_op jit(solution)/shard_map/ppermute | solution.py:214
  20.1 2.2 %collective-permute-start.5 = (bf16[32,4096]{1,0:T(8,128)(2,1)S(1)}, bf16[32,4096]{1,0:T(8,128)(2,1)S(1)}, u32[]{:S(2)}, u32[]{:S(2)}) collective-permute-start(bf16[32,4096]{1,0:T(8,128)(2,1)S(1)} %get-tuple-element.31.a), channel_id=1, source_target_pairs={{0,2},{2,0},{4,6},{6,4},{8,10},{10,8},{12,14},{14,12},{1,3},{3,1},... | collective-permute-start | bytes 786440 | tf_op jit(solution)/shard_map/ppermute | solution.py:215
  22.3 3.4 %collective-permute-start.6 = (bf16[32,4096]{1,0:T(8,128)(2,1)S(1)}, bf16[32,4096]{1,0:T(8,128)(2,1)S(1)}, u32[]{:S(2)}, u32[]{:S(2)}) collective-permute-start(bf16[32,4096]{1,0:T(8,128)(2,1)S(1)} %collective-permute-done.b), channel_id=1, source_target_pairs={{0,2},{2,0},{4,6},{6,4},{8,10},{10,8},{12,14},{14,12},{1,3},{3,1},... | collective-permute-start | bytes 786440 | tf_op jit(solution)/shard_map/ppermute | solution.py:215
  25.7 1.9 %collective-permute-start.7 = (bf16[32,4096]{1,0:T(8,128)(2,1)S(1)}, bf16[32,4096]{1,0:T(8,128)(2,1)S(1)}, u32[]{:S(2)}, u32[]{:S(2)}) collective-permute-start(bf16[32,4096]{1,0:T(8,128)(2,1)S(1)} %collective-permute-done.1.c), channel_id=1, source_target_pairs={{0,2},{2,0},{4,6},{6,4},{8,10},{10,8},{12,14},{14,12},{1,3},{3,1},... | collective-permute-start | bytes 786440 | tf_op jit(solution)/shard_map/ppermute | solution.py:215
  27.6 6.7 %collective-permute-done.2.d = bf16[32,4096]{1,0:T(8,128)(2,1)S(1)} collective-permute-done((bf16[32,4096]{1,0:T(8,128)(2,1)S(1)}, bf16[32,4096]{1,0:T(8,128)(2,1)S(1)}, u32[]{:S(2)}, u32[]{:S(2)}) %collective-permute-start.2) | collective-permute-done | bytes 262176 | tf_op jit(solution)/shard_map/ppermute | solution.py:214
  34.3 4.1 %collective-permute-start.8 = (bf16[32,4096]{1,0:T(8,128)(2,1)S(1)}, bf16[32,4096]{1,0:T(8,128)(2,1)S(1)}, u32[]{:S(2)}, u32[]{:S(2)}) collective-permute-start(bf16[32,4096]{1,0:T(8,128)(2,1)S(1)} %collective-permute-done.2.d), channel_id=1, source_target_pairs={{0,2},{2,0},{4,6},{6,4},{8,10},{10,8},{12,14},{14,12},{1,3},{3,1},... | collective-permute-start | bytes 786440 | tf_op jit(solution)/shard_map/ppermute | solution.py:215
  38.4 5.8 %collective-permute-start.3 = (bf16[128,4096]{1,0:T(8,128)(2,1)S(1)}, bf16[128,4096]{1,0:T(8,128)(2,1)S(1)}, u32[]{:S(2)}, u32[]{:S(2)}) collective-permute-start(bf16[128,4096]{1,0:T(8,128)(2,1)S(1)} %shard_map.96.mine.xa), channel_id=1, source_target_pairs={{0,1},{1,0},{2,3},{3,2},{4,5},{5,4},{6,7},{7,6},{8,9},{9,8},{10,11... | collective-permute-start | bytes 3145736 | tf_op jit(solution)/shard_map/ppermute | solution.py:217
  44.3 4.6 %collective-permute-done.8.d = bf16[32,4096]{1,0:T(8,128)(2,1)S(1)} collective-permute-done((bf16[32,4096]{1,0:T(8,128)(2,1)S(1)}, bf16[32,4096]{1,0:T(8,128)(2,1)S(1)}, u32[]{:S(2)}, u32[]{:S(2)}) %collective-permute-start.8) | collective-permute-done | bytes 262176 | tf_op jit(solution)/shard_map/ppermute | solution.py:215
  49.0 6.1 %collective-permute-start.9 = (bf16[128,4096]{1,0:T(8,128)(2,1)S(1)}, bf16[128,4096]{1,0:T(8,128)(2,1)S(1)}, u32[]{:S(2)}, u32[]{:S(2)}) collective-permute-start(bf16[128,4096]{1,0:T(8,128)(2,1)S(1)} %shard_map.98.mine.xc), channel_id=1, source_target_pairs={{0,1},{1,0},{2,3},{3,2},{4,5},{5,4},{6,7},{7,6},{8,9},{9,8},{10,11... | collective-permute-start | bytes 3145736 | tf_op jit(solution)/shard_map/ppermute | solution.py:219
  55.1 2.3 %shard_map.97 = (bf16[128,2048]{1,0:T(8,128)(2,1)S(1)}, bf16[128,2048]{1,0:T(8,128)(2,1)S(1)}, bf16[256,768]{1,0:T(8,128)(2,1)S(1)}) custom-call(s32[1,16]{1,0:T(1,128)S(1)} %copy-done.6, bf16[128,4096]{1,0:T(8,128)(2,1)S(1)} %shard_map.96.mine.xa, bf16[128,4096]{1,0:T(8,128)(2,1)S(1)} %collective-permute-done.3.mates.xb, bf16[2048,256]{1,0:T(8,128)(2,1)S(1)} %bitcast.9, ...), custom_call_target="tpu_custom_call" | custom-call | flops 1073741824 | bytes 6291456 | tf_op jit(solution)/shard_map/pallas_call | solution.py:40
  58.2 2.3 %shard_map.99 = (bf16[128,2048]{1,0:T(8,128)(2,1)S(1)}, bf16[128,2048]{1,0:T(8,128)(2,1)S(1)}, bf16[256,768]{1,0:T(8,128)(2,1)S(1)}) custom-call(s32[1,16]{1,0:T(1,128)S(1)} %copy-done.6, bf16[128,4096]{1,0:T(8,128)(2,1)S(1)} %shard_map.98.mine.xc, bf16[128,4096]{1,0:T(8,128)(2,1)S(1)} %collective-permute-done.9.mates.xd, bf16[2048,256]{1,0:T(8,128)(2,1)S(1)} %bitcast.10, ...), custom_call_target="tpu_custom_call" | custom-call | flops 1073741824 | bytes 6291456 | tf_op jit(solution)/shard_map/pallas_call | solution.py:40
  60.5 3.1 %shard_map.103 = (bf16[4,8,128,256]{3,2,1,0:T(8,128)(2,1)S(1)}, bf16[4,64,256]{2,1,0:T(8,128)(2,1)S(1)}, bf16[4,64,256]{2,1,0:T(8,128)(2,1)S(1)}, bf16[4,64,256]...) custom-call(s32[3]{0:T(128)S(1)} %pad_add_fusion.at, ...), custom_call_target="tpu_custom_call" | custom-call | flops 1610612736 | bytes 7340032 | tf_op jit(solution)/shard_map/pallas_call | solution.py:40
  67.6 3.6 %all-to-all-start = ((bf16[4,8,128,256]{3,2,1,0:T(8,128)(2,1)}), bf16[4,8,128,256]{3,2,1,0:T(8,128)(2,1)S(1)}, u32[]{:S(2)}, u32[]{:S(2)}) async-start(bf16[4,8,128,256]{3,2,1,0:T(8,128)(2,1)} %copy-done.3), calls=%async_computation | async-start | bytes 4194304 | tf_op jit(solution)/shard_map/all_to_all | solution.py:226
  71.3 1.9 %collective-permute-start.10 = (bf16[128,2048]{1,0:T(8,128)(2,1)}, bf16[128,2048]{1,0:T(8,128)(2,1)}, u32[]{:S(2)}, u32[]{:S(2)}) collective-permute-start(bf16[128,2048]{1,0:T(8,128)(2,1)} %copy-done.10), channel_id=1, source_target_pairs={{0,1},{1,0},{2,3},{3,2},{4,5},{5,4},{6,7},{7,6},{8,9},{9,8},{10,11... | collective-permute-start | bytes 1572872 | tf_op jit(solution)/shard_map/ppermute | solution.py:223
  73.2 24.5 %all-to-all-done.got = bf16[4,8,128,256]{3,2,1,0:T(8,128)(2,1)S(1)} async-done(((bf16[4,8,128,256]{3,2,1,0:T(8,128)(2,1)}), bf16[4,8,128,256]{3,2,1,0:T(8,128)(2,1)S(1)}, u32[]{:S(2)}, u32[]{:S(2)}) %all-to-all-start) | async-done | bytes 2097184 | tf_op jit(solution)/shard_map/all_to_all | solution.py:226
  98.8 8.6 %all-to-all-start.1 = ((bf16[8,128,256]{2,1,0:T(8,128)(2,1)}), bf16[8,128,256]{2,1,0:T(8,128)(2,1)S(1)}, u32[]{:S(2)}, u32[]{:S(2)}) async-start(bf16[8,128,256]{2,1,0:T(8,128)(2,1)} %shard_map.104), calls=%async_computation.1 | async-start | bytes 1048576 | tf_op jit(solution)/shard_map/all_to_all | solution.py:231
  107.4 3.3 %collective-permute-start.4 = (bf16[128,2048]{1,0:T(8,128)(2,1)}, bf16[128,2048]{1,0:T(8,128)(2,1)S(1)}, u32[]{:S(2)}, u32[]{:S(2)}) collective-permute-start(bf16[128,2048]{1,0:T(8,128)(2,1)} %copy-done.9), channel_id=1, source_target_pairs={{0,1},{1,0},{2,3},{3,2},{4,5},{5,4},{6,7},{7,6},{8,9},{9,8},{10,11... | collective-permute-start | bytes 1572872 | tf_op jit(solution)/shard_map/ppermute | solution.py:222
  111.9 3.8 %collective-permute-start.11 = (bf16[128,2048]{1,0:T(8,128)(2,1)S(1)}, bf16[128,2048]{1,0:T(8,128)(2,1)S(1)}, u32[]{:S(2)}, u32[]{:S(2)}) collective-permute-start(bf16[128,2048]{1,0:T(8,128)(2,1)S(1)} %shard_map.100), channel_id=1, source_target_pairs={{0,2},{2,0},{4,6},{6,4},{8,10},{10,8},{12,14},{14,12},{1,3},{3,1},... | collective-permute-start | bytes 1572872 | tf_op jit(solution)/shard_map/ppermute | solution.py:239
  115.6 3.6 %collective-permute-start.15 = (bf16[4,64,256]{2,1,0:T(8,128)(2,1)S(1)}, bf16[4,64,256]{2,1,0:T(8,128)(2,1)S(1)}, u32[]{:S(2)}, u32[]{:S(2)}) collective-permute-start(bf16[4,64,256]{2,1,0:T(8,128)(2,1)S(1)} %copy-done.15), channel_id=1, source_target_pairs={{0,16},{16,32},{32,48},{48,64},{64,80},{80,96},{96,112},{112,0},{1... | collective-permute-start | bytes 393224 | tf_op jit(solution)/shard_map/ppermute | solution.py:228
  119.3 4.0 %collective-permute-start.16 = (bf16[4,64,256]{2,1,0:T(8,128)(2,1)}, bf16[4,64,256]{2,1,0:T(8,128)(2,1)S(1)}, u32[]{:S(2)}, u32[]{:S(2)}) collective-permute-start(bf16[4,64,256]{2,1,0:T(8,128)(2,1)} %get-tuple-element.50), channel_id=1, source_target_pairs={{0,32},{16,48},{32,64},{48,80},{64,96},{80,112},{96,0},{112,16},{1... | collective-permute-start | bytes 393224 | tf_op jit(solution)/shard_map/ppermute | solution.py:228
  123.3 4.3 %collective-permute-start.17 = (bf16[4,64,256]{2,1,0:T(8,128)(2,1)}, bf16[4,64,256]{2,1,0:T(8,128)(2,1)S(1)}, u32[]{:S(2)}, u32[]{:S(2)}) collective-permute-start(bf16[4,64,256]{2,1,0:T(8,128)(2,1)} %get-tuple-element.51), channel_id=1, source_target_pairs={{0,48},{16,64},{32,80},{48,96},{64,112},{80,0},{96,16},{112,32},{1... | collective-permute-start | bytes 393224 | tf_op jit(solution)/shard_map/ppermute | solution.py:228
  127.6 4.0 %collective-permute-start.18 = (bf16[4,64,256]{2,1,0:T(8,128)(2,1)}, bf16[4,64,256]{2,1,0:T(8,128)(2,1)S(1)}, u32[]{:S(2)}, u32[]{:S(2)}) collective-permute-start(bf16[4,64,256]{2,1,0:T(8,128)(2,1)} %copy-done.13), channel_id=1, source_target_pairs={{0,64},{16,80},{32,96},{48,112},{64,0},{80,16},{96,32},{112,48},{1... | collective-permute-start | bytes 393224 | tf_op jit(solution)/shard_map/ppermute | solution.py:228
  131.6 4.9 %collective-permute-start.19 = (bf16[4,64,256]{2,1,0:T(8,128)(2,1)}, bf16[4,64,256]{2,1,0:T(8,128)(2,1)S(1)}, u32[]{:S(2)}, u32[]{:S(2)}) collective-permute-start(bf16[4,64,256]{2,1,0:T(8,128)(2,1)} %copy-done.12), channel_id=1, source_target_pairs={{0,80},{16,96},{32,112},{48,0},{64,16},{80,32},{96,48},{112,64},{1... | collective-permute-start | bytes 393224 | tf_op jit(solution)/shard_map/ppermute | solution.py:228
  136.6 4.6 %collective-permute-start.20 = (bf16[4,64,256]{2,1,0:T(8,128)(2,1)}, bf16[4,64,256]{2,1,0:T(8,128)(2,1)S(1)}, u32[]{:S(2)}, u32[]{:S(2)}) collective-permute-start(bf16[4,64,256]{2,1,0:T(8,128)(2,1)} %copy-done.11), channel_id=1, source_target_pairs={{0,96},{16,112},{32,0},{48,16},{64,32},{80,48},{96,64},{112,80},{1... | collective-permute-start | bytes 393224 | tf_op jit(solution)/shard_map/ppermute | solution.py:228
  141.2 3.1 %collective-permute-start.21 = (bf16[4,64,256]{2,1,0:T(8,128)(2,1)S(1)}, bf16[4,64,256]{2,1,0:T(8,128)(2,1)S(1)}, u32[]{:S(2)}, u32[]{:S(2)}) collective-permute-start(bf16[4,64,256]{2,1,0:T(8,128)(2,1)S(1)} %get-tuple-element.55), channel_id=1, source_target_pairs={{0,112},{16,0},{32,16},{48,32},{64,48},{80,64},{96,80},{112,96},{1... | collective-permute-start | bytes 393224 | tf_op jit(solution)/shard_map/ppermute | solution.py:228
  147.3 3.9 %collective-permute-start.13 = (bf16[32,2048]{1,0:T(8,128)(2,1)S(1)}, bf16[32,2048]{1,0:T(8,128)(2,1)S(1)}, u32[]{:S(2)}, u32[]{:S(2)}) collective-permute-start(bf16[32,2048]{1,0:T(8,128)(2,1)S(1)} %get-tuple-element.41), channel_id=1, source_target_pairs={{4,0},{14,2},{8,4},{2,6},{12,8},{6,10},{0,12},{10,14},{5,1},{15,3}... | collective-permute-start | bytes 393224 | tf_op jit(solution)/shard_map/ppermute | solution.py:242
  151.3 4.6 %collective-permute-start.14 = (bf16[32,2048]{1,0:T(8,128)(2,1)S(1)}, bf16[32,2048]{1,0:T(8,128)(2,1)S(1)}, u32[]{:S(2)}, u32[]{:S(2)}) collective-permute-start(bf16[32,2048]{1,0:T(8,128)(2,1)S(1)} %get-tuple-element.42), channel_id=1, source_target_pairs={{10,0},{8,2},{14,4},{12,6},{2,8},{0,10},{6,12},{4,14},{11,1},{9,3}... | collective-permute-start | bytes 393224 | tf_op jit(solution)/shard_map/ppermute | solution.py:242
  156.6 2.2 %collective-permute-start.22 = (bf16[64,256]{1,0:T(8,128)(2,1)S(1)}, bf16[64,256]{1,0:T(8,128)(2,1)S(1)}, u32[]{:S(2)}, u32[]{:S(2)}) collective-permute-start(bf16[64,256]{1,0:T(8,128)(2,1)S(1)} %get-tuple-element.57), channel_id=1, source_target_pairs={{0,128},{128,256},{256,384},{384,0},{1,129},{129,257},{257,385},{3... | collective-permute-start | bytes 98312 | tf_op jit(solution)/shard_map/ppermute | solution.py:234
  158.8 3.7 %collective-permute-start.23 = (bf16[64,256]{1,0:T(8,128)(2,1)S(1)}, bf16[64,256]{1,0:T(8,128)(2,1)S(1)}, u32[]{:S(2)}, u32[]{:S(2)}) collective-permute-start(bf16[64,256]{1,0:T(8,128)(2,1)S(1)} %get-tuple-element.58), channel_id=1, source_target_pairs={{0,256},{128,384},{256,0},{384,128},{1,257},{129,385},{257,1},{385... | collective-permute-start | bytes 98312 | tf_op jit(solution)/shard_map/ppermute | solution.py:234
  162.5 2.5 %collective-permute-start.24 = (bf16[64,256]{1,0:T(8,128)(2,1)S(1)}, bf16[64,256]{1,0:T(8,128)(2,1)S(1)}, u32[]{:S(2)}, u32[]{:S(2)}) collective-permute-start(bf16[64,256]{1,0:T(8,128)(2,1)S(1)} %get-tuple-element.59), channel_id=1, source_target_pairs={{0,384},{128,0},{256,128},{384,256},{1,385},{129,1},{257,129},{385... | collective-permute-start | bytes 98312 | tf_op jit(solution)/shard_map/ppermute | solution.py:234
  (67 shorter events, 18.6 us)
Async XLA Ops:
  5.2 17.1 %collective-permute-start = (bf16[32,4096]{1,0:T(8,128)(2,1)S(1)}, bf16[32,4096]{1,0:T(8,128)(2,1)S(1)}, u32[]{:S(2)}, u32[]{:S(2)}) collective-permute-start(bf16[32,4096]{1,0:T(8,128)(2,1)S(1)} %get-tuple-element.32), channel_id=1, source_target_pairs={{0,14},{2,4},{4,2},{6,8},{8,6},{10,12},{12,10},{14,0},{1,15},{3,5}... | collective-permute-start | bytes 786440 | tf_op jit(solution)/shard_map/ppermute | solution.py:214
  11.1 14.5 %collective-permute-start.1 = (bf16[32,4096]{1,0:T(8,128)(2,1)S(1)}, bf16[32,4096]{1,0:T(8,128)(2,1)S(1)}, u32[]{:S(2)}, u32[]{:S(2)}) collective-permute-start(bf16[32,4096]{1,0:T(8,128)(2,1)S(1)} %get-tuple-element.33), channel_id=1, source_target_pairs={{0,4},{2,14},{4,8},{6,2},{8,12},{10,6},{12,0},{14,10},{1,5},{3,15}... | collective-permute-start | bytes 786440 | tf_op jit(solution)/shard_map/ppermute | solution.py:214
  13.1 21.2 %collective-permute-start.2 = (bf16[32,4096]{1,0:T(8,128)(2,1)S(1)}, bf16[32,4096]{1,0:T(8,128)(2,1)S(1)}, u32[]{:S(2)}, u32[]{:S(2)}) collective-permute-start(bf16[32,4096]{1,0:T(8,128)(2,1)S(1)} %get-tuple-element.34), channel_id=1, source_target_pairs={{0,10},{2,8},{4,14},{6,12},{8,2},{10,0},{12,6},{14,4},{1,11},{3,9}... | collective-permute-start | bytes 786440 | tf_op jit(solution)/shard_map/ppermute | solution.py:214
  20.0 35.1 %copy-start = (bf16[1,2048,256]{2,1,0:T(8,128)(2,1)S(1)}, bf16[1,2048,256]{2,1,0:T(8,128)(2,1)}, u32[]{:S(2)}) copy-start(bf16[1,2048,256]{2,1,0:T(8,128)(2,1)} %param.12) | copy-start | bytes 3145732
  20.0 35.1 %copy-start.1 = (bf16[1,2048,256]{2,1,0:T(8,128)(2,1)S(1)}, bf16[1,2048,256]{2,1,0:T(8,128)(2,1)}, u32[]{:S(2)}) copy-start(bf16[1,2048,256]{2,1,0:T(8,128)(2,1)} %param.13) | copy-start | bytes 3145732
  20.0 35.1 %copy-start.2 = (bf16[1,256,2048]{2,1,0:T(8,128)(2,1)S(1)}, bf16[1,256,2048]{2,1,0:T(8,128)(2,1)}, u32[]{:S(2)}) copy-start(bf16[1,256,2048]{2,1,0:T(8,128)(2,1)} %param.14) | copy-start | bytes 3145732
  20.1 35.1 %copy-start.6 = (s32[1,16]{1,0:T(1,128)S(1)}, s32[1,16]{1,0:T(1,128)}, u32[]{:S(2)}) copy-start(s32[1,16]{1,0:T(1,128)} %touched.3) | copy-start | bytes 196
  20.1 24.2 %collective-permute-start.5 = (bf16[32,4096]{1,0:T(8,128)(2,1)S(1)}, bf16[32,4096]{1,0:T(8,128)(2,1)S(1)}, u32[]{:S(2)}, u32[]{:S(2)}) collective-permute-start(bf16[32,4096]{1,0:T(8,128)(2,1)S(1)} %get-tuple-element.31.a), channel_id=1, source_target_pairs={{0,2},{2,0},{4,6},{6,4},{8,10},{10,8},{12,14},{14,12},{1,3},{3,1},... | collective-permute-start | bytes 786440 | tf_op jit(solution)/shard_map/ppermute | solution.py:215
  22.3 22.0 %collective-permute-start.6 = (bf16[32,4096]{1,0:T(8,128)(2,1)S(1)}, bf16[32,4096]{1,0:T(8,128)(2,1)S(1)}, u32[]{:S(2)}, u32[]{:S(2)}) collective-permute-start(bf16[32,4096]{1,0:T(8,128)(2,1)S(1)} %collective-permute-done.b), channel_id=1, source_target_pairs={{0,2},{2,0},{4,6},{6,4},{8,10},{10,8},{12,14},{14,12},{1,3},{3,1},... | collective-permute-start | bytes 786440 | tf_op jit(solution)/shard_map/ppermute | solution.py:215
  25.7 18.6 %collective-permute-start.7 = (bf16[32,4096]{1,0:T(8,128)(2,1)S(1)}, bf16[32,4096]{1,0:T(8,128)(2,1)S(1)}, u32[]{:S(2)}, u32[]{:S(2)}) collective-permute-start(bf16[32,4096]{1,0:T(8,128)(2,1)S(1)} %collective-permute-done.1.c), channel_id=1, source_target_pairs={{0,2},{2,0},{4,6},{6,4},{8,10},{10,8},{12,14},{14,12},{1,3},{3,1},... | collective-permute-start | bytes 786440 | tf_op jit(solution)/shard_map/ppermute | solution.py:215
  34.3 14.6 %collective-permute-start.8 = (bf16[32,4096]{1,0:T(8,128)(2,1)S(1)}, bf16[32,4096]{1,0:T(8,128)(2,1)S(1)}, u32[]{:S(2)}, u32[]{:S(2)}) collective-permute-start(bf16[32,4096]{1,0:T(8,128)(2,1)S(1)} %collective-permute-done.2.d), channel_id=1, source_target_pairs={{0,2},{2,0},{4,6},{6,4},{8,10},{10,8},{12,14},{14,12},{1,3},{3,1},... | collective-permute-start | bytes 786440 | tf_op jit(solution)/shard_map/ppermute | solution.py:215
  38.4 16.6 %collective-permute-start.3 = (bf16[128,4096]{1,0:T(8,128)(2,1)S(1)}, bf16[128,4096]{1,0:T(8,128)(2,1)S(1)}, u32[]{:S(2)}, u32[]{:S(2)}) collective-permute-start(bf16[128,4096]{1,0:T(8,128)(2,1)S(1)} %shard_map.96.mine.xa), channel_id=1, source_target_pairs={{0,1},{1,0},{2,3},{3,2},{4,5},{5,4},{6,7},{7,6},{8,9},{9,8},{10,11... | collective-permute-start | bytes 3145736 | tf_op jit(solution)/shard_map/ppermute | solution.py:217
  49.0 9.2 %collective-permute-start.9 = (bf16[128,4096]{1,0:T(8,128)(2,1)S(1)}, bf16[128,4096]{1,0:T(8,128)(2,1)S(1)}, u32[]{:S(2)}, u32[]{:S(2)}) collective-permute-start(bf16[128,4096]{1,0:T(8,128)(2,1)S(1)} %shard_map.98.mine.xc), channel_id=1, source_target_pairs={{0,1},{1,0},{2,3},{3,2},{4,5},{5,4},{6,7},{7,6},{8,9},{9,8},{10,11... | collective-permute-start | bytes 3145736 | tf_op jit(solution)/shard_map/ppermute | solution.py:219
  67.6 30.1 %all-to-all-start = ((bf16[4,8,128,256]{3,2,1,0:T(8,128)(2,1)}), bf16[4,8,128,256]{3,2,1,0:T(8,128)(2,1)S(1)}, u32[]{:S(2)}, u32[]{:S(2)}) async-start(bf16[4,8,128,256]{3,2,1,0:T(8,128)(2,1)} %copy-done.3), calls=%async_computation | async-start | bytes 4194304 | tf_op jit(solution)/shard_map/all_to_all | solution.py:226
  71.3 39.4 %collective-permute-start.10 = (bf16[128,2048]{1,0:T(8,128)(2,1)}, bf16[128,2048]{1,0:T(8,128)(2,1)}, u32[]{:S(2)}, u32[]{:S(2)}) collective-permute-start(bf16[128,2048]{1,0:T(8,128)(2,1)} %copy-done.10), channel_id=1, source_target_pairs={{0,1},{1,0},{2,3},{3,2},{4,5},{5,4},{6,7},{7,6},{8,9},{9,8},{10,11... | collective-permute-start | bytes 1572872 | tf_op jit(solution)/shard_map/ppermute | solution.py:223
  98.8 16.9 %copy-start.15 = (bf16[4,64,256]{2,1,0:T(8,128)(2,1)S(1)}, bf16[4,64,256]{2,1,0:T(8,128)(2,1)}, u32[]{:S(2)}) copy-start(bf16[4,64,256]{2,1,0:T(8,128)(2,1)} %copy-done.14) | copy-start | bytes 393220
  98.8 68.7 %all-to-all-start.1 = ((bf16[8,128,256]{2,1,0:T(8,128)(2,1)}), bf16[8,128,256]{2,1,0:T(8,128)(2,1)S(1)}, u32[]{:S(2)}, u32[]{:S(2)}) async-start(bf16[8,128,256]{2,1,0:T(8,128)(2,1)} %shard_map.104), calls=%async_computation.1 | async-start | bytes 1048576 | tf_op jit(solution)/shard_map/all_to_all | solution.py:231
  107.4 29.2 %collective-permute-start.4 = (bf16[128,2048]{1,0:T(8,128)(2,1)}, bf16[128,2048]{1,0:T(8,128)(2,1)S(1)}, u32[]{:S(2)}, u32[]{:S(2)}) collective-permute-start(bf16[128,2048]{1,0:T(8,128)(2,1)} %copy-done.9), channel_id=1, source_target_pairs={{0,1},{1,0},{2,3},{3,2},{4,5},{5,4},{6,7},{7,6},{8,9},{9,8},{10,11... | collective-permute-start | bytes 1572872 | tf_op jit(solution)/shard_map/ppermute | solution.py:222
  111.9 29.3 %collective-permute-start.11 = (bf16[128,2048]{1,0:T(8,128)(2,1)S(1)}, bf16[128,2048]{1,0:T(8,128)(2,1)S(1)}, u32[]{:S(2)}, u32[]{:S(2)}) collective-permute-start(bf16[128,2048]{1,0:T(8,128)(2,1)S(1)} %shard_map.100), channel_id=1, source_target_pairs={{0,2},{2,0},{4,6},{6,4},{8,10},{10,8},{12,14},{14,12},{1,3},{3,1},... | collective-permute-start | bytes 1572872 | tf_op jit(solution)/shard_map/ppermute | solution.py:239
  115.6 12.0 %collective-permute-start.15 = (bf16[4,64,256]{2,1,0:T(8,128)(2,1)S(1)}, bf16[4,64,256]{2,1,0:T(8,128)(2,1)S(1)}, u32[]{:S(2)}, u32[]{:S(2)}) collective-permute-start(bf16[4,64,256]{2,1,0:T(8,128)(2,1)S(1)} %copy-done.15), channel_id=1, source_target_pairs={{0,16},{16,32},{32,48},{48,64},{64,80},{80,96},{96,112},{112,0},{1... | collective-permute-start | bytes 393224 | tf_op jit(solution)/shard_map/ppermute | solution.py:228
  119.3 12.3 %collective-permute-start.16 = (bf16[4,64,256]{2,1,0:T(8,128)(2,1)}, bf16[4,64,256]{2,1,0:T(8,128)(2,1)S(1)}, u32[]{:S(2)}, u32[]{:S(2)}) collective-permute-start(bf16[4,64,256]{2,1,0:T(8,128)(2,1)} %get-tuple-element.50), channel_id=1, source_target_pairs={{0,32},{16,48},{32,64},{48,80},{64,96},{80,112},{96,0},{112,16},{1... | collective-permute-start | bytes 393224 | tf_op jit(solution)/shard_map/ppermute | solution.py:228
  123.3 22.1 %collective-permute-start.17 = (bf16[4,64,256]{2,1,0:T(8,128)(2,1)}, bf16[4,64,256]{2,1,0:T(8,128)(2,1)S(1)}, u32[]{:S(2)}, u32[]{:S(2)}) collective-permute-start(bf16[4,64,256]{2,1,0:T(8,128)(2,1)} %get-tuple-element.51), channel_id=1, source_target_pairs={{0,48},{16,64},{32,80},{48,96},{64,112},{80,0},{96,16},{112,32},{1... | collective-permute-start | bytes 393224 | tf_op jit(solution)/shard_map/ppermute | solution.py:228
  127.6 19.7 %collective-permute-start.18 = (bf16[4,64,256]{2,1,0:T(8,128)(2,1)}, bf16[4,64,256]{2,1,0:T(8,128)(2,1)S(1)}, u32[]{:S(2)}, u32[]{:S(2)}) collective-permute-start(bf16[4,64,256]{2,1,0:T(8,128)(2,1)} %copy-done.13), channel_id=1, source_target_pairs={{0,64},{16,80},{32,96},{48,112},{64,0},{80,16},{96,32},{112,48},{1... | collective-permute-start | bytes 393224 | tf_op jit(solution)/shard_map/ppermute | solution.py:228
  131.6 19.6 %collective-permute-start.19 = (bf16[4,64,256]{2,1,0:T(8,128)(2,1)}, bf16[4,64,256]{2,1,0:T(8,128)(2,1)S(1)}, u32[]{:S(2)}, u32[]{:S(2)}) collective-permute-start(bf16[4,64,256]{2,1,0:T(8,128)(2,1)} %copy-done.12), channel_id=1, source_target_pairs={{0,80},{16,96},{32,112},{48,0},{64,16},{80,32},{96,48},{112,64},{1... | collective-permute-start | bytes 393224 | tf_op jit(solution)/shard_map/ppermute | solution.py:228
  136.6 19.3 %collective-permute-start.20 = (bf16[4,64,256]{2,1,0:T(8,128)(2,1)}, bf16[4,64,256]{2,1,0:T(8,128)(2,1)S(1)}, u32[]{:S(2)}, u32[]{:S(2)}) collective-permute-start(bf16[4,64,256]{2,1,0:T(8,128)(2,1)} %copy-done.11), channel_id=1, source_target_pairs={{0,96},{16,112},{32,0},{48,16},{64,32},{80,48},{96,64},{112,80},{1... | collective-permute-start | bytes 393224 | tf_op jit(solution)/shard_map/ppermute | solution.py:228
  141.2 14.8 %collective-permute-start.21 = (bf16[4,64,256]{2,1,0:T(8,128)(2,1)S(1)}, bf16[4,64,256]{2,1,0:T(8,128)(2,1)S(1)}, u32[]{:S(2)}, u32[]{:S(2)}) collective-permute-start(bf16[4,64,256]{2,1,0:T(8,128)(2,1)S(1)} %get-tuple-element.55), channel_id=1, source_target_pairs={{0,112},{16,0},{32,16},{48,32},{64,48},{80,64},{96,80},{112,96},{1... | collective-permute-start | bytes 393224 | tf_op jit(solution)/shard_map/ppermute | solution.py:228
  145.4 17.1 %collective-permute-start.12 = (bf16[32,2048]{1,0:T(8,128)(2,1)S(1)}, bf16[32,2048]{1,0:T(8,128)(2,1)S(1)}, u32[]{:S(2)}, u32[]{:S(2)}) collective-permute-start(bf16[32,2048]{1,0:T(8,128)(2,1)S(1)} %get-tuple-element.40), channel_id=1, source_target_pairs={{14,0},{4,2},{2,4},{8,6},{6,8},{12,10},{10,12},{0,14},{15,1},{5,3}... | collective-permute-start | bytes 393224 | tf_op jit(solution)/shard_map/ppermute | solution.py:242
  147.3 17.8 %collective-permute-start.13 = (bf16[32,2048]{1,0:T(8,128)(2,1)S(1)}, bf16[32,2048]{1,0:T(8,128)(2,1)S(1)}, u32[]{:S(2)}, u32[]{:S(2)}) collective-permute-start(bf16[32,2048]{1,0:T(8,128)(2,1)S(1)} %get-tuple-element.41), channel_id=1, source_target_pairs={{4,0},{14,2},{8,4},{2,6},{12,8},{6,10},{0,12},{10,14},{5,1},{15,3}... | collective-permute-start | bytes 393224 | tf_op jit(solution)/shard_map/ppermute | solution.py:242
  151.3 13.8 %collective-permute-start.14 = (bf16[32,2048]{1,0:T(8,128)(2,1)S(1)}, bf16[32,2048]{1,0:T(8,128)(2,1)S(1)}, u32[]{:S(2)}, u32[]{:S(2)}) collective-permute-start(bf16[32,2048]{1,0:T(8,128)(2,1)S(1)} %get-tuple-element.42), channel_id=1, source_target_pairs={{10,0},{8,2},{14,4},{12,6},{2,8},{0,10},{6,12},{4,14},{11,1},{9,3}... | collective-permute-start | bytes 393224 | tf_op jit(solution)/shard_map/ppermute | solution.py:242
  156.6 9.6 %collective-permute-start.22 = (bf16[64,256]{1,0:T(8,128)(2,1)S(1)}, bf16[64,256]{1,0:T(8,128)(2,1)S(1)}, u32[]{:S(2)}, u32[]{:S(2)}) collective-permute-start(bf16[64,256]{1,0:T(8,128)(2,1)S(1)} %get-tuple-element.57), channel_id=1, source_target_pairs={{0,128},{128,256},{256,384},{384,0},{1,129},{129,257},{257,385},{3... | collective-permute-start | bytes 98312 | tf_op jit(solution)/shard_map/ppermute | solution.py:234
  158.8 7.4 %collective-permute-start.23 = (bf16[64,256]{1,0:T(8,128)(2,1)S(1)}, bf16[64,256]{1,0:T(8,128)(2,1)S(1)}, u32[]{:S(2)}, u32[]{:S(2)}) collective-permute-start(bf16[64,256]{1,0:T(8,128)(2,1)S(1)} %get-tuple-element.58), channel_id=1, source_target_pairs={{0,256},{128,384},{256,0},{384,128},{1,257},{129,385},{257,1},{385... | collective-permute-start | bytes 98312 | tf_op jit(solution)/shard_map/ppermute | solution.py:234
  162.5 5.0 %collective-permute-start.24 = (bf16[64,256]{1,0:T(8,128)(2,1)S(1)}, bf16[64,256]{1,0:T(8,128)(2,1)S(1)}, u32[]{:S(2)}, u32[]{:S(2)}) collective-permute-start(bf16[64,256]{1,0:T(8,128)(2,1)S(1)} %get-tuple-element.59), channel_id=1, source_target_pairs={{0,384},{128,0},{256,128},{384,256},{1,385},{129,1},{257,129},{385... | collective-permute-start | bytes 98312 | tf_op jit(solution)/shard_map/ppermute | solution.py:234
  (11 other events, 11.3 us)

commit v3 on v2

v3 whole, which is shorter than its diff:
```python
import functools

import jax
import jax.numpy as jnp
from jax import lax
from jax.experimental import pallas as pl
from jax.experimental.pallas import tpu as pltpu
from jax.sharding import Mesh, PartitionSpec as P

EW = 4
SHARE = 192
TILE = 16
X, Z, Y, C = 4, 8, 8, 2
AXES = ("x", "z", "y", "c")
CAP = 32
D = 2048
HID = 256
SHARE = 192
bf16 = jnp.bfloat16
f32 = jnp.float32

PERM1 = [(i, (i - 1) % Y if i % 2 == 0 else (i + 1) % Y) for i in range(Y)]
PERM2 = [(i, (i + 2) % Y if i % 2 == 0 else (i - 2) % Y) for i in range(Y)]
PERM3 = [(i, ((i + 4) ^ 1) % Y) for i in range(Y)]
PAIR = [(i, i ^ 1) for i in range(Y)]
SWAP = [(0, 1), (1, 0)]
VMEM_LIMIT = 16 * 1024 * 1024
VMEM_WIDE = 50 * 1024 * 1024
VMEM_WHOLE = 62 * 1024 * 1024

VM = pl.BlockSpec(memory_space=pltpu.VMEM)
SM = pl.BlockSpec(memory_space=pltpu.SMEM)
HB = pl.BlockSpec(memory_space=pl.ANY)
TN = (((0,), (0,)), ((), ()))
NT = (((1,), (1,)), ((), ()))
NN = (((1,), (0,)), ((), ()))


def mm(a, b, dims=NN):
    return lax.dot_general(a, b, dims, preferred_element_type=f32)


class Load:
    def __init__(self, copy, ref):
        self.copy, self.ref, self.waited = copy, ref, False

    def get(self):
        if not self.waited:
            self.copy.wait()
            self.waited = True
        return self.ref


class Store:
    def __init__(self, copy, ref):
        self.copy, self.ref = copy, ref

    def send(self):
        self.copy.start()


def call(kernel, outs, args, flops, moved, space="", out_space="", scratch=(), limit=VMEM_LIMIT):
    single = not isinstance(outs, tuple)
    outs = (outs,) if single else outs
    space = space or "v" * len(args)
    out_space = out_space or "v" * len(outs)
    kind = {"s": SM, "v": VM, "h": HB, "p": HB}
    flat = tuple(args) + outs
    marks = space + out_space
    moving = [i for i, m in enumerate(marks) if m in "hp"]
    parts = outs[0].shape[0] if out_space == "p" else 1
    n_in = len(args)

    def run(*refs):
        main, extra = list(refs[:len(flat)]), refs[len(flat):]
        own, held = extra[:len(scratch)], extra[len(scratch):len(scratch) + len(moving)]
        sems = extra[-1] if moving else None
        loads, stores = [], []
        for k, i in enumerate(moving):
            if i < n_in:
                copy = pltpu.make_async_copy(main[i], held[k], sems.at[k])
                copy.start()
                main[i] = Load(copy, held[k])
                loads.append(main[i])
            elif marks[i] == "h":
                main[i] = Store(pltpu.make_async_copy(held[k], main[i], sems.at[k]), held[k])
                stores.append(main[i])
            else:
                stores = [
                    Store(pltpu.make_async_copy(held[k].at[j], main[i].at[j], sems.at[k + j]), held[k].at[j])
                    for j in range(parts)
                ]
                main[i:] = stores
        kernel(*main, *own)
        for load in loads:
            load.get()
        for store in stores:
            store.copy.wait()

    extra = list(scratch)
    if moving:
        extra += [pltpu.VMEM(flat[i].shape, flat[i].dtype) for i in moving]
        extra.append(pltpu.SemaphoreType.DMA((len(moving) + parts - 1,)))
    got = pl.pallas_call(
        run,
        out_shape=outs,
        in_specs=[kind[m] for m in space],
        out_specs=tuple(kind[m] for m in out_space),
        scratch_shapes=extra,
        compiler_params=pltpu.CompilerParams(vmem_limit_bytes=limit),
        cost_estimate=pl.CostEstimate(flops=flops, bytes_accessed=moved, transcendentals=0),
    )(*args)
    return got[0] if single else got


def shaped(*shape, dtype=bf16):
    return jax.ShapeDtypeStruct(shape, dtype)


def back_perm(perm):
    return [(b, a) for a, b in perm]


def place_kernel(at, ids, gate, tokens, cotangent, own, one, two, three, placer_out, gate_out):
    ids, gate = ids.get(), gate.get()
    y = at[2]
    odd = y % 2
    pair = y // 2
    rows = ids.shape[1]
    e = ids[...]
    expert = lax.broadcasted_iota(jnp.int32, (8, rows), 0)
    onehot = (expert == e).astype(f32)
    before = (
        lax.broadcasted_iota(jnp.int32, (rows, rows), 0)
        < lax.broadcasted_iota(jnp.int32, (rows, rows), 1)
    ).astype(bf16)
    earlier = mm(onehot.astype(bf16), before)
    slot = jnp.sum(onehot * earlier, axis=0, keepdims=True).astype(jnp.int32)
    away = (e - pair + EW) & 3
    near = 1 + 2 * odd
    near = 4 - near
    place = jnp.where(away == 0, 0, jnp.where(away == 2, 3, jnp.where(away == near, 1, 2)))
    target = place * CAP + slot
    placer = (lax.broadcasted_iota(jnp.int32, (rows, rows), 0) == target).astype(f32)
    placed_gate = jnp.sum(placer * gate[...], axis=1, keepdims=True)
    gate_out[...] = jnp.broadcast_to(placed_gate, (rows, rows))
    placer = placer.astype(bf16)
    placer_out[...] = placer
    xs = mm(placer, tokens.get()[...]).astype(bf16)
    ds = (mm(placer, cotangent.get()[...]) * placed_gate).astype(bf16)
    for k, ref in enumerate((own, one, two, three)):
        ref[:, :D] = xs[k * CAP:(k + 1) * CAP]
        ref[:, D:] = ds[k * CAP:(k + 1) * CAP]


def join_kernel(a, b, c, d, out):
    for k, ref in enumerate((a, b, c, d)):
        out[k * CAP:(k + 1) * CAP, :] = ref[...]


def join(parts):
    return call(join_kernel, shaped(4 * CAP, 2 * D), parts, 0, 4 * CAP * 4 * D * 2)


def layer_kernel(n, with_out, touched, *refs):
    blocks, (wg, wu, wd), grads = refs[:n], refs[n:n + 3], refs[n + 3]
    outs = refs[n + 4:]
    row = jnp.zeros((1, HID), f32)
    tile = lax.broadcasted_iota(jnp.int32, (1, HID), 1) // TILE
    for k in range(HID // TILE):
        row = jnp.where(tile == k, touched[0, k].astype(f32), row)
    for k in range(n):
        xs = blocks[k][:, :D]
        ds = blocks[k][:, D:]
        h = mm(xs, wg[...])
        u = mm(xs, wu[...])
        g = mm(ds, wd[...], NT)
        s = 1.0 / (1.0 + jnp.exp(-h))
        act = (h * s * u).astype(bf16)
        here = slice(k * 4 * CAP, (k + 1) * 4 * CAP)
        if with_out:
            outs[k].ref[...] = mm(act, wd[...]).astype(bf16)
            outs[k].send()
        else:
            outs[0][here] = act
        grads[here, :HID] = (g * u * (s * (1.0 + h * (1.0 - s))) * row).astype(bf16)
        grads[here, HID:2 * HID] = (g * (h * s) * row).astype(bf16)
        grads[here, 2 * HID:] = (act.astype(f32) * row).astype(bf16)


def layer(touched, blocks, wg, wu, wd, with_out):
    n = len(blocks)
    rows = n * 4 * CAP
    return call(
        functools.partial(layer_kernel, n, with_out),
        (shaped(rows, 3 * HID),) + ((shaped(4 * CAP, D),) * n if with_out else (shaped(rows, HID),)),
        (touched, *blocks, wg, wu, wd),
        2 * 4 * rows * D * HID, 2 * (3 * D * HID + rows * 3 * D),
        "s" + "v" * (n + 3), "v" + ("h" * n if with_out else "v"),
    )


def out_kernel(mine, mates, wd, out_mine, out_mates):
    out_mates.ref[...] = mm(mates[...], wd[...]).astype(bf16)
    out_mates.send()
    out_mine.ref[...] = mm(mine[...], wd[...]).astype(bf16)
    out_mine.send()


STEP = 512


def delta_kernel(xa, xb, xc, xd, ga, gb, gc, *outs):
    grads = jnp.concatenate([ga[...], gb[...], gc[...]], axis=0)
    left_over = [Z * SHARE] * X
    for base, lo, n in ((0, 0, 2), (D, 2 * HID, 1)):
        right = grads[:, lo:lo + n * HID]
        for c0 in range(0, D, STEP):
            cols = slice(base + c0, base + c0 + STEP)
            left = jnp.concatenate([r[:, cols] for r in (xa, xb, xc, xd)], axis=0)
            out = mm(left, right, TN).astype(bf16)
            for k in range(n):
                start = (k if n == 2 else 2) * D + c0
                for rep in range(start // SHARE, (start + STEP - 1) // SHARE + 1):
                    first = max(rep * SHARE, start)
                    last = min((rep + 1) * SHARE, start + STEP)
                    put = slice(first - rep * SHARE, last - rep * SHARE)
                    x = rep // Z
                    outs[x].ref[rep % Z, put, :] = out[first - start:last - start, k * HID:(k + 1) * HID]
                    left_over[x] -= last - first
                    if left_over[x] == 0:
                        outs[x].send()


def delta(xs, grads):
    return call(
        delta_kernel, shaped(X, Z, SHARE, HID), (*xs, *grads),
        2 * 3 * 16 * CAP * D * HID, 2 * (16 * CAP * 2 * D + 3 * D * HID), "v" * 7, "p", limit=VMEM_WIDE,
    )


ROWS = 64


def fold_kernel(n, chunks, scale, got, out, held, total, in_sems, out_sems):
    per = got.shape[1] // chunks
    loads, stores = [], []
    for c in range(chunks):
        here = pl.ds(c * per, per)
        loads.append(pltpu.make_async_copy(got.at[:, here], held.at[:, here], in_sems.at[c]))
        stores.append(pltpu.make_async_copy(total.at[here], out.at[here], out_sems.at[c]))
        loads[c].start()
    for c in range(chunks):
        loads[c].wait()
        for i in range(c * per, (c + 1) * per):
            value = held[0, i].astype(f32)
            for k in range(1, n):
                value += held[k, i].astype(f32)
            total[i] = (value * scale).astype(bf16)
        stores[c].start()
    for store in stores:
        store.wait()


def fold(got, chunks, scale):
    n = got.shape[0]
    shape = got.shape[1:]
    got = got.reshape(n, -1, ROWS, HID)
    out = pl.pallas_call(
        functools.partial(fold_kernel, n, chunks, scale),
        out_shape=shaped(*got.shape[1:]),
        in_specs=[HB],
        out_specs=HB,
        scratch_shapes=[
            pltpu.VMEM(got.shape, bf16),
            pltpu.VMEM(got.shape[1:], bf16),
            pltpu.SemaphoreType.DMA((chunks,)),
            pltpu.SemaphoreType.DMA((chunks,)),
        ],
        compiler_params=pltpu.CompilerParams(vmem_limit_bytes=VMEM_WHOLE),
        cost_estimate=pl.CostEstimate(flops=0, bytes_accessed=2 * got.size, transcendentals=0),
    )(got)
    return out.reshape(shape)


def add_kernel(a, b, out):
    out.ref[...] = (a[...].astype(f32) + b[...].astype(f32)).astype(bf16)
    out.send()


def add_split_kernel(a, b, c, *outs):
    a, b, c = a.get(), b.get(), c.get()
    for k in range(4):
        here = slice(k * CAP, (k + 1) * CAP)
        outs[k].ref[...] = (a[here].astype(f32) + b[here].astype(f32) + c[here].astype(f32)).astype(bf16)
        outs[k].send()


def mixed_kernel(a, b, c, d, gate, placer, out):
    parts = []
    for k, ref in enumerate((a, b, c, d)):
        parts.append((ref[...].astype(f32) * gate[k * CAP:(k + 1) * CAP, :1]).astype(bf16))
    out[...] = mm(placer[...], jnp.concatenate(parts, axis=0), TN).astype(bf16)


def body(tokens, expert_ids, gate_prob, cotangent, w_gate, w_up, w_down, touched):
    rows = tokens.shape[0]
    at = jnp.stack([lax.axis_index("x"), lax.axis_index("z"), lax.axis_index("y")]).astype(jnp.int32)
    wg, wu, wd = w_gate[0], w_up[0], w_down[0]
    own, one, two, three, placer, gate = call(
        place_kernel,
        (shaped(CAP, 2 * D),) * 4 + (shaped(rows, rows), shaped(rows, rows, dtype=f32)),
        (at, expert_ids.T, gate_prob[None, :], tokens, cotangent),
        2 * 2 * rows * rows * D, 2 * 4 * rows * D, "shhhh", limit=VMEM_WHOLE,
    )
    near = [own, lax.ppermute(one, "y", PERM1), lax.ppermute(two, "y", PERM2), lax.ppermute(three, "y", PERM3)]
    far = [lax.ppermute(part, "y", PAIR) for part in near]
    mine = join(near)
    mates = lax.ppermute(mine, "c", SWAP)
    pair_mine = join(far)
    pair_mates = lax.ppermute(pair_mine, "c", SWAP)
    ga, p_mine, p_mates = layer(touched, (mine, mates), wg, wu, wd, True)
    p_got = lax.ppermute(p_mates, "c", SWAP)
    gb, act_mine = layer(touched, (pair_mine,), wg, wu, wd, False)
    gc, act_mates = layer(touched, (pair_mates,), wg, wu, wd, False)
    deltas = delta((mine, mates, pair_mine, pair_mates), (ga, gb, gc))
    over_x = lax.all_to_all(deltas, "x", split_axis=0, concat_axis=0, tiled=True)
    q_mine, q_mates = call(
        out_kernel, (shaped(4 * CAP, D),) * 2, (act_mine, act_mates, wd), 0, 0, "vvv", "hh"
    )
    q_got = lax.ppermute(q_mates, "c", SWAP)
    q_sum = call(add_kernel, shaped(4 * CAP, D), (q_mine, q_got), 0, 0, "vv", "h")
    from_pair = lax.ppermute(q_sum, "y", PAIR)
    blocks = call(
        add_split_kernel, (shaped(CAP, D),) * 4, (p_mine, p_got, from_pair), 0, 0,
        "hhh", "hhhh", limit=VMEM_WHOLE,
    )
    back = [blocks[0]] + [
        lax.ppermute(block, "y", back_perm(perm)) for block, perm in zip(blocks[1:], (PERM1, PERM2, PERM3))
    ]
    over_x, back[1:3] = lax.optimization_barrier((over_x, back[1:3]))
    got = lax.all_to_all(fold(over_x, 8, 1.0), "z", split_axis=0, concat_axis=0, tiled=True)
    got, back = lax.optimization_barrier((got, back))
    averaged = fold(got, 3, 1.0 / (X * Z)).T
    mixed = call(mixed_kernel, shaped(rows, D), (*back, gate, placer), 2 * rows * rows * D, 2 * 2 * rows * D)
    return mixed, averaged


def solution(mesh):
    fine = Mesh(mesh.devices.reshape(X, Z, Y, C), AXES)
    rep, exp = ("x", "z"), ("y", "c")
    return jax.shard_map(
        body,
        mesh=fine,
        in_specs=(
            P(AXES, None),
            P(AXES, None),
            P(AXES),
            P(AXES, None),
            P(rep, None, exp),
            P(rep, None, exp),
            P(rep, exp, None),
            P(rep, exp),
        ),
        out_specs=(P(AXES, None), P(exp, rep)),
        check_vma=False,
    )
```

time: 171 us -> 146 us (0.85); the launches traced: 168 us -> 146 us
  starting transfers between devices: 107 us -> 69.4 us
  waiting for transfers between devices: 38.1 us -> 49.9 us
  Pallas kernels: 13.9 us -> 21.9 us
  local copies, waits for them, and re-layouts: 8.18 us -> 2.66 us
    ppermute x10 -> x0, starting transfers between devices: 36.9 us -> none  [the longest x7 28.5 us: body(): lax.ppermute(second[j], 'z', [(i, (i + j) % Z) for i in range(Z)])]
    ppermute x1, waiting for transfers between devices: 0.01 us -> 13.6 us  [body(): from_pair = lax.ppermute(q_sum, 'y', PAIR)]
    pallas_call x12 -> x13, Pallas kernels: 13.9 us -> 21.9 us  [the longest x11 17.4 us: call(): pl.pallas_call(run, out_shape=outs, in_specs=[kind[m] for m in space], ou...]
    ppermute x3, waiting for transfers between devices: 0.01 us -> 7.49 us  [body(): lax.ppermute(block, 'y', back_perm(perm))]
    all_to_all x2, waiting for transfers between devices: 24.5 us -> 17.9 us  [the longest x1 13.4 us: body(): lax.all_to_all(fold(over_x, 8, 1.0), 'z', split_axis=0, concat_axis=0, ti...]
    unnamed x32 -> x28, local copies, waits for them, and re-layouts: 8.18 us -> 2.66 us
    ppermute x10 -> x0, waiting for transfers between devices: 2.19 us -> none  [the longest x3 1.24 us: body(): lax.ppermute(sums[j], 'x', [(i, (i + j) % X) for i in range(X)])]
    ppermute x1, starting transfers between devices: 3.76 us -> 1.94 us  [body(): from_pair = lax.ppermute(q_sum, 'y', PAIR)]
  transfers between devices with their start and end apart: 27 -> 17, of which waited for: 5 -> 8; matrix products, arithmetic and copies ran while one was open for 0% -> 0% of each run, Pallas kernels for 4% -> 5%
where the time goes in v3:
time: 146 us
  starting transfers between devices  69.4 us (48%)
  waiting for transfers between devices  49.9 us (34%)
  Pallas kernels  21.9 us (15%)
  local copies, waits for them, and re-layouts  2.66 us (2%)
    pallas_call x11, Pallas kernels, call(): pl.pallas_call(run, out_shape=outs, in_specs=[kind[m] for m in space], ou...  17.4 us
    ppermute x1, waiting for transfers between devices, body(): from_pair = lax.ppermute(q_sum, 'y', PAIR)  13.6 us
    all_to_all x1, waiting for transfers between devices, body(): lax.all_to_all(fold(over_x, 8, 1.0), 'z', split_axis=0, concat_axis=0, ti...  13.4 us
    ppermute x3, starting transfers between devices, body(): lax.ppermute(block, 'y', back_perm(perm))  12.1 us
    ppermute x4, starting transfers between devices, body(): far = [lax.ppermute(part, 'y', PAIR) for part in near]  11.2 us
    all_to_all x1, starting transfers between devices, body(): lax.all_to_all(fold(over_x, 8, 1.0), 'z', split_axis=0, concat_axis=0, ti...  8.39 us
    ppermute x3, waiting for transfers between devices, body(): lax.ppermute(block, 'y', back_perm(perm))  7.49 us
    ppermute x1, waiting for transfers between devices, body(): lax.ppermute(three, 'y', PERM3)  7.32 us
  transfers between devices with their start and end apart: 17, of which 8 were waited for; matrix products, arithmetic and copies ran while one was open for 0% of the time, Pallas kernels for 5%

profile of v3, /device:TPU:1, one launch (start us, length us, event | category | flops | bytes accessed | tf_op | source)
XLA Modules:
  0.0 145.6 jit_solution(15441110493553609504)
XLA Ops:
  1.3 3.3 %shard_map.95 = (bf16[32,4096]{1,0:T(8,128)(2,1)}, bf16[32,4096]{1,0:T(8,128)(2,1)}, bf16[32,4096]{1,0:T(8,128)(2,1)}, bf16[32,4096]{1,0:T(8,128)(2,1)}, bf16[128,128]{1,0:T(8,128)(2,1)}, /*index=5*/f32[128,128]{1,0:T(8,128)}) custom-call(s32[3]{0:T(128)} %pad_add_fusion.refs_0_, s32[1,128]{1,0:T(1,128)} %bitcast.27, f32[1,128]{1,0:T(1,128)} %bitcast.28, ...), custom_call_target="tpu_custom_call" | custom-call | flops 134217728 | bytes 2097152 | tf_op jit(solution)/shard_map/pallas_call | solution.py:104
  4.6 6.1 %collective-permute-start = (bf16[32,4096]{1,0:T(8,128)(2,1)}, bf16[32,4096]{1,0:T(8,128)(2,1)S(1)}, u32[]{:S(2)}, u32[]{:S(2)}) collective-permute-start(bf16[32,4096]{1,0:T(8,128)(2,1)} %get-tuple-element.30), channel_id=1, source_target_pairs={{0,14},{2,4},{4,2},{6,8},{8,6},{10,12},{12,10},{14,0},{1,15},{3,5}... | collective-permute-start | bytes 786440 | tf_op jit(solution)/shard_map/ppermute | solution.py:316
  10.7 1.9 %collective-permute-start.1 = (bf16[32,4096]{1,0:T(8,128)(2,1)}, bf16[32,4096]{1,0:T(8,128)(2,1)S(1)}, u32[]{:S(2)}, u32[]{:S(2)}) collective-permute-start(bf16[32,4096]{1,0:T(8,128)(2,1)} %get-tuple-element.31), channel_id=1, source_target_pairs={{0,4},{2,14},{4,8},{6,2},{8,12},{10,6},{12,0},{14,10},{1,5},{3,15}... | collective-permute-start | bytes 786440 | tf_op jit(solution)/shard_map/ppermute | solution.py:316
  12.6 6.9 %collective-permute-start.2 = (bf16[32,4096]{1,0:T(8,128)(2,1)}, bf16[32,4096]{1,0:T(8,128)(2,1)S(1)}, u32[]{:S(2)}, u32[]{:S(2)}) collective-permute-start(bf16[32,4096]{1,0:T(8,128)(2,1)} %get-tuple-element.32), channel_id=1, source_target_pairs={{0,10},{2,8},{4,14},{6,12},{8,2},{10,0},{12,6},{14,4},{1,11},{3,9}... | collective-permute-start | bytes 786440 | tf_op jit(solution)/shard_map/ppermute | solution.py:316
  19.6 1.9 %collective-permute-start.4 = (bf16[32,4096]{1,0:T(8,128)(2,1)}, bf16[32,4096]{1,0:T(8,128)(2,1)S(1)}, u32[]{:S(2)}, u32[]{:S(2)}) collective-permute-start(bf16[32,4096]{1,0:T(8,128)(2,1)} %get-tuple-element.29.refs_0_), channel_id=1, source_target_pairs={{0,2},{2,0},{4,6},{6,4},{8,10},{10,8},{12,14},{14,12},{1,3},{3,1},... | collective-permute-start | bytes 786440 | tf_op jit(solution)/shard_map/ppermute | solution.py:317
  21.5 3.4 %collective-permute-start.5 = (bf16[32,4096]{1,0:T(8,128)(2,1)S(1)}, bf16[32,4096]{1,0:T(8,128)(2,1)S(1)}, u32[]{:S(2)}, u32[]{:S(2)}) collective-permute-start(bf16[32,4096]{1,0:T(8,128)(2,1)S(1)} %collective-permute-done.refs_1_), channel_id=1, source_target_pairs={{0,2},{2,0},{4,6},{6,4},{8,10},{10,8},{12,14},{14,12},{1,3},{3,1},... | collective-permute-start | bytes 786440 | tf_op jit(solution)/shard_map/ppermute | solution.py:317
  24.9 1.9 %collective-permute-start.6 = (bf16[32,4096]{1,0:T(8,128)(2,1)S(1)}, bf16[32,4096]{1,0:T(8,128)(2,1)S(1)}, u32[]{:S(2)}, u32[]{:S(2)}) collective-permute-start(bf16[32,4096]{1,0:T(8,128)(2,1)S(1)} %collective-permute-done.1.refs_2_), channel_id=1, source_target_pairs={{0,2},{2,0},{4,6},{6,4},{8,10},{10,8},{12,14},{14,12},{1,3},{3,1},... | collective-permute-start | bytes 786440 | tf_op jit(solution)/shard_map/ppermute | solution.py:317
  26.8 7.3 %collective-permute-done.2.refs_3_ = bf16[32,4096]{1,0:T(8,128)(2,1)S(1)} collective-permute-done((bf16[32,4096]{1,0:T(8,128)(2,1)}, bf16[32,4096]{1,0:T(8,128)(2,1)S(1)}, u32[]{:S(2)}, u32[]{:S(2)}) %collective-permute-start.2) | collective-permute-done | bytes 262176 | tf_op jit(solution)/shard_map/ppermute | solution.py:316
  34.1 4.0 %collective-permute-start.7 = (bf16[32,4096]{1,0:T(8,128)(2,1)S(1)}, bf16[32,4096]{1,0:T(8,128)(2,1)S(1)}, u32[]{:S(2)}, u32[]{:S(2)}) collective-permute-start(bf16[32,4096]{1,0:T(8,128)(2,1)S(1)} %collective-permute-done.2.refs_3_), channel_id=1, source_target_pairs={{0,2},{2,0},{4,6},{6,4},{8,10},{10,8},{12,14},{14,12},{1,3},{3,1},... | collective-permute-start | bytes 786440 | tf_op jit(solution)/shard_map/ppermute | solution.py:317
  39.2 5.8 %collective-permute-start.3 = (bf16[128,4096]{1,0:T(8,128)(2,1)S(1)}, bf16[128,4096]{1,0:T(8,128)(2,1)S(1)}, u32[]{:S(2)}, u32[]{:S(2)}) collective-permute-start(bf16[128,4096]{1,0:T(8,128)(2,1)S(1)} %shard_map.96.refs_1_.refs_0_), channel_id=1, source_target_pairs={{0,1},{1,0},{2,3},{3,2},{4,5},{5,4},{6,7},{7,6},{8,9},{9,8},{10,11... | collective-permute-start | bytes 3145736 | tf_op jit(solution)/shard_map/ppermute | solution.py:319
  45.1 3.6 %collective-permute-done.7.refs_3_ = bf16[32,4096]{1,0:T(8,128)(2,1)S(1)} collective-permute-done((bf16[32,4096]{1,0:T(8,128)(2,1)S(1)}, bf16[32,4096]{1,0:T(8,128)(2,1)S(1)}, u32[]{:S(2)}, u32[]{:S(2)}) %collective-permute-start.7) | collective-permute-done | bytes 262176 | tf_op jit(solution)/shard_map/ppermute | solution.py:317
  48.7 6.1 %collective-permute-start.8 = (bf16[128,4096]{1,0:T(8,128)(2,1)S(1)}, bf16[128,4096]{1,0:T(8,128)(2,1)S(1)}, u32[]{:S(2)}, u32[]{:S(2)}) collective-permute-start(bf16[128,4096]{1,0:T(8,128)(2,1)S(1)} %shard_map.97.refs_1_.refs_2_), channel_id=1, source_target_pairs={{0,1},{1,0},{2,3},{3,2},{4,5},{5,4},{6,7},{7,6},{8,9},{9,8},{10,11... | collective-permute-start | bytes 3145736 | tf_op jit(solution)/shard_map/ppermute | solution.py:321
  54.9 1.3 shard_map.99
  56.2 2.8 %shard_map.98 = (bf16[256,768]{1,0:T(8,128)(2,1)S(1)}, bf16[128,2048]{1,0:T(8,128)(2,1)S(1)}, bf16[128,2048]{1,0:T(8,128)(2,1)S(1)}) custom-call(s32[1,16]{1,0:T(1,128)S(1)} %copy-done.9, bf16[128,4096]{1,0:T(8,128)(2,1)S(1)} %shard_map.96.refs_1_.refs_0_, bf16[128,4096]{1,0:T(8,128)(2,1)S(1)} %collective-permute-done.3.refs_2_.refs_1_, ...), custom_call_target="tpu_custom_call" | custom-call | flops 1073741824 | bytes 6291456 | tf_op jit(solution)/shard_map/pallas_call | solution.py:104
  59.1 1.3 shard_map.100
  60.5 4.1 %shard_map.101 = bf16[4,8,192,256]{3,2,1,0:T(8,128)(2,1)} custom-call(bf16[128,4096]{1,0:T(8,128)(2,1)S(1)} %shard_map.96.refs_1_.refs_0_, bf16[128,4096]{1,0:T(8,128)(2,1)S(1)} %collective-permute-done.3.refs_2_.refs_1_, bf16[128,4096]{1,0:T(8,128)(2,1)S(1)} %shard_map.97.refs_1_.refs_2_, bf16[128,4096]{1,0:T(8,128)(2,1)} %copy-done.3, ...), custom_call_target="tpu_custom_call" | custom-call | flops 1610612736 | bytes 7340032 | tf_op jit(solution)/shard_map/pallas_call | solution.py:104
  64.6 4.7 %all-to-all-start = ((bf16[4,8,192,256]{3,2,1,0:T(8,128)(2,1)}), bf16[4,8,192,256]{3,2,1,0:T(8,128)(2,1)}, u32[]{:S(2)}, u32[]{:S(2)}) async-start(bf16[4,8,192,256]{3,2,1,0:T(8,128)(2,1)} %shard_map.101), calls=%async_computation | async-start | bytes 6291456 | tf_op jit(solution)/shard_map/all_to_all | solution.py:327
  70.0 1.9 %collective-permute-start.10 = (bf16[128,2048]{1,0:T(8,128)(2,1)S(1)}, bf16[128,2048]{1,0:T(8,128)(2,1)S(1)}, u32[]{:S(2)}, u32[]{:S(2)}) collective-permute-start(bf16[128,2048]{1,0:T(8,128)(2,1)S(1)} %get-tuple-element.41), channel_id=1, source_target_pairs={{0,1},{1,0},{2,3},{3,2},{4,5},{5,4},{6,7},{7,6},{8,9},{9,8},{10,11... | collective-permute-start | bytes 1572872 | tf_op jit(solution)/shard_map/ppermute | solution.py:331
  71.9 2.4 %collective-permute-start.9 = (bf16[128,2048]{1,0:T(8,128)(2,1)S(1)}, bf16[128,2048]{1,0:T(8,128)(2,1)S(1)}, u32[]{:S(2)}, u32[]{:S(2)}) collective-permute-start(bf16[128,2048]{1,0:T(8,128)(2,1)S(1)} %get-tuple-element.37), channel_id=1, source_target_pairs={{0,1},{1,0},{2,3},{3,2},{4,5},{5,4},{6,7},{7,6},{8,9},{9,8},{10,11... | collective-permute-start | bytes 1572872 | tf_op jit(solution)/shard_map/ppermute | solution.py:323
  74.5 1.9 %collective-permute-start.11 = (bf16[128,2048]{1,0:T(8,128)(2,1)S(1)}, bf16[128,2048]{1,0:T(8,128)(2,1)S(1)}, u32[]{:S(2)}, u32[]{:S(2)}) collective-permute-start(bf16[128,2048]{1,0:T(8,128)(2,1)S(1)} %shard_map.103), channel_id=1, source_target_pairs={{0,2},{2,0},{4,6},{6,4},{8,10},{10,8},{12,14},{14,12},{1,3},{3,1},... | collective-permute-start | bytes 1572872 | tf_op jit(solution)/shard_map/ppermute | solution.py:333
  76.5 13.6 %collective-permute-done.11.refs_2_ = bf16[128,2048]{1,0:T(8,128)(2,1)S(1)} collective-permute-done((bf16[128,2048]{1,0:T(8,128)(2,1)S(1)}, bf16[128,2048]{1,0:T(8,128)(2,1)S(1)}, u32[]{:S(2)}, u32[]{:S(2)}) %collective-permute-start.11) | collective-permute-done | bytes 524320 | tf_op jit(solution)/shard_map/ppermute | solution.py:333
  90.8 2.3 %shard_map.104 = (bf16[32,2048]{1,0:T(8,128)(2,1)}, bf16[32,2048]{1,0:T(8,128)(2,1)}, bf16[32,2048]{1,0:T(8,128)(2,1)}, bf16[32,2048]{1,0:T(8,128)(2,1)}) custom-call(bf16[128,2048]{1,0:T(8,128)(2,1)} %copy-done.4, bf16[128,2048]{1,0:T(8,128)(2,1)} %copy-done.11, bf16[128,2048]{1,0:T(8,128)(2,1)} %copy-done.12), custom_call_target="tpu_custom_call" | custom-call | tf_op jit(solution)/shard_map/pallas_call | solution.py:104
  93.2 2.2 %collective-permute-start.12 = (bf16[32,2048]{1,0:T(8,128)(2,1)}, bf16[32,2048]{1,0:T(8,128)(2,1)S(1)}, u32[]{:S(2)}, u32[]{:S(2)}) collective-permute-start(bf16[32,2048]{1,0:T(8,128)(2,1)} %get-tuple-element.42), channel_id=1, source_target_pairs={{14,0},{4,2},{2,4},{8,6},{6,8},{12,10},{10,12},{0,14},{15,1},{5,3}... | collective-permute-start | bytes 393224 | tf_op jit(solution)/shard_map/ppermute | solution.py:339
  95.4 4.9 %collective-permute-start.13 = (bf16[32,2048]{1,0:T(8,128)(2,1)}, bf16[32,2048]{1,0:T(8,128)(2,1)S(1)}, u32[]{:S(2)}, u32[]{:S(2)}) collective-permute-start(bf16[32,2048]{1,0:T(8,128)(2,1)} %get-tuple-element.43), channel_id=1, source_target_pairs={{4,0},{14,2},{8,4},{2,6},{12,8},{6,10},{0,12},{10,14},{5,1},{15,3}... | collective-permute-start | bytes 393224 | tf_op jit(solution)/shard_map/ppermute | solution.py:339
  101.1 1.5 %collective-permute-done.13.refs_2_ = bf16[32,2048]{1,0:T(8,128)(2,1)S(1)} collective-permute-done((bf16[32,2048]{1,0:T(8,128)(2,1)}, bf16[32,2048]{1,0:T(8,128)(2,1)S(1)}, u32[]{:S(2)}, u32[]{:S(2)}) %collective-permute-start.13) | collective-permute-done | bytes 131104 | tf_op jit(solution)/shard_map/ppermute | solution.py:339
  102.6 4.5 %all-to-all-done = bf16[4,8,192,256]{3,2,1,0:T(8,128)(2,1)} async-done(((bf16[4,8,192,256]{3,2,1,0:T(8,128)(2,1)}), bf16[4,8,192,256]{3,2,1,0:T(8,128)(2,1)}, u32[]{:S(2)}, u32[]{:S(2)}) %all-to-all-start) | async-done | bytes 3145760 | tf_op jit(solution)/shard_map/all_to_all | solution.py:327
  107.0 2.7 %shard_map.105 = bf16[24,64,256]{2,1,0:T(8,128)(2,1)} custom-call(bf16[4,24,64,256]{3,2,1,0:T(8,128)(2,1)} %bitcast.8.got), custom_call_target="tpu_custom_call" | custom-call | bytes 3145728 | tf_op jit(solution)/shard_map/pallas_call | solution.py:269
  109.7 8.4 %all-to-all-start.1 = ((bf16[8,192,256]{2,1,0:T(8,128)(2,1)}), bf16[8,192,256]{2,1,0:T(8,128)(2,1)S(1)}, u32[]{:S(2)}, u32[]{:S(2)}) async-start(bf16[8,192,256]{2,1,0:T(8,128)(2,1)} %bitcast.25), calls=%async_computation.1 | async-start | bytes 1572864 | tf_op jit(solution)/shard_map/all_to_all | solution.py:342
  118.1 4.9 %collective-permute-start.14 = (bf16[32,2048]{1,0:T(8,128)(2,1)S(1)}, bf16[32,2048]{1,0:T(8,128)(2,1)S(1)}, u32[]{:S(2)}, u32[]{:S(2)}) collective-permute-start(bf16[32,2048]{1,0:T(8,128)(2,1)S(1)} %copy-done.13), channel_id=1, source_target_pairs={{10,0},{8,2},{14,4},{12,6},{2,8},{0,10},{6,12},{4,14},{11,1},{9,3}... | collective-permute-start | bytes 393224 | tf_op jit(solution)/shard_map/ppermute | solution.py:339
  123.1 5.2 %collective-permute-done.14.refs_3_ = bf16[32,2048]{1,0:T(8,128)(2,1)S(1)} collective-permute-done((bf16[32,2048]{1,0:T(8,128)(2,1)S(1)}, bf16[32,2048]{1,0:T(8,128)(2,1)S(1)}, u32[]{:S(2)}, u32[]{:S(2)}) %collective-permute-start.14) | collective-permute-done | bytes 131104 | tf_op jit(solution)/shard_map/ppermute | solution.py:339
  128.3 13.4 %all-to-all-done.1 = bf16[8,192,256]{2,1,0:T(8,128)(2,1)S(1)} async-done(((bf16[8,192,256]{2,1,0:T(8,128)(2,1)}), bf16[8,192,256]{2,1,0:T(8,128)(2,1)S(1)}, u32[]{:S(2)}, u32[]{:S(2)}) %all-to-all-start.1) | async-done | bytes 786464 | tf_op jit(solution)/shard_map/all_to_all | solution.py:342
  142.6 1.8 %shard_map.107 = bf16[3,64,256]{2,1,0:T(8,128)(2,1)} custom-call(bf16[8,3,64,256]{3,2,1,0:T(8,128)(2,1)} %bitcast.24), custom_call_target="tpu_custom_call" | custom-call | bytes 786432 | tf_op jit(solution)/shard_map/pallas_call | solution.py:269
  (44 shorter events, 6.3 us)
Async XLA Ops:
  0.6 54.2 %copy-start = (bf16[1,256,2048]{2,1,0:T(8,128)(2,1)S(1)}, bf16[1,256,2048]{2,1,0:T(8,128)(2,1)}, u32[]{:S(2)}) copy-start(bf16[1,256,2048]{2,1,0:T(8,128)(2,1)} %param.14) | copy-start | bytes 3145732
  0.6 54.2 %copy-start.9 = (s32[1,16]{1,0:T(1,128)S(1)}, s32[1,16]{1,0:T(1,128)}, u32[]{:S(2)}) copy-start(s32[1,16]{1,0:T(1,128)} %refs_0_.5) | copy-start | bytes 196
  4.6 50.2 %copy-start.1 = (bf16[1,2048,256]{2,1,0:T(8,128)(2,1)S(1)}, bf16[1,2048,256]{2,1,0:T(8,128)(2,1)}, u32[]{:S(2)}) copy-start(bf16[1,2048,256]{2,1,0:T(8,128)(2,1)} %param.12) | copy-start | bytes 3145732
  4.6 50.2 %copy-start.2 = (bf16[1,2048,256]{2,1,0:T(8,128)(2,1)S(1)}, bf16[1,2048,256]{2,1,0:T(8,128)(2,1)}, u32[]{:S(2)}) copy-start(bf16[1,2048,256]{2,1,0:T(8,128)(2,1)} %param.13) | copy-start | bytes 3145732
  4.6 16.9 %collective-permute-start = (bf16[32,4096]{1,0:T(8,128)(2,1)}, bf16[32,4096]{1,0:T(8,128)(2,1)S(1)}, u32[]{:S(2)}, u32[]{:S(2)}) collective-permute-start(bf16[32,4096]{1,0:T(8,128)(2,1)} %get-tuple-element.30), channel_id=1, source_target_pairs={{0,14},{2,4},{4,2},{6,8},{8,6},{10,12},{12,10},{14,0},{1,15},{3,5}... | collective-permute-start | bytes 786440 | tf_op jit(solution)/shard_map/ppermute | solution.py:316
  10.7 14.2 %collective-permute-start.1 = (bf16[32,4096]{1,0:T(8,128)(2,1)}, bf16[32,4096]{1,0:T(8,128)(2,1)S(1)}, u32[]{:S(2)}, u32[]{:S(2)}) collective-permute-start(bf16[32,4096]{1,0:T(8,128)(2,1)} %get-tuple-element.31), channel_id=1, source_target_pairs={{0,4},{2,14},{4,8},{6,2},{8,12},{10,6},{12,0},{14,10},{1,5},{3,15}... | collective-permute-start | bytes 786440 | tf_op jit(solution)/shard_map/ppermute | solution.py:316
  12.6 21.5 %collective-permute-start.2 = (bf16[32,4096]{1,0:T(8,128)(2,1)}, bf16[32,4096]{1,0:T(8,128)(2,1)S(1)}, u32[]{:S(2)}, u32[]{:S(2)}) collective-permute-start(bf16[32,4096]{1,0:T(8,128)(2,1)} %get-tuple-element.32), channel_id=1, source_target_pairs={{0,10},{2,8},{4,14},{6,12},{8,2},{10,0},{12,6},{14,4},{1,11},{3,9}... | collective-permute-start | bytes 786440 | tf_op jit(solution)/shard_map/ppermute | solution.py:316
  19.6 25.5 %collective-permute-start.4 = (bf16[32,4096]{1,0:T(8,128)(2,1)}, bf16[32,4096]{1,0:T(8,128)(2,1)S(1)}, u32[]{:S(2)}, u32[]{:S(2)}) collective-permute-start(bf16[32,4096]{1,0:T(8,128)(2,1)} %get-tuple-element.29.refs_0_), channel_id=1, source_target_pairs={{0,2},{2,0},{4,6},{6,4},{8,10},{10,8},{12,14},{14,12},{1,3},{3,1},... | collective-permute-start | bytes 786440 | tf_op jit(solution)/shard_map/ppermute | solution.py:317
  21.5 23.5 %collective-permute-start.5 = (bf16[32,4096]{1,0:T(8,128)(2,1)S(1)}, bf16[32,4096]{1,0:T(8,128)(2,1)S(1)}, u32[]{:S(2)}, u32[]{:S(2)}) collective-permute-start(bf16[32,4096]{1,0:T(8,128)(2,1)S(1)} %collective-permute-done.refs_1_), channel_id=1, source_target_pairs={{0,2},{2,0},{4,6},{6,4},{8,10},{10,8},{12,14},{14,12},{1,3},{3,1},... | collective-permute-start | bytes 786440 | tf_op jit(solution)/shard_map/ppermute | solution.py:317
  24.9 20.2 %collective-permute-start.6 = (bf16[32,4096]{1,0:T(8,128)(2,1)S(1)}, bf16[32,4096]{1,0:T(8,128)(2,1)S(1)}, u32[]{:S(2)}, u32[]{:S(2)}) collective-permute-start(bf16[32,4096]{1,0:T(8,128)(2,1)S(1)} %collective-permute-done.1.refs_2_), channel_id=1, source_target_pairs={{0,2},{2,0},{4,6},{6,4},{8,10},{10,8},{12,14},{14,12},{1,3},{3,1},... | collective-permute-start | bytes 786440 | tf_op jit(solution)/shard_map/ppermute | solution.py:317
  34.1 14.5 %collective-permute-start.7 = (bf16[32,4096]{1,0:T(8,128)(2,1)S(1)}, bf16[32,4096]{1,0:T(8,128)(2,1)S(1)}, u32[]{:S(2)}, u32[]{:S(2)}) collective-permute-start(bf16[32,4096]{1,0:T(8,128)(2,1)S(1)} %collective-permute-done.2.refs_3_), channel_id=1, source_target_pairs={{0,2},{2,0},{4,6},{6,4},{8,10},{10,8},{12,14},{14,12},{1,3},{3,1},... | collective-permute-start | bytes 786440 | tf_op jit(solution)/shard_map/ppermute | solution.py:317
  38.1 1.0 copy-start.5
  39.2 17.1 %collective-permute-start.3 = (bf16[128,4096]{1,0:T(8,128)(2,1)S(1)}, bf16[128,4096]{1,0:T(8,128)(2,1)S(1)}, u32[]{:S(2)}, u32[]{:S(2)}) collective-permute-start(bf16[128,4096]{1,0:T(8,128)(2,1)S(1)} %shard_map.96.refs_1_.refs_0_), channel_id=1, source_target_pairs={{0,1},{1,0},{2,3},{3,2},{4,5},{5,4},{6,7},{7,6},{8,9},{9,8},{10,11... | collective-permute-start | bytes 3145736 | tf_op jit(solution)/shard_map/ppermute | solution.py:319
  48.7 10.3 %collective-permute-start.8 = (bf16[128,4096]{1,0:T(8,128)(2,1)S(1)}, bf16[128,4096]{1,0:T(8,128)(2,1)S(1)}, u32[]{:S(2)}, u32[]{:S(2)}) collective-permute-start(bf16[128,4096]{1,0:T(8,128)(2,1)S(1)} %shard_map.97.refs_1_.refs_2_), channel_id=1, source_target_pairs={{0,1},{1,0},{2,3},{3,2},{4,5},{5,4},{6,7},{7,6},{8,9},{9,8},{10,11... | collective-permute-start | bytes 3145736 | tf_op jit(solution)/shard_map/ppermute | solution.py:321
  59.1 1.4 copy-start.4
  59.1 1.4 copy-start.3
  64.6 42.5 %all-to-all-start = ((bf16[4,8,192,256]{3,2,1,0:T(8,128)(2,1)}), bf16[4,8,192,256]{3,2,1,0:T(8,128)(2,1)}, u32[]{:S(2)}, u32[]{:S(2)}) async-start(bf16[4,8,192,256]{3,2,1,0:T(8,128)(2,1)} %shard_map.101), calls=%async_computation | async-start | bytes 6291456 | tf_op jit(solution)/shard_map/all_to_all | solution.py:327
  70.0 4.3 %collective-permute-start.10 = (bf16[128,2048]{1,0:T(8,128)(2,1)S(1)}, bf16[128,2048]{1,0:T(8,128)(2,1)S(1)}, u32[]{:S(2)}, u32[]{:S(2)}) collective-permute-start(bf16[128,2048]{1,0:T(8,128)(2,1)S(1)} %get-tuple-element.41), channel_id=1, source_target_pairs={{0,1},{1,0},{2,3},{3,2},{4,5},{5,4},{6,7},{7,6},{8,9},{9,8},{10,11... | collective-permute-start | bytes 1572872 | tf_op jit(solution)/shard_map/ppermute | solution.py:331
  71.9 4.6 %collective-permute-start.9 = (bf16[128,2048]{1,0:T(8,128)(2,1)S(1)}, bf16[128,2048]{1,0:T(8,128)(2,1)S(1)}, u32[]{:S(2)}, u32[]{:S(2)}) collective-permute-start(bf16[128,2048]{1,0:T(8,128)(2,1)S(1)} %get-tuple-element.37), channel_id=1, source_target_pairs={{0,1},{1,0},{2,3},{3,2},{4,5},{5,4},{6,7},{7,6},{8,9},{9,8},{10,11... | collective-permute-start | bytes 1572872 | tf_op jit(solution)/shard_map/ppermute | solution.py:323
  74.5 15.5 %collective-permute-start.11 = (bf16[128,2048]{1,0:T(8,128)(2,1)S(1)}, bf16[128,2048]{1,0:T(8,128)(2,1)S(1)}, u32[]{:S(2)}, u32[]{:S(2)}) collective-permute-start(bf16[128,2048]{1,0:T(8,128)(2,1)S(1)} %shard_map.103), channel_id=1, source_target_pairs={{0,2},{2,0},{4,6},{6,4},{8,10},{10,8},{12,14},{14,12},{1,3},{3,1},... | collective-permute-start | bytes 1572872 | tf_op jit(solution)/shard_map/ppermute | solution.py:333
  76.5 13.6 %copy-start.11 = (bf16[128,2048]{1,0:T(8,128)(2,1)}, bf16[128,2048]{1,0:T(8,128)(2,1)S(1)}, u32[]{:S(2)}) copy-start(bf16[128,2048]{1,0:T(8,128)(2,1)S(1)} %collective-permute-done.9.refs_1_) | copy-start | bytes 1572868
  90.1 0.8 copy-start.12
  93.2 25.0 %copy-start.13 = (bf16[32,2048]{1,0:T(8,128)(2,1)S(1)}, bf16[32,2048]{1,0:T(8,128)(2,1)}, u32[]{:S(2)}) copy-start(bf16[32,2048]{1,0:T(8,128)(2,1)} %get-tuple-element.48) | copy-start | bytes 393220
  93.2 7.9 %collective-permute-start.12 = (bf16[32,2048]{1,0:T(8,128)(2,1)}, bf16[32,2048]{1,0:T(8,128)(2,1)S(1)}, u32[]{:S(2)}, u32[]{:S(2)}) collective-permute-start(bf16[32,2048]{1,0:T(8,128)(2,1)} %get-tuple-element.42), channel_id=1, source_target_pairs={{14,0},{4,2},{2,4},{8,6},{6,8},{12,10},{10,12},{0,14},{15,1},{5,3}... | collective-permute-start | bytes 393224 | tf_op jit(solution)/shard_map/ppermute | solution.py:339
  95.4 7.2 %collective-permute-start.13 = (bf16[32,2048]{1,0:T(8,128)(2,1)}, bf16[32,2048]{1,0:T(8,128)(2,1)S(1)}, u32[]{:S(2)}, u32[]{:S(2)}) collective-permute-start(bf16[32,2048]{1,0:T(8,128)(2,1)} %get-tuple-element.43), channel_id=1, source_target_pairs={{4,0},{14,2},{8,4},{2,6},{12,8},{6,10},{0,12},{10,14},{5,1},{15,3}... | collective-permute-start | bytes 393224 | tf_op jit(solution)/shard_map/ppermute | solution.py:339
  107.0 37.4 %copy-start.6 = (bf16[32,2048]{1,0:T(8,128)(2,1)S(1)}, bf16[32,2048]{1,0:T(8,128)(2,1)}, u32[]{:S(2)}) copy-start(bf16[32,2048]{1,0:T(8,128)(2,1)} %get-tuple-element.49.refs_0_) | copy-start | bytes 393220
  107.0 37.4 %copy-start.7 = (f32[128,128]{1,0:T(8,128)S(1)}, f32[128,128]{1,0:T(8,128)}, u32[]{:S(2)}) copy-start(f32[128,128]{1,0:T(8,128)} %get-tuple-element.53.refs_4_) | copy-start | bytes 196612
  107.0 37.4 %copy-start.8 = (bf16[128,128]{1,0:T(8,128)(2,1)S(1)}, bf16[128,128]{1,0:T(8,128)(2,1)}, u32[]{:S(2)}) copy-start(bf16[128,128]{1,0:T(8,128)(2,1)} %get-tuple-element.54.refs_5_) | copy-start | bytes 98308
  109.7 32.0 %all-to-all-start.1 = ((bf16[8,192,256]{2,1,0:T(8,128)(2,1)}), bf16[8,192,256]{2,1,0:T(8,128)(2,1)S(1)}, u32[]{:S(2)}, u32[]{:S(2)}) async-start(bf16[8,192,256]{2,1,0:T(8,128)(2,1)} %bitcast.25), calls=%async_computation.1 | async-start | bytes 1572864 | tf_op jit(solution)/shard_map/all_to_all | solution.py:342
  118.1 10.2 %collective-permute-start.14 = (bf16[32,2048]{1,0:T(8,128)(2,1)S(1)}, bf16[32,2048]{1,0:T(8,128)(2,1)S(1)}, u32[]{:S(2)}, u32[]{:S(2)}) collective-permute-start(bf16[32,2048]{1,0:T(8,128)(2,1)S(1)} %copy-done.13), channel_id=1, source_target_pairs={{10,0},{8,2},{14,4},{12,6},{2,8},{0,10},{6,12},{4,14},{11,1},{9,3}... | collective-permute-start | bytes 393224 | tf_op jit(solution)/shard_map/ppermute | solution.py:339
  141.7 0.9 copy-start.10

commit v4 on v3

--- a/solution.py
+++ b/solution.py
@@ -242,21 +242,17 @@
 ROWS = 64
 
 
-def fold_kernel(n, chunks, scale, got, out, held, total, in_sems, out_sems):
+def fold_kernel(n, chunks, scale, got, out, total, sems):
     per = got.shape[1] // chunks
-    loads, stores = [], []
+    stores = []
     for c in range(chunks):
+        for i in range(c * per, (c + 1) * per):
+            value = got[0, i].astype(f32)
+            for k in range(1, n):
+                value += got[k, i].astype(f32)
+            total[i] = (value * scale).astype(bf16)
         here = pl.ds(c * per, per)
-        loads.append(pltpu.make_async_copy(got.at[:, here], held.at[:, here], in_sems.at[c]))
-        stores.append(pltpu.make_async_copy(total.at[here], out.at[here], out_sems.at[c]))
-        loads[c].start()
-    for c in range(chunks):
-        loads[c].wait()
-        for i in range(c * per, (c + 1) * per):
-            value = held[0, i].astype(f32)
-            for k in range(1, n):
-                value += held[k, i].astype(f32)
-            total[i] = (value * scale).astype(bf16)
+        stores.append(pltpu.make_async_copy(total.at[here], out.at[here], sems.at[c]))
         stores[c].start()
     for store in stores:
         store.wait()
@@ -269,15 +265,10 @@
     out = pl.pallas_call(
         functools.partial(fold_kernel, n, chunks, scale),
         out_shape=shaped(*got.shape[1:]),
-        in_specs=[HB],
+        in_specs=[VM],
         out_specs=HB,
-        scratch_shapes=[
-            pltpu.VMEM(got.shape, bf16),
-            pltpu.VMEM(got.shape[1:], bf16),
-            pltpu.SemaphoreType.DMA((chunks,)),
-            pltpu.SemaphoreType.DMA((chunks,)),
-        ],
-        compiler_params=pltpu.CompilerParams(vmem_limit_bytes=VMEM_WHOLE),
+        scratch_shapes=[pltpu.VMEM(got.shape[1:], bf16), pltpu.SemaphoreType.DMA((chunks,))],
+        compiler_params=pltpu.CompilerParams(vmem_limit_bytes=VMEM_WIDE),
         cost_estimate=pl.CostEstimate(flops=0, bytes_accessed=2 * got.size, transcendentals=0),
     )(got)
     return out.reshape(shape)
@@ -289,7 +280,6 @@
 
 
 def add_split_kernel(a, b, c, *outs):
-    a, b, c = a.get(), b.get(), c.get()
     for k in range(4):
         here = slice(k * CAP, (k + 1) * CAP)
         outs[k].ref[...] = (a[here].astype(f32) + b[here].astype(f32) + c[here].astype(f32)).astype(bf16)
@@ -321,9 +311,10 @@
     pair_mates = lax.ppermute(pair_mine, "c", SWAP)
     ga, p_mine, p_mates = layer(touched, (mine, mates), wg, wu, wd, True)
     p_got = lax.ppermute(p_mates, "c", SWAP)
-    gb, act_mine = layer(touched, (pair_mine,), wg, wu, wd, False)
-    gc, act_mates = layer(touched, (pair_mates,), wg, wu, wd, False)
-    deltas = delta((mine, mates, pair_mine, pair_mates), (ga, gb, gc))
+    gc, act_mine = layer(touched, (pair_mine,), wg, wu, wd, False)
+    gd, act_mates = layer(touched, (pair_mates,), wg, wu, wd, False)
+
+    deltas = delta((mine, mates, pair_mine, pair_mates), (ga, gc, gd))
     over_x = lax.all_to_all(deltas, "x", split_axis=0, concat_axis=0, tiled=True)
     q_mine, q_mates = call(
         out_kernel, (shaped(4 * CAP, D),) * 2, (act_mine, act_mates, wd), 0, 0, "vvv", "hh"
@@ -333,16 +324,16 @@
     from_pair = lax.ppermute(q_sum, "y", PAIR)
     blocks = call(
         add_split_kernel, (shaped(CAP, D),) * 4, (p_mine, p_got, from_pair), 0, 0,
-        "hhh", "hhhh", limit=VMEM_WHOLE,
+        "vvv", "hhhh", limit=VMEM_WIDE,
     )
     back = [blocks[0]] + [
         lax.ppermute(block, "y", back_perm(perm)) for block, perm in zip(blocks[1:], (PERM1, PERM2, PERM3))
     ]
     over_x, back[1:3] = lax.optimization_barrier((over_x, back[1:3]))
     got = lax.all_to_all(fold(over_x, 8, 1.0), "z", split_axis=0, concat_axis=0, tiled=True)
-    got, back = lax.optimization_barrier((got, back))
+    mixed = call(mixed_kernel, shaped(rows, D), (*back, gate, placer), 2 * rows * rows * D, 2 * 2 * rows * D)
+    got, mixed = lax.optimization_barrier((got, mixed))
     averaged = fold(got, 3, 1.0 / (X * Z)).T
-    mixed = call(mixed_kernel, shaped(rows, D), (*back, gate, placer), 2 * rows * rows * D, 2 * 2 * rows * D)
     return mixed, averaged
 
 

time: 146 us -> 144 us (0.986)
  Pallas kernels: 21.9 us -> 19.7 us
  local copies, waits for them, and re-layouts: 2.66 us -> 0.98 us
    all_to_all x1, waiting for transfers between devices: 4.45 us -> 6.84 us  [body(): lax.all_to_all(deltas, 'x', split_axis=0, concat_axis=0, tiled=True)]
    unnamed x28 -> x16, local copies, waits for them, and re-layouts: 2.66 us -> 0.98 us
where the time goes in v4:
time: 144 us; the launch traced here: 143 us
  starting transfers between devices  69.4 us (48%)
  waiting for transfers between devices  50.9 us (35%)
  Pallas kernels  19.7 us (14%)
    pallas_call x11, Pallas kernels, call(): pl.pallas_call(run, out_shape=outs, in_specs=[kind[m] for m in space], ou...  16 us
    ppermute x1, waiting for transfers between devices, body(): from_pair = lax.ppermute(q_sum, 'y', PAIR)  13.6 us
    all_to_all x1, waiting for transfers between devices, body(): lax.all_to_all(fold(over_x, 8, 1.0), 'z', split_axis=0, concat_axis=0, ti...  12.3 us
    ppermute x3, starting transfers between devices, body(): lax.ppermute(block, 'y', back_perm(perm))  12 us
    ppermute x4, starting transfers between devices, body(): far = [lax.ppermute(part, 'y', PAIR) for part in near]  11.2 us
    all_to_all x1, starting transfers between devices, body(): lax.all_to_all(fold(over_x, 8, 1.0), 'z', split_axis=0, concat_axis=0, ti...  8.4 us
    ppermute x1, waiting for transfers between devices, body(): lax.ppermute(three, 'y', PERM3)  7.31 us
    ppermute x3, waiting for transfers between devices, body(): lax.ppermute(block, 'y', back_perm(perm))  7.29 us
  transfers between devices with their start and end apart: 17, of which 8 were waited for; matrix products, arithmetic and copies ran while one was open for 0% of the time, Pallas kernels for 5%

profile of v4, /device:TPU:1, one launch (start us, length us, event | category | flops | bytes accessed | tf_op | source)
XLA Modules:
  0.0 142.7 jit_solution(2179234388067069244)
XLA Ops:
  1.3 3.3 %shard_map.95 = (bf16[32,4096]{1,0:T(8,128)(2,1)}, bf16[32,4096]{1,0:T(8,128)(2,1)}, bf16[32,4096]{1,0:T(8,128)(2,1)}, bf16[32,4096]{1,0:T(8,128)(2,1)}, bf16[128,128]{1,0:T(8,128)(2,1)}, /*index=5*/f32[128,128]{1,0:T(8,128)}) custom-call(s32[3]{0:T(128)} %pad_add_fusion.refs_0_, s32[1,128]{1,0:T(1,128)} %bitcast.26, f32[1,128]{1,0:T(1,128)} %bitcast.27, ...), custom_call_target="tpu_custom_call" | custom-call | flops 134217728 | bytes 2097152 | tf_op jit(solution)/shard_map/pallas_call | solution.py:104
  4.6 6.1 %collective-permute-start = (bf16[32,4096]{1,0:T(8,128)(2,1)}, bf16[32,4096]{1,0:T(8,128)(2,1)S(1)}, u32[]{:S(2)}, u32[]{:S(2)}) collective-permute-start(bf16[32,4096]{1,0:T(8,128)(2,1)} %get-tuple-element.27), channel_id=1, source_target_pairs={{0,14},{2,4},{4,2},{6,8},{8,6},{10,12},{12,10},{14,0},{1,15},{3,5}... | collective-permute-start | bytes 786440 | tf_op jit(solution)/shard_map/ppermute | solution.py:306
  10.7 1.9 %collective-permute-start.1 = (bf16[32,4096]{1,0:T(8,128)(2,1)}, bf16[32,4096]{1,0:T(8,128)(2,1)S(1)}, u32[]{:S(2)}, u32[]{:S(2)}) collective-permute-start(bf16[32,4096]{1,0:T(8,128)(2,1)} %get-tuple-element.28), channel_id=1, source_target_pairs={{0,4},{2,14},{4,8},{6,2},{8,12},{10,6},{12,0},{14,10},{1,5},{3,15}... | collective-permute-start | bytes 786440 | tf_op jit(solution)/shard_map/ppermute | solution.py:306
  12.6 6.9 %collective-permute-start.2 = (bf16[32,4096]{1,0:T(8,128)(2,1)}, bf16[32,4096]{1,0:T(8,128)(2,1)S(1)}, u32[]{:S(2)}, u32[]{:S(2)}) collective-permute-start(bf16[32,4096]{1,0:T(8,128)(2,1)} %get-tuple-element.29), channel_id=1, source_target_pairs={{0,10},{2,8},{4,14},{6,12},{8,2},{10,0},{12,6},{14,4},{1,11},{3,9}... | collective-permute-start | bytes 786440 | tf_op jit(solution)/shard_map/ppermute | solution.py:306
  19.5 1.9 %collective-permute-start.4 = (bf16[32,4096]{1,0:T(8,128)(2,1)}, bf16[32,4096]{1,0:T(8,128)(2,1)S(1)}, u32[]{:S(2)}, u32[]{:S(2)}) collective-permute-start(bf16[32,4096]{1,0:T(8,128)(2,1)} %get-tuple-element.26.refs_0_), channel_id=1, source_target_pairs={{0,2},{2,0},{4,6},{6,4},{8,10},{10,8},{12,14},{14,12},{1,3},{3,1},... | collective-permute-start | bytes 786440 | tf_op jit(solution)/shard_map/ppermute | solution.py:307
  21.5 3.4 %collective-permute-start.5 = (bf16[32,4096]{1,0:T(8,128)(2,1)S(1)}, bf16[32,4096]{1,0:T(8,128)(2,1)S(1)}, u32[]{:S(2)}, u32[]{:S(2)}) collective-permute-start(bf16[32,4096]{1,0:T(8,128)(2,1)S(1)} %collective-permute-done.refs_1_), channel_id=1, source_target_pairs={{0,2},{2,0},{4,6},{6,4},{8,10},{10,8},{12,14},{14,12},{1,3},{3,1},... | collective-permute-start | bytes 786440 | tf_op jit(solution)/shard_map/ppermute | solution.py:307
  24.8 1.9 %collective-permute-start.6 = (bf16[32,4096]{1,0:T(8,128)(2,1)S(1)}, bf16[32,4096]{1,0:T(8,128)(2,1)S(1)}, u32[]{:S(2)}, u32[]{:S(2)}) collective-permute-start(bf16[32,4096]{1,0:T(8,128)(2,1)S(1)} %collective-permute-done.1.refs_2_), channel_id=1, source_target_pairs={{0,2},{2,0},{4,6},{6,4},{8,10},{10,8},{12,14},{14,12},{1,3},{3,1},... | collective-permute-start | bytes 786440 | tf_op jit(solution)/shard_map/ppermute | solution.py:307
  26.8 7.3 %collective-permute-done.2.refs_3_ = bf16[32,4096]{1,0:T(8,128)(2,1)S(1)} collective-permute-done((bf16[32,4096]{1,0:T(8,128)(2,1)}, bf16[32,4096]{1,0:T(8,128)(2,1)S(1)}, u32[]{:S(2)}, u32[]{:S(2)}) %collective-permute-start.2) | collective-permute-done | bytes 262176 | tf_op jit(solution)/shard_map/ppermute | solution.py:306
  34.1 4.0 %collective-permute-start.7 = (bf16[32,4096]{1,0:T(8,128)(2,1)S(1)}, bf16[32,4096]{1,0:T(8,128)(2,1)S(1)}, u32[]{:S(2)}, u32[]{:S(2)}) collective-permute-start(bf16[32,4096]{1,0:T(8,128)(2,1)S(1)} %collective-permute-done.2.refs_3_), channel_id=1, source_target_pairs={{0,2},{2,0},{4,6},{6,4},{8,10},{10,8},{12,14},{14,12},{1,3},{3,1},... | collective-permute-start | bytes 786440 | tf_op jit(solution)/shard_map/ppermute | solution.py:307
  38.1 0.9 copy-done.4
  39.1 5.9 %collective-permute-start.3 = (bf16[128,4096]{1,0:T(8,128)(2,1)S(1)}, bf16[128,4096]{1,0:T(8,128)(2,1)S(1)}, u32[]{:S(2)}, u32[]{:S(2)}) collective-permute-start(bf16[128,4096]{1,0:T(8,128)(2,1)S(1)} %shard_map.96.refs_1_.refs_0_), channel_id=1, source_target_pairs={{0,1},{1,0},{2,3},{3,2},{4,5},{5,4},{6,7},{7,6},{8,9},{9,8},{10,11... | collective-permute-start | bytes 3145736 | tf_op jit(solution)/shard_map/ppermute | solution.py:309
  45.0 3.6 %collective-permute-done.7.refs_3_ = bf16[32,4096]{1,0:T(8,128)(2,1)S(1)} collective-permute-done((bf16[32,4096]{1,0:T(8,128)(2,1)S(1)}, bf16[32,4096]{1,0:T(8,128)(2,1)S(1)}, u32[]{:S(2)}, u32[]{:S(2)}) %collective-permute-start.7) | collective-permute-done | bytes 262176 | tf_op jit(solution)/shard_map/ppermute | solution.py:307
  48.7 6.1 %collective-permute-start.8 = (bf16[128,4096]{1,0:T(8,128)(2,1)S(1)}, bf16[128,4096]{1,0:T(8,128)(2,1)S(1)}, u32[]{:S(2)}, u32[]{:S(2)}) collective-permute-start(bf16[128,4096]{1,0:T(8,128)(2,1)S(1)} %shard_map.97.refs_1_.refs_2_), channel_id=1, source_target_pairs={{0,1},{1,0},{2,3},{3,2},{4,5},{5,4},{6,7},{7,6},{8,9},{9,8},{10,11... | collective-permute-start | bytes 3145736 | tf_op jit(solution)/shard_map/ppermute | solution.py:311
  54.8 1.3 shard_map.99
  56.2 2.8 %shard_map.98 = (bf16[256,768]{1,0:T(8,128)(2,1)S(1)}, bf16[128,2048]{1,0:T(8,128)(2,1)S(1)}, bf16[128,2048]{1,0:T(8,128)(2,1)S(1)}) custom-call(s32[1,16]{1,0:T(1,128)S(1)} %copy-done.7, bf16[128,4096]{1,0:T(8,128)(2,1)S(1)} %shard_map.96.refs_1_.refs_0_, bf16[128,4096]{1,0:T(8,128)(2,1)S(1)} %collective-permute-done.3.refs_2_.refs_1_, ...), custom_call_target="tpu_custom_call" | custom-call | flops 1073741824 | bytes 6291456 | tf_op jit(solution)/shard_map/pallas_call | solution.py:104
  59.0 1.3 shard_map.100
  60.4 4.1 %shard_map.101 = bf16[4,8,192,256]{3,2,1,0:T(8,128)(2,1)} custom-call(bf16[128,4096]{1,0:T(8,128)(2,1)S(1)} %shard_map.96.refs_1_.refs_0_, bf16[128,4096]{1,0:T(8,128)(2,1)S(1)} %collective-permute-done.3.refs_2_.refs_1_, bf16[128,4096]{1,0:T(8,128)(2,1)S(1)} %shard_map.97.refs_1_.refs_2_, bf16[128,4096]{1,0:T(8,128)(2,1)} %copy-done.3, ...), custom_call_target="tpu_custom_call" | custom-call | flops 1610612736 | bytes 7340032 | tf_op jit(solution)/shard_map/pallas_call | solution.py:104
  64.5 4.7 %all-to-all-start = ((bf16[4,8,192,256]{3,2,1,0:T(8,128)(2,1)}), bf16[4,8,192,256]{3,2,1,0:T(8,128)(2,1)}, u32[]{:S(2)}, u32[]{:S(2)}) async-start(bf16[4,8,192,256]{3,2,1,0:T(8,128)(2,1)} %shard_map.101), calls=%async_computation | async-start | bytes 6291456 | tf_op jit(solution)/shard_map/all_to_all | solution.py:318
  69.9 1.9 %collective-permute-start.10 = (bf16[128,2048]{1,0:T(8,128)(2,1)S(1)}, bf16[128,2048]{1,0:T(8,128)(2,1)S(1)}, u32[]{:S(2)}, u32[]{:S(2)}) collective-permute-start(bf16[128,2048]{1,0:T(8,128)(2,1)S(1)} %get-tuple-element.38), channel_id=1, source_target_pairs={{0,1},{1,0},{2,3},{3,2},{4,5},{5,4},{6,7},{7,6},{8,9},{9,8},{10,11... | collective-permute-start | bytes 1572872 | tf_op jit(solution)/shard_map/ppermute | solution.py:322
  71.8 2.4 %collective-permute-start.9 = (bf16[128,2048]{1,0:T(8,128)(2,1)S(1)}, bf16[128,2048]{1,0:T(8,128)(2,1)S(1)}, u32[]{:S(2)}, u32[]{:S(2)}) collective-permute-start(bf16[128,2048]{1,0:T(8,128)(2,1)S(1)} %get-tuple-element.34), channel_id=1, source_target_pairs={{0,1},{1,0},{2,3},{3,2},{4,5},{5,4},{6,7},{7,6},{8,9},{9,8},{10,11... | collective-permute-start | bytes 1572872 | tf_op jit(solution)/shard_map/ppermute | solution.py:313
  74.5 1.9 %collective-permute-start.11 = (bf16[128,2048]{1,0:T(8,128)(2,1)S(1)}, bf16[128,2048]{1,0:T(8,128)(2,1)S(1)}, u32[]{:S(2)}, u32[]{:S(2)}) collective-permute-start(bf16[128,2048]{1,0:T(8,128)(2,1)S(1)} %shard_map.103), channel_id=1, source_target_pairs={{0,2},{2,0},{4,6},{6,4},{8,10},{10,8},{12,14},{14,12},{1,3},{3,1},... | collective-permute-start | bytes 1572872 | tf_op jit(solution)/shard_map/ppermute | solution.py:324
  76.4 13.6 %collective-permute-done.11.refs_2_ = bf16[128,2048]{1,0:T(8,128)(2,1)S(1)} collective-permute-done((bf16[128,2048]{1,0:T(8,128)(2,1)S(1)}, bf16[128,2048]{1,0:T(8,128)(2,1)S(1)}, u32[]{:S(2)}, u32[]{:S(2)}) %collective-permute-start.11) | collective-permute-done | bytes 524320 | tf_op jit(solution)/shard_map/ppermute | solution.py:324
  90.9 2.2 %collective-permute-start.12 = (bf16[32,2048]{1,0:T(8,128)(2,1)S(1)}, bf16[32,2048]{1,0:T(8,128)(2,1)S(1)}, u32[]{:S(2)}, u32[]{:S(2)}) collective-permute-start(bf16[32,2048]{1,0:T(8,128)(2,1)S(1)} %get-tuple-element.39), channel_id=1, source_target_pairs={{14,0},{4,2},{2,4},{8,6},{6,8},{12,10},{10,12},{0,14},{15,1},{5,3}... | collective-permute-start | bytes 393224 | tf_op jit(solution)/shard_map/ppermute | solution.py:330
  93.1 4.9 %collective-permute-start.13 = (bf16[32,2048]{1,0:T(8,128)(2,1)S(1)}, bf16[32,2048]{1,0:T(8,128)(2,1)S(1)}, u32[]{:S(2)}, u32[]{:S(2)}) collective-permute-start(bf16[32,2048]{1,0:T(8,128)(2,1)S(1)} %get-tuple-element.40), channel_id=1, source_target_pairs={{4,0},{14,2},{8,4},{2,6},{12,8},{6,10},{0,12},{10,14},{5,1},{15,3}... | collective-permute-start | bytes 393224 | tf_op jit(solution)/shard_map/ppermute | solution.py:330
  98.6 1.5 %collective-permute-done.13.refs_2_ = bf16[32,2048]{1,0:T(8,128)(2,1)S(1)} collective-permute-done((bf16[32,2048]{1,0:T(8,128)(2,1)S(1)}, bf16[32,2048]{1,0:T(8,128)(2,1)S(1)}, u32[]{:S(2)}, u32[]{:S(2)}) %collective-permute-start.13) | collective-permute-done | bytes 131104 | tf_op jit(solution)/shard_map/ppermute | solution.py:330
  100.1 6.8 %all-to-all-done = bf16[4,8,192,256]{3,2,1,0:T(8,128)(2,1)} async-done(((bf16[4,8,192,256]{3,2,1,0:T(8,128)(2,1)}), bf16[4,8,192,256]{3,2,1,0:T(8,128)(2,1)}, u32[]{:S(2)}, u32[]{:S(2)}) %all-to-all-start) | async-done | bytes 3145760 | tf_op jit(solution)/shard_map/all_to_all | solution.py:318
  107.0 3.0 %shard_map.105 = bf16[24,64,256]{2,1,0:T(8,128)(2,1)} custom-call(bf16[4,24,64,256]{3,2,1,0:T(8,128)(2,1)} %bitcast.8.got), custom_call_target="tpu_custom_call" | custom-call | bytes 3145728 | tf_op jit(solution)/shard_map/pallas_call | solution.py:265
  110.0 8.4 %all-to-all-start.1 = ((bf16[8,192,256]{2,1,0:T(8,128)(2,1)}), bf16[8,192,256]{2,1,0:T(8,128)(2,1)S(1)}, u32[]{:S(2)}, u32[]{:S(2)}) async-start(bf16[8,192,256]{2,1,0:T(8,128)(2,1)} %bitcast.9), calls=%async_computation.1 | async-start | bytes 1572864 | tf_op jit(solution)/shard_map/all_to_all | solution.py:333
  118.3 4.9 %collective-permute-start.14 = (bf16[32,2048]{1,0:T(8,128)(2,1)S(1)}, bf16[32,2048]{1,0:T(8,128)(2,1)S(1)}, u32[]{:S(2)}, u32[]{:S(2)}) collective-permute-start(bf16[32,2048]{1,0:T(8,128)(2,1)S(1)} %get-tuple-element.45), channel_id=1, source_target_pairs={{10,0},{8,2},{14,4},{12,6},{2,8},{0,10},{6,12},{4,14},{11,1},{9,3}... | collective-permute-start | bytes 393224 | tf_op jit(solution)/shard_map/ppermute | solution.py:330
  123.3 5.2 %collective-permute-done.14.refs_3_ = bf16[32,2048]{1,0:T(8,128)(2,1)S(1)} collective-permute-done((bf16[32,2048]{1,0:T(8,128)(2,1)S(1)}, bf16[32,2048]{1,0:T(8,128)(2,1)S(1)}, u32[]{:S(2)}, u32[]{:S(2)}) %collective-permute-start.14) | collective-permute-done | bytes 131104 | tf_op jit(solution)/shard_map/ppermute | solution.py:330
  128.5 1.2 shard_map.106
  129.7 12.3 %all-to-all-done.1 = bf16[8,192,256]{2,1,0:T(8,128)(2,1)S(1)} async-done(((bf16[8,192,256]{2,1,0:T(8,128)(2,1)}), bf16[8,192,256]{2,1,0:T(8,128)(2,1)S(1)}, u32[]{:S(2)}, u32[]{:S(2)}) %all-to-all-start.1) | async-done | bytes 786464 | tf_op jit(solution)/shard_map/all_to_all | solution.py:333
  (32 shorter events, 3.9 us)
Async XLA Ops:
  0.6 54.2 %copy-start = (bf16[1,256,2048]{2,1,0:T(8,128)(2,1)S(1)}, bf16[1,256,2048]{2,1,0:T(8,128)(2,1)}, u32[]{:S(2)}) copy-start(bf16[1,256,2048]{2,1,0:T(8,128)(2,1)} %param.14) | copy-start | bytes 3145732
  0.6 54.2 %copy-start.7 = (s32[1,16]{1,0:T(1,128)S(1)}, s32[1,16]{1,0:T(1,128)}, u32[]{:S(2)}) copy-start(s32[1,16]{1,0:T(1,128)} %refs_0_.5) | copy-start | bytes 196
  4.6 50.2 %copy-start.1 = (bf16[1,2048,256]{2,1,0:T(8,128)(2,1)S(1)}, bf16[1,2048,256]{2,1,0:T(8,128)(2,1)}, u32[]{:S(2)}) copy-start(bf16[1,2048,256]{2,1,0:T(8,128)(2,1)} %param.12) | copy-start | bytes 3145732
  4.6 50.2 %copy-start.2 = (bf16[1,2048,256]{2,1,0:T(8,128)(2,1)S(1)}, bf16[1,2048,256]{2,1,0:T(8,128)(2,1)}, u32[]{:S(2)}) copy-start(bf16[1,2048,256]{2,1,0:T(8,128)(2,1)} %param.13) | copy-start | bytes 3145732
  4.6 16.9 %collective-permute-start = (bf16[32,4096]{1,0:T(8,128)(2,1)}, bf16[32,4096]{1,0:T(8,128)(2,1)S(1)}, u32[]{:S(2)}, u32[]{:S(2)}) collective-permute-start(bf16[32,4096]{1,0:T(8,128)(2,1)} %get-tuple-element.27), channel_id=1, source_target_pairs={{0,14},{2,4},{4,2},{6,8},{8,6},{10,12},{12,10},{14,0},{1,15},{3,5}... | collective-permute-start | bytes 786440 | tf_op jit(solution)/shard_map/ppermute | solution.py:306
  10.7 14.2 %collective-permute-start.1 = (bf16[32,4096]{1,0:T(8,128)(2,1)}, bf16[32,4096]{1,0:T(8,128)(2,1)S(1)}, u32[]{:S(2)}, u32[]{:S(2)}) collective-permute-start(bf16[32,4096]{1,0:T(8,128)(2,1)} %get-tuple-element.28), channel_id=1, source_target_pairs={{0,4},{2,14},{4,8},{6,2},{8,12},{10,6},{12,0},{14,10},{1,5},{3,15}... | collective-permute-start | bytes 786440 | tf_op jit(solution)/shard_map/ppermute | solution.py:306
  12.6 21.5 %collective-permute-start.2 = (bf16[32,4096]{1,0:T(8,128)(2,1)}, bf16[32,4096]{1,0:T(8,128)(2,1)S(1)}, u32[]{:S(2)}, u32[]{:S(2)}) collective-permute-start(bf16[32,4096]{1,0:T(8,128)(2,1)} %get-tuple-element.29), channel_id=1, source_target_pairs={{0,10},{2,8},{4,14},{6,12},{8,2},{10,0},{12,6},{14,4},{1,11},{3,9}... | collective-permute-start | bytes 786440 | tf_op jit(solution)/shard_map/ppermute | solution.py:306
  19.5 25.5 %collective-permute-start.4 = (bf16[32,4096]{1,0:T(8,128)(2,1)}, bf16[32,4096]{1,0:T(8,128)(2,1)S(1)}, u32[]{:S(2)}, u32[]{:S(2)}) collective-permute-start(bf16[32,4096]{1,0:T(8,128)(2,1)} %get-tuple-element.26.refs_0_), channel_id=1, source_target_pairs={{0,2},{2,0},{4,6},{6,4},{8,10},{10,8},{12,14},{14,12},{1,3},{3,1},... | collective-permute-start | bytes 786440 | tf_op jit(solution)/shard_map/ppermute | solution.py:307
  21.5 23.5 %collective-permute-start.5 = (bf16[32,4096]{1,0:T(8,128)(2,1)S(1)}, bf16[32,4096]{1,0:T(8,128)(2,1)S(1)}, u32[]{:S(2)}, u32[]{:S(2)}) collective-permute-start(bf16[32,4096]{1,0:T(8,128)(2,1)S(1)} %collective-permute-done.refs_1_), channel_id=1, source_target_pairs={{0,2},{2,0},{4,6},{6,4},{8,10},{10,8},{12,14},{14,12},{1,3},{3,1},... | collective-permute-start | bytes 786440 | tf_op jit(solution)/shard_map/ppermute | solution.py:307
  24.8 20.2 %collective-permute-start.6 = (bf16[32,4096]{1,0:T(8,128)(2,1)S(1)}, bf16[32,4096]{1,0:T(8,128)(2,1)S(1)}, u32[]{:S(2)}, u32[]{:S(2)}) collective-permute-start(bf16[32,4096]{1,0:T(8,128)(2,1)S(1)} %collective-permute-done.1.refs_2_), channel_id=1, source_target_pairs={{0,2},{2,0},{4,6},{6,4},{8,10},{10,8},{12,14},{14,12},{1,3},{3,1},... | collective-permute-start | bytes 786440 | tf_op jit(solution)/shard_map/ppermute | solution.py:307
  34.1 14.5 %collective-permute-start.7 = (bf16[32,4096]{1,0:T(8,128)(2,1)S(1)}, bf16[32,4096]{1,0:T(8,128)(2,1)S(1)}, u32[]{:S(2)}, u32[]{:S(2)}) collective-permute-start(bf16[32,4096]{1,0:T(8,128)(2,1)S(1)} %collective-permute-done.2.refs_3_), channel_id=1, source_target_pairs={{0,2},{2,0},{4,6},{6,4},{8,10},{10,8},{12,14},{14,12},{1,3},{3,1},... | collective-permute-start | bytes 786440 | tf_op jit(solution)/shard_map/ppermute | solution.py:307
  38.0 1.0 copy-start.4
  39.1 17.1 %collective-permute-start.3 = (bf16[128,4096]{1,0:T(8,128)(2,1)S(1)}, bf16[128,4096]{1,0:T(8,128)(2,1)S(1)}, u32[]{:S(2)}, u32[]{:S(2)}) collective-permute-start(bf16[128,4096]{1,0:T(8,128)(2,1)S(1)} %shard_map.96.refs_1_.refs_0_), channel_id=1, source_target_pairs={{0,1},{1,0},{2,3},{3,2},{4,5},{5,4},{6,7},{7,6},{8,9},{9,8},{10,11... | collective-permute-start | bytes 3145736 | tf_op jit(solution)/shard_map/ppermute | solution.py:309
  48.7 10.3 %collective-permute-start.8 = (bf16[128,4096]{1,0:T(8,128)(2,1)S(1)}, bf16[128,4096]{1,0:T(8,128)(2,1)S(1)}, u32[]{:S(2)}, u32[]{:S(2)}) collective-permute-start(bf16[128,4096]{1,0:T(8,128)(2,1)S(1)} %shard_map.97.refs_1_.refs_2_), channel_id=1, source_target_pairs={{0,1},{1,0},{2,3},{3,2},{4,5},{5,4},{6,7},{7,6},{8,9},{9,8},{10,11... | collective-permute-start | bytes 3145736 | tf_op jit(solution)/shard_map/ppermute | solution.py:311
  59.0 1.4 copy-start.3
  64.5 42.5 %all-to-all-start = ((bf16[4,8,192,256]{3,2,1,0:T(8,128)(2,1)}), bf16[4,8,192,256]{3,2,1,0:T(8,128)(2,1)}, u32[]{:S(2)}, u32[]{:S(2)}) async-start(bf16[4,8,192,256]{3,2,1,0:T(8,128)(2,1)} %shard_map.101), calls=%async_computation | async-start | bytes 6291456 | tf_op jit(solution)/shard_map/all_to_all | solution.py:318
  69.9 4.3 %collective-permute-start.10 = (bf16[128,2048]{1,0:T(8,128)(2,1)S(1)}, bf16[128,2048]{1,0:T(8,128)(2,1)S(1)}, u32[]{:S(2)}, u32[]{:S(2)}) collective-permute-start(bf16[128,2048]{1,0:T(8,128)(2,1)S(1)} %get-tuple-element.38), channel_id=1, source_target_pairs={{0,1},{1,0},{2,3},{3,2},{4,5},{5,4},{6,7},{7,6},{8,9},{9,8},{10,11... | collective-permute-start | bytes 1572872 | tf_op jit(solution)/shard_map/ppermute | solution.py:322
  71.8 4.5 %collective-permute-start.9 = (bf16[128,2048]{1,0:T(8,128)(2,1)S(1)}, bf16[128,2048]{1,0:T(8,128)(2,1)S(1)}, u32[]{:S(2)}, u32[]{:S(2)}) collective-permute-start(bf16[128,2048]{1,0:T(8,128)(2,1)S(1)} %get-tuple-element.34), channel_id=1, source_target_pairs={{0,1},{1,0},{2,3},{3,2},{4,5},{5,4},{6,7},{7,6},{8,9},{9,8},{10,11... | collective-permute-start | bytes 1572872 | tf_op jit(solution)/shard_map/ppermute | solution.py:313
  74.5 15.5 %collective-permute-start.11 = (bf16[128,2048]{1,0:T(8,128)(2,1)S(1)}, bf16[128,2048]{1,0:T(8,128)(2,1)S(1)}, u32[]{:S(2)}, u32[]{:S(2)}) collective-permute-start(bf16[128,2048]{1,0:T(8,128)(2,1)S(1)} %shard_map.103), channel_id=1, source_target_pairs={{0,2},{2,0},{4,6},{6,4},{8,10},{10,8},{12,14},{14,12},{1,3},{3,1},... | collective-permute-start | bytes 1572872 | tf_op jit(solution)/shard_map/ppermute | solution.py:324
  90.9 37.6 %copy-start.5 = (f32[128,128]{1,0:T(8,128)S(1)}, f32[128,128]{1,0:T(8,128)}, u32[]{:S(2)}) copy-start(f32[128,128]{1,0:T(8,128)} %get-tuple-element.46.refs_4_) | copy-start | bytes 196612
  90.9 37.6 %copy-start.6 = (bf16[128,128]{1,0:T(8,128)(2,1)S(1)}, bf16[128,128]{1,0:T(8,128)(2,1)}, u32[]{:S(2)}) copy-start(bf16[128,128]{1,0:T(8,128)(2,1)} %get-tuple-element.47.refs_5_) | copy-start | bytes 98308
  90.9 7.7 %collective-permute-start.12 = (bf16[32,2048]{1,0:T(8,128)(2,1)S(1)}, bf16[32,2048]{1,0:T(8,128)(2,1)S(1)}, u32[]{:S(2)}, u32[]{:S(2)}) collective-permute-start(bf16[32,2048]{1,0:T(8,128)(2,1)S(1)} %get-tuple-element.39), channel_id=1, source_target_pairs={{14,0},{4,2},{2,4},{8,6},{6,8},{12,10},{10,12},{0,14},{15,1},{5,3}... | collective-permute-start | bytes 393224 | tf_op jit(solution)/shard_map/ppermute | solution.py:330
  93.1 7.0 %collective-permute-start.13 = (bf16[32,2048]{1,0:T(8,128)(2,1)S(1)}, bf16[32,2048]{1,0:T(8,128)(2,1)S(1)}, u32[]{:S(2)}, u32[]{:S(2)}) collective-permute-start(bf16[32,2048]{1,0:T(8,128)(2,1)S(1)} %get-tuple-element.40), channel_id=1, source_target_pairs={{4,0},{14,2},{8,4},{2,6},{12,8},{6,10},{0,12},{10,14},{5,1},{15,3}... | collective-permute-start | bytes 393224 | tf_op jit(solution)/shard_map/ppermute | solution.py:330
  110.0 32.0 %all-to-all-start.1 = ((bf16[8,192,256]{2,1,0:T(8,128)(2,1)}), bf16[8,192,256]{2,1,0:T(8,128)(2,1)S(1)}, u32[]{:S(2)}, u32[]{:S(2)}) async-start(bf16[8,192,256]{2,1,0:T(8,128)(2,1)} %bitcast.9), calls=%async_computation.1 | async-start | bytes 1572864 | tf_op jit(solution)/shard_map/all_to_all | solution.py:333
  118.3 10.2 %collective-permute-start.14 = (bf16[32,2048]{1,0:T(8,128)(2,1)S(1)}, bf16[32,2048]{1,0:T(8,128)(2,1)S(1)}, u32[]{:S(2)}, u32[]{:S(2)}) collective-permute-start(bf16[32,2048]{1,0:T(8,128)(2,1)S(1)} %get-tuple-element.45), channel_id=1, source_target_pairs={{10,0},{8,2},{14,4},{12,6},{2,8},{0,10},{6,12},{4,14},{11,1},{9,3}... | collective-permute-start | bytes 393224 | tf_op jit(solution)/shard_map/ppermute | solution.py:330

commit v5 on v4

--- a/solution.py
+++ b/solution.py
@@ -123,7 +123,7 @@
 
 def place_kernel(at, ids, gate, tokens, cotangent, own, one, two, three, placer_out, gate_out):
     ids, gate = ids.get(), gate.get()
-    y = at[2]
+    y = at[0]
     odd = y % 2
     pair = y // 2
     rows = ids.shape[1]
@@ -169,23 +169,23 @@
     tile = lax.broadcasted_iota(jnp.int32, (1, HID), 1) // TILE
     for k in range(HID // TILE):
         row = jnp.where(tile == k, touched[0, k].astype(f32), row)
-    for k in range(n):
-        xs = blocks[k][:, :D]
-        ds = blocks[k][:, D:]
-        h = mm(xs, wg[...])
-        u = mm(xs, wu[...])
-        g = mm(ds, wd[...], NT)
-        s = 1.0 / (1.0 + jnp.exp(-h))
-        act = (h * s * u).astype(bf16)
-        here = slice(k * 4 * CAP, (k + 1) * 4 * CAP)
-        if with_out:
-            outs[k].ref[...] = mm(act, wd[...]).astype(bf16)
+    xs = jnp.concatenate([block[:, :D] for block in blocks], axis=0)
+    ds = jnp.concatenate([block[:, D:] for block in blocks], axis=0)
+    h = mm(xs, wg[...])
+    u = mm(xs, wu[...])
+    g = mm(ds, wd[...], NT)
+    s = 1.0 / (1.0 + jnp.exp(-h))
+    act = (h * s * u).astype(bf16)
+    if with_out:
+        made = mm(act, wd[...]).astype(bf16)
+        for k in range(n):
+            outs[k].ref[...] = made[k * 4 * CAP:(k + 1) * 4 * CAP]
             outs[k].send()
-        else:
-            outs[0][here] = act
-        grads[here, :HID] = (g * u * (s * (1.0 + h * (1.0 - s))) * row).astype(bf16)
-        grads[here, HID:2 * HID] = (g * (h * s) * row).astype(bf16)
-        grads[here, 2 * HID:] = (act.astype(f32) * row).astype(bf16)
+    else:
+        outs[0][...] = act
+    grads[:, :HID] = (g * u * (s * (1.0 + h * (1.0 - s))) * row).astype(bf16)
+    grads[:, HID:2 * HID] = (g * (h * s) * row).astype(bf16)
+    grads[:, 2 * HID:] = (act.astype(f32) * row).astype(bf16)
 
 
 def layer(touched, blocks, wg, wu, wd, with_out):
@@ -210,9 +210,12 @@
 STEP = 512
 
 
+PAIRED = 2
+
+
 def delta_kernel(xa, xb, xc, xd, ga, gb, gc, *outs):
     grads = jnp.concatenate([ga[...], gb[...], gc[...]], axis=0)
-    left_over = [Z * SHARE] * X
+    left_over = [PAIRED * SHARE] * len(outs)
     for base, lo, n in ((0, 0, 2), (D, 2 * HID, 1)):
         right = grads[:, lo:lo + n * HID]
         for c0 in range(0, D, STEP):
@@ -224,51 +227,63 @@
                 for rep in range(start // SHARE, (start + STEP - 1) // SHARE + 1):
                     first = max(rep * SHARE, start)
                     last = min((rep + 1) * SHARE, start + STEP)
-                    put = slice(first - rep * SHARE, last - rep * SHARE)
-                    x = rep // Z
-                    outs[x].ref[rep % Z, put, :] = out[first - start:last - start, k * HID:(k + 1) * HID]
-                    left_over[x] -= last - first
-                    if left_over[x] == 0:
-                        outs[x].send()
+                    part, off = rep // PAIRED, (rep // PAIRED) * PAIRED * SHARE
+                    put = slice(first - off, last - off)
+                    outs[part].ref[put, :] = out[first - start:last - start, k * HID:(k + 1) * HID]
+                    left_over[part] -= last - first
+                    if left_over[part] == 0:
+                        outs[part].send()
 
 
 def delta(xs, grads):
-    return call(
-        delta_kernel, shaped(X, Z, SHARE, HID), (*xs, *grads),
+    out = call(
+        delta_kernel, shaped(X * Z // PAIRED, PAIRED * SHARE, HID), (*xs, *grads),
         2 * 3 * 16 * CAP * D * HID, 2 * (16 * CAP * 2 * D + 3 * D * HID), "v" * 7, "p", limit=VMEM_WIDE,
     )
+    return out.reshape(X, Z, SHARE, HID)
 
 
 ROWS = 64
 
 
-def fold_kernel(n, chunks, scale, got, out, total, sems):
+def fold_kernel(n, chunks, scale, staged, got, out, total, sems, *rest):
     per = got.shape[1] // chunks
-    stores = []
-    for c in range(chunks):
+    parts = [pl.ds(c * per, per) for c in range(chunks)]
+    stores, loads = [], []
+    if staged:
+        held, in_sems = rest
+        for c, here in enumerate(parts):
+            loads.append(pltpu.make_async_copy(got.at[:, here], held.at[:, here], in_sems.at[c]))
+            loads[c].start()
+        got = held
+    for c, here in enumerate(parts):
+        if staged:
+            loads[c].wait()
         for i in range(c * per, (c + 1) * per):
             value = got[0, i].astype(f32)
             for k in range(1, n):
                 value += got[k, i].astype(f32)
             total[i] = (value * scale).astype(bf16)
-        here = pl.ds(c * per, per)
         stores.append(pltpu.make_async_copy(total.at[here], out.at[here], sems.at[c]))
         stores[c].start()
     for store in stores:
         store.wait()
 
 
-def fold(got, chunks, scale):
+def fold(got, chunks, scale, staged):
     n = got.shape[0]
     shape = got.shape[1:]
     got = got.reshape(n, -1, ROWS, HID)
+    scratch = [pltpu.VMEM(got.shape[1:], bf16), pltpu.SemaphoreType.DMA((chunks,))]
+    if staged:
+        scratch += [pltpu.VMEM(got.shape, bf16), pltpu.SemaphoreType.DMA((chunks,))]
     out = pl.pallas_call(
-        functools.partial(fold_kernel, n, chunks, scale),
+        functools.partial(fold_kernel, n, chunks, scale, staged),
         out_shape=shaped(*got.shape[1:]),
-        in_specs=[VM],
+        in_specs=[HB if staged else VM],
         out_specs=HB,
-        scratch_shapes=[pltpu.VMEM(got.shape[1:], bf16), pltpu.SemaphoreType.DMA((chunks,))],
-        compiler_params=pltpu.CompilerParams(vmem_limit_bytes=VMEM_WIDE),
+        scratch_shapes=scratch,
+        compiler_params=pltpu.CompilerParams(vmem_limit_bytes=VMEM_WHOLE if staged else VMEM_WIDE),
         cost_estimate=pl.CostEstimate(flops=0, bytes_accessed=2 * got.size, transcendentals=0),
     )(got)
     return out.reshape(shape)
@@ -295,7 +310,7 @@
 
 def body(tokens, expert_ids, gate_prob, cotangent, w_gate, w_up, w_down, touched):
     rows = tokens.shape[0]
-    at = jnp.stack([lax.axis_index("x"), lax.axis_index("z"), lax.axis_index("y")]).astype(jnp.int32)
+    at = lax.axis_index("y").astype(jnp.int32).reshape(1)
     wg, wu, wd = w_gate[0], w_up[0], w_down[0]
     own, one, two, three, placer, gate = call(
         place_kernel,
@@ -330,10 +345,10 @@
         lax.ppermute(block, "y", back_perm(perm)) for block, perm in zip(blocks[1:], (PERM1, PERM2, PERM3))
     ]
     over_x, back[1:3] = lax.optimization_barrier((over_x, back[1:3]))
-    got = lax.all_to_all(fold(over_x, 8, 1.0), "z", split_axis=0, concat_axis=0, tiled=True)
+    got = lax.all_to_all(fold(over_x, 8, 1.0, True), "z", split_axis=0, concat_axis=0, tiled=True)
     mixed = call(mixed_kernel, shaped(rows, D), (*back, gate, placer), 2 * rows * rows * D, 2 * 2 * rows * D)
     got, mixed = lax.optimization_barrier((got, mixed))
-    averaged = fold(got, 3, 1.0 / (X * Z)).T
+    averaged = fold(got, 3, 1.0 / (X * Z), False).T
     return mixed, averaged
 
 

time: 144 us -> 141 us (0.979)
  Pallas kernels: 19.7 us -> 18.1 us
where the time goes in v5:
time: 141 us; the launch traced here: 140 us
  starting transfers between devices  69.5 us (49%)
  waiting for transfers between devices  50.9 us (36%)
  Pallas kernels  18.1 us (13%)
    pallas_call x11, Pallas kernels, call(): pl.pallas_call(run, out_shape=outs, in_specs=[kind[m] for m in space], ou...  14.7 us
    ppermute x1, waiting for transfers between devices, body(): from_pair = lax.ppermute(q_sum, 'y', PAIR)  13.6 us
    all_to_all x1, waiting for transfers between devices, body(): lax.all_to_all(fold(over_x, 8, 1.0, True), 'z', split_axis=0, concat_axis...  12.2 us
    ppermute x3, starting transfers between devices, body(): lax.ppermute(block, 'y', back_perm(perm))  12.1 us
    ppermute x4, starting transfers between devices, body(): far = [lax.ppermute(part, 'y', PAIR) for part in near]  11.2 us
    all_to_all x1, starting transfers between devices, body(): lax.all_to_all(fold(over_x, 8, 1.0, True), 'z', split_axis=0, concat_axis...  8.38 us
    ppermute x1, waiting for transfers between devices, body(): lax.ppermute(three, 'y', PERM3)  7.32 us
    ppermute x3, waiting for transfers between devices, body(): lax.ppermute(block, 'y', back_perm(perm))  7.29 us
  transfers between devices with their start and end apart: 17, of which 8 were waited for; matrix products, arithmetic and copies ran while one was open for 0% of the time, Pallas kernels for 5%

profile of v5, /device:TPU:1, one launch (start us, length us, event | category | flops | bytes accessed | tf_op | source)
XLA Modules:
  0.0 140.4 jit_solution(32108025499525022)
XLA Ops:
  0.7 2.7 %shard_map.95 = (bf16[32,4096]{1,0:T(8,128)(2,1)}, bf16[32,4096]{1,0:T(8,128)(2,1)}, bf16[32,4096]{1,0:T(8,128)(2,1)}, bf16[32,4096]{1,0:T(8,128)(2,1)}, bf16[128,128]{1,0:T(8,128)(2,1)}, /*index=5*/f32[128,128]{1,0:T(8,128)}) custom-call(s32[1]{0:T(128)} %bitcast.refs_0_, s32[1,128]{1,0:T(1,128)} %bitcast.27, f32[1,128]{1,0:T(1,128)} %bitcast.28, ...), custom_call_target="tpu_custom_call" | custom-call | flops 134217728 | bytes 2097152 | tf_op jit(solution)/shard_map/pallas_call | solution.py:104
  3.4 6.1 %collective-permute-start = (bf16[32,4096]{1,0:T(8,128)(2,1)}, bf16[32,4096]{1,0:T(8,128)(2,1)S(1)}, u32[]{:S(2)}, u32[]{:S(2)}) collective-permute-start(bf16[32,4096]{1,0:T(8,128)(2,1)} %get-tuple-element.27), channel_id=1, source_target_pairs={{0,14},{2,4},{4,2},{6,8},{8,6},{10,12},{12,10},{14,0},{1,15},{3,5}... | collective-permute-start | bytes 786440 | tf_op jit(solution)/shard_map/ppermute | solution.py:321
  9.5 1.9 %collective-permute-start.1 = (bf16[32,4096]{1,0:T(8,128)(2,1)}, bf16[32,4096]{1,0:T(8,128)(2,1)S(1)}, u32[]{:S(2)}, u32[]{:S(2)}) collective-permute-start(bf16[32,4096]{1,0:T(8,128)(2,1)} %get-tuple-element.28), channel_id=1, source_target_pairs={{0,4},{2,14},{4,8},{6,2},{8,12},{10,6},{12,0},{14,10},{1,5},{3,15}... | collective-permute-start | bytes 786440 | tf_op jit(solution)/shard_map/ppermute | solution.py:321
  11.4 6.9 %collective-permute-start.2 = (bf16[32,4096]{1,0:T(8,128)(2,1)}, bf16[32,4096]{1,0:T(8,128)(2,1)S(1)}, u32[]{:S(2)}, u32[]{:S(2)}) collective-permute-start(bf16[32,4096]{1,0:T(8,128)(2,1)} %get-tuple-element.29), channel_id=1, source_target_pairs={{0,10},{2,8},{4,14},{6,12},{8,2},{10,0},{12,6},{14,4},{1,11},{3,9}... | collective-permute-start | bytes 786440 | tf_op jit(solution)/shard_map/ppermute | solution.py:321
  18.3 1.9 %collective-permute-start.4 = (bf16[32,4096]{1,0:T(8,128)(2,1)}, bf16[32,4096]{1,0:T(8,128)(2,1)S(1)}, u32[]{:S(2)}, u32[]{:S(2)}) collective-permute-start(bf16[32,4096]{1,0:T(8,128)(2,1)} %get-tuple-element.26.refs_0_), channel_id=1, source_target_pairs={{0,2},{2,0},{4,6},{6,4},{8,10},{10,8},{12,14},{14,12},{1,3},{3,1},... | collective-permute-start | bytes 786440 | tf_op jit(solution)/shard_map/ppermute | solution.py:322
  20.3 3.4 %collective-permute-start.5 = (bf16[32,4096]{1,0:T(8,128)(2,1)S(1)}, bf16[32,4096]{1,0:T(8,128)(2,1)S(1)}, u32[]{:S(2)}, u32[]{:S(2)}) collective-permute-start(bf16[32,4096]{1,0:T(8,128)(2,1)S(1)} %collective-permute-done.refs_1_), channel_id=1, source_target_pairs={{0,2},{2,0},{4,6},{6,4},{8,10},{10,8},{12,14},{14,12},{1,3},{3,1},... | collective-permute-start | bytes 786440 | tf_op jit(solution)/shard_map/ppermute | solution.py:322
  23.7 1.9 %collective-permute-start.6 = (bf16[32,4096]{1,0:T(8,128)(2,1)S(1)}, bf16[32,4096]{1,0:T(8,128)(2,1)S(1)}, u32[]{:S(2)}, u32[]{:S(2)}) collective-permute-start(bf16[32,4096]{1,0:T(8,128)(2,1)S(1)} %collective-permute-done.1.refs_2_), channel_id=1, source_target_pairs={{0,2},{2,0},{4,6},{6,4},{8,10},{10,8},{12,14},{14,12},{1,3},{3,1},... | collective-permute-start | bytes 786440 | tf_op jit(solution)/shard_map/ppermute | solution.py:322
  25.6 7.3 %collective-permute-done.2.refs_3_ = bf16[32,4096]{1,0:T(8,128)(2,1)S(1)} collective-permute-done((bf16[32,4096]{1,0:T(8,128)(2,1)}, bf16[32,4096]{1,0:T(8,128)(2,1)S(1)}, u32[]{:S(2)}, u32[]{:S(2)}) %collective-permute-start.2) | collective-permute-done | bytes 262176 | tf_op jit(solution)/shard_map/ppermute | solution.py:321
  32.9 4.0 %collective-permute-start.7 = (bf16[32,4096]{1,0:T(8,128)(2,1)S(1)}, bf16[32,4096]{1,0:T(8,128)(2,1)S(1)}, u32[]{:S(2)}, u32[]{:S(2)}) collective-permute-start(bf16[32,4096]{1,0:T(8,128)(2,1)S(1)} %collective-permute-done.2.refs_3_), channel_id=1, source_target_pairs={{0,2},{2,0},{4,6},{6,4},{8,10},{10,8},{12,14},{14,12},{1,3},{3,1},... | collective-permute-start | bytes 786440 | tf_op jit(solution)/shard_map/ppermute | solution.py:322
  36.9 0.9 copy-done.4
  37.9 5.8 %collective-permute-start.3 = (bf16[128,4096]{1,0:T(8,128)(2,1)S(1)}, bf16[128,4096]{1,0:T(8,128)(2,1)S(1)}, u32[]{:S(2)}, u32[]{:S(2)}) collective-permute-start(bf16[128,4096]{1,0:T(8,128)(2,1)S(1)} %shard_map.96.refs_1_.refs_0_), channel_id=1, source_target_pairs={{0,1},{1,0},{2,3},{3,2},{4,5},{5,4},{6,7},{7,6},{8,9},{9,8},{10,11... | collective-permute-start | bytes 3145736 | tf_op jit(solution)/shard_map/ppermute | solution.py:324
  43.8 3.6 %collective-permute-done.7.refs_3_ = bf16[32,4096]{1,0:T(8,128)(2,1)S(1)} collective-permute-done((bf16[32,4096]{1,0:T(8,128)(2,1)S(1)}, bf16[32,4096]{1,0:T(8,128)(2,1)S(1)}, u32[]{:S(2)}, u32[]{:S(2)}) %collective-permute-start.7) | collective-permute-done | bytes 262176 | tf_op jit(solution)/shard_map/ppermute | solution.py:322
  47.5 6.1 %collective-permute-start.8 = (bf16[128,4096]{1,0:T(8,128)(2,1)S(1)}, bf16[128,4096]{1,0:T(8,128)(2,1)S(1)}, u32[]{:S(2)}, u32[]{:S(2)}) collective-permute-start(bf16[128,4096]{1,0:T(8,128)(2,1)S(1)} %shard_map.97.refs_1_.refs_2_), channel_id=1, source_target_pairs={{0,1},{1,0},{2,3},{3,2},{4,5},{5,4},{6,7},{7,6},{8,9},{9,8},{10,11... | collective-permute-start | bytes 3145736 | tf_op jit(solution)/shard_map/ppermute | solution.py:326
  53.6 1.3 shard_map.99
  55.0 2.1 %shard_map.98 = (bf16[256,768]{1,0:T(8,128)(2,1)S(1)}, bf16[128,2048]{1,0:T(8,128)(2,1)S(1)}, bf16[128,2048]{1,0:T(8,128)(2,1)S(1)}) custom-call(s32[1,16]{1,0:T(1,128)S(1)} %copy-done.7, bf16[128,4096]{1,0:T(8,128)(2,1)S(1)} %shard_map.96.refs_1_.refs_0_, bf16[128,4096]{1,0:T(8,128)(2,1)S(1)} %collective-permute-done.3.refs_2_.refs_1_, ...), custom_call_target="tpu_custom_call" | custom-call | flops 1073741824 | bytes 6291456 | tf_op jit(solution)/shard_map/pallas_call | solution.py:104
  57.2 1.3 shard_map.100
  58.5 4.1 %shard_map.101 = bf16[16,384,256]{2,1,0:T(8,128)(2,1)} custom-call(bf16[128,4096]{1,0:T(8,128)(2,1)S(1)} %shard_map.96.refs_1_.refs_0_, bf16[128,4096]{1,0:T(8,128)(2,1)S(1)} %collective-permute-done.3.refs_2_.refs_1_, bf16[128,4096]{1,0:T(8,128)(2,1)S(1)} %shard_map.97.refs_1_.refs_2_, bf16[128,4096]{1,0:T(8,128)(2,1)} %copy-done.3, ...), custom_call_target="tpu_custom_call" | custom-call | flops 1610612736 | bytes 7340032 | tf_op jit(solution)/shard_map/pallas_call | solution.py:104
  62.6 4.7 %all-to-all-start = ((bf16[4,8,192,256]{3,2,1,0:T(8,128)(2,1)}), bf16[4,8,192,256]{3,2,1,0:T(8,128)(2,1)}, u32[]{:S(2)}, u32[]{:S(2)}) async-start(bf16[4,8,192,256]{3,2,1,0:T(8,128)(2,1)} %bitcast.24), calls=%async_computation | async-start | bytes 6291456 | tf_op jit(solution)/shard_map/all_to_all | solution.py:333
  68.0 1.9 %collective-permute-start.10 = (bf16[128,2048]{1,0:T(8,128)(2,1)S(1)}, bf16[128,2048]{1,0:T(8,128)(2,1)S(1)}, u32[]{:S(2)}, u32[]{:S(2)}) collective-permute-start(bf16[128,2048]{1,0:T(8,128)(2,1)S(1)} %get-tuple-element.38), channel_id=1, source_target_pairs={{0,1},{1,0},{2,3},{3,2},{4,5},{5,4},{6,7},{7,6},{8,9},{9,8},{10,11... | collective-permute-start | bytes 1572872 | tf_op jit(solution)/shard_map/ppermute | solution.py:337
  69.9 2.4 %collective-permute-start.9 = (bf16[128,2048]{1,0:T(8,128)(2,1)S(1)}, bf16[128,2048]{1,0:T(8,128)(2,1)S(1)}, u32[]{:S(2)}, u32[]{:S(2)}) collective-permute-start(bf16[128,2048]{1,0:T(8,128)(2,1)S(1)} %get-tuple-element.34), channel_id=1, source_target_pairs={{0,1},{1,0},{2,3},{3,2},{4,5},{5,4},{6,7},{7,6},{8,9},{9,8},{10,11... | collective-permute-start | bytes 1572872 | tf_op jit(solution)/shard_map/ppermute | solution.py:328
  72.5 1.9 %collective-permute-start.11 = (bf16[128,2048]{1,0:T(8,128)(2,1)S(1)}, bf16[128,2048]{1,0:T(8,128)(2,1)S(1)}, u32[]{:S(2)}, u32[]{:S(2)}) collective-permute-start(bf16[128,2048]{1,0:T(8,128)(2,1)S(1)} %shard_map.103), channel_id=1, source_target_pairs={{0,2},{2,0},{4,6},{6,4},{8,10},{10,8},{12,14},{14,12},{1,3},{3,1},... | collective-permute-start | bytes 1572872 | tf_op jit(solution)/shard_map/ppermute | solution.py:339
  74.5 13.6 %collective-permute-done.11.refs_2_ = bf16[128,2048]{1,0:T(8,128)(2,1)S(1)} collective-permute-done((bf16[128,2048]{1,0:T(8,128)(2,1)S(1)}, bf16[128,2048]{1,0:T(8,128)(2,1)S(1)}, u32[]{:S(2)}, u32[]{:S(2)}) %collective-permute-start.11) | collective-permute-done | bytes 524320 | tf_op jit(solution)/shard_map/ppermute | solution.py:339
  89.0 2.2 %collective-permute-start.12 = (bf16[32,2048]{1,0:T(8,128)(2,1)S(1)}, bf16[32,2048]{1,0:T(8,128)(2,1)S(1)}, u32[]{:S(2)}, u32[]{:S(2)}) collective-permute-start(bf16[32,2048]{1,0:T(8,128)(2,1)S(1)} %get-tuple-element.39), channel_id=1, source_target_pairs={{14,0},{4,2},{2,4},{8,6},{6,8},{12,10},{10,12},{0,14},{15,1},{5,3}... | collective-permute-start | bytes 393224 | tf_op jit(solution)/shard_map/ppermute | solution.py:345
  91.2 4.9 %collective-permute-start.13 = (bf16[32,2048]{1,0:T(8,128)(2,1)S(1)}, bf16[32,2048]{1,0:T(8,128)(2,1)S(1)}, u32[]{:S(2)}, u32[]{:S(2)}) collective-permute-start(bf16[32,2048]{1,0:T(8,128)(2,1)S(1)} %get-tuple-element.40), channel_id=1, source_target_pairs={{4,0},{14,2},{8,4},{2,6},{12,8},{6,10},{0,12},{10,14},{5,1},{15,3}... | collective-permute-start | bytes 393224 | tf_op jit(solution)/shard_map/ppermute | solution.py:345
  96.7 1.5 %collective-permute-done.13.refs_2_ = bf16[32,2048]{1,0:T(8,128)(2,1)S(1)} collective-permute-done((bf16[32,2048]{1,0:T(8,128)(2,1)S(1)}, bf16[32,2048]{1,0:T(8,128)(2,1)S(1)}, u32[]{:S(2)}, u32[]{:S(2)}) %collective-permute-start.13) | collective-permute-done | bytes 131104 | tf_op jit(solution)/shard_map/ppermute | solution.py:345
  98.2 6.9 %all-to-all-done = bf16[4,8,192,256]{3,2,1,0:T(8,128)(2,1)} async-done(((bf16[4,8,192,256]{3,2,1,0:T(8,128)(2,1)}), bf16[4,8,192,256]{3,2,1,0:T(8,128)(2,1)}, u32[]{:S(2)}, u32[]{:S(2)}) %all-to-all-start) | async-done | bytes 3145760 | tf_op jit(solution)/shard_map/all_to_all | solution.py:333
  105.1 2.6 %shard_map.105 = bf16[24,64,256]{2,1,0:T(8,128)(2,1)} custom-call(bf16[4,24,64,256]{3,2,1,0:T(8,128)(2,1)} %bitcast.7.got), custom_call_target="tpu_custom_call" | custom-call | bytes 3145728 | tf_op jit(solution)/shard_map/pallas_call | solution.py:280
  107.7 8.4 %all-to-all-start.1 = ((bf16[8,192,256]{2,1,0:T(8,128)(2,1)}), bf16[8,192,256]{2,1,0:T(8,128)(2,1)S(1)}, u32[]{:S(2)}, u32[]{:S(2)}) async-start(bf16[8,192,256]{2,1,0:T(8,128)(2,1)} %bitcast.25), calls=%async_computation.1 | async-start | bytes 1572864 | tf_op jit(solution)/shard_map/all_to_all | solution.py:348
  116.1 5.0 %collective-permute-start.14 = (bf16[32,2048]{1,0:T(8,128)(2,1)S(1)}, bf16[32,2048]{1,0:T(8,128)(2,1)S(1)}, u32[]{:S(2)}, u32[]{:S(2)}) collective-permute-start(bf16[32,2048]{1,0:T(8,128)(2,1)S(1)} %get-tuple-element.45), channel_id=1, source_target_pairs={{10,0},{8,2},{14,4},{12,6},{2,8},{0,10},{6,12},{4,14},{11,1},{9,3}... | collective-permute-start | bytes 393224 | tf_op jit(solution)/shard_map/ppermute | solution.py:345
  121.1 5.2 %collective-permute-done.14.refs_3_ = bf16[32,2048]{1,0:T(8,128)(2,1)S(1)} collective-permute-done((bf16[32,2048]{1,0:T(8,128)(2,1)S(1)}, bf16[32,2048]{1,0:T(8,128)(2,1)S(1)}, u32[]{:S(2)}, u32[]{:S(2)}) %collective-permute-start.14) | collective-permute-done | bytes 131104 | tf_op jit(solution)/shard_map/ppermute | solution.py:345
  126.3 1.2 shard_map.106
  127.5 12.2 %all-to-all-done.1 = bf16[8,192,256]{2,1,0:T(8,128)(2,1)S(1)} async-done(((bf16[8,192,256]{2,1,0:T(8,128)(2,1)}), bf16[8,192,256]{2,1,0:T(8,128)(2,1)S(1)}, u32[]{:S(2)}, u32[]{:S(2)}) %all-to-all-start.1) | async-done | bytes 786464 | tf_op jit(solution)/shard_map/all_to_all | solution.py:348
  (31 shorter events, 3.3 us)
Async XLA Ops:
  0.6 53.0 %copy-start = (bf16[1,256,2048]{2,1,0:T(8,128)(2,1)S(1)}, bf16[1,256,2048]{2,1,0:T(8,128)(2,1)}, u32[]{:S(2)}) copy-start(bf16[1,256,2048]{2,1,0:T(8,128)(2,1)} %param.14) | copy-start | bytes 3145732
  0.6 53.0 %copy-start.7 = (s32[1,16]{1,0:T(1,128)S(1)}, s32[1,16]{1,0:T(1,128)}, u32[]{:S(2)}) copy-start(s32[1,16]{1,0:T(1,128)} %refs_0_.5) | copy-start | bytes 196
  3.4 50.2 %copy-start.1 = (bf16[1,2048,256]{2,1,0:T(8,128)(2,1)S(1)}, bf16[1,2048,256]{2,1,0:T(8,128)(2,1)}, u32[]{:S(2)}) copy-start(bf16[1,2048,256]{2,1,0:T(8,128)(2,1)} %param.12) | copy-start | bytes 3145732
  3.4 50.2 %copy-start.2 = (bf16[1,2048,256]{2,1,0:T(8,128)(2,1)S(1)}, bf16[1,2048,256]{2,1,0:T(8,128)(2,1)}, u32[]{:S(2)}) copy-start(bf16[1,2048,256]{2,1,0:T(8,128)(2,1)} %param.13) | copy-start | bytes 3145732
  3.4 16.9 %collective-permute-start = (bf16[32,4096]{1,0:T(8,128)(2,1)}, bf16[32,4096]{1,0:T(8,128)(2,1)S(1)}, u32[]{:S(2)}, u32[]{:S(2)}) collective-permute-start(bf16[32,4096]{1,0:T(8,128)(2,1)} %get-tuple-element.27), channel_id=1, source_target_pairs={{0,14},{2,4},{4,2},{6,8},{8,6},{10,12},{12,10},{14,0},{1,15},{3,5}... | collective-permute-start | bytes 786440 | tf_op jit(solution)/shard_map/ppermute | solution.py:321
  9.5 14.2 %collective-permute-start.1 = (bf16[32,4096]{1,0:T(8,128)(2,1)}, bf16[32,4096]{1,0:T(8,128)(2,1)S(1)}, u32[]{:S(2)}, u32[]{:S(2)}) collective-permute-start(bf16[32,4096]{1,0:T(8,128)(2,1)} %get-tuple-element.28), channel_id=1, source_target_pairs={{0,4},{2,14},{4,8},{6,2},{8,12},{10,6},{12,0},{14,10},{1,5},{3,15}... | collective-permute-start | bytes 786440 | tf_op jit(solution)/shard_map/ppermute | solution.py:321
  11.4 21.5 %collective-permute-start.2 = (bf16[32,4096]{1,0:T(8,128)(2,1)}, bf16[32,4096]{1,0:T(8,128)(2,1)S(1)}, u32[]{:S(2)}, u32[]{:S(2)}) collective-permute-start(bf16[32,4096]{1,0:T(8,128)(2,1)} %get-tuple-element.29), channel_id=1, source_target_pairs={{0,10},{2,8},{4,14},{6,12},{8,2},{10,0},{12,6},{14,4},{1,11},{3,9}... | collective-permute-start | bytes 786440 | tf_op jit(solution)/shard_map/ppermute | solution.py:321
  18.3 25.5 %collective-permute-start.4 = (bf16[32,4096]{1,0:T(8,128)(2,1)}, bf16[32,4096]{1,0:T(8,128)(2,1)S(1)}, u32[]{:S(2)}, u32[]{:S(2)}) collective-permute-start(bf16[32,4096]{1,0:T(8,128)(2,1)} %get-tuple-element.26.refs_0_), channel_id=1, source_target_pairs={{0,2},{2,0},{4,6},{6,4},{8,10},{10,8},{12,14},{14,12},{1,3},{3,1},... | collective-permute-start | bytes 786440 | tf_op jit(solution)/shard_map/ppermute | solution.py:322
  20.3 23.5 %collective-permute-start.5 = (bf16[32,4096]{1,0:T(8,128)(2,1)S(1)}, bf16[32,4096]{1,0:T(8,128)(2,1)S(1)}, u32[]{:S(2)}, u32[]{:S(2)}) collective-permute-start(bf16[32,4096]{1,0:T(8,128)(2,1)S(1)} %collective-permute-done.refs_1_), channel_id=1, source_target_pairs={{0,2},{2,0},{4,6},{6,4},{8,10},{10,8},{12,14},{14,12},{1,3},{3,1},... | collective-permute-start | bytes 786440 | tf_op jit(solution)/shard_map/ppermute | solution.py:322
  23.7 20.2 %collective-permute-start.6 = (bf16[32,4096]{1,0:T(8,128)(2,1)S(1)}, bf16[32,4096]{1,0:T(8,128)(2,1)S(1)}, u32[]{:S(2)}, u32[]{:S(2)}) collective-permute-start(bf16[32,4096]{1,0:T(8,128)(2,1)S(1)} %collective-permute-done.1.refs_2_), channel_id=1, source_target_pairs={{0,2},{2,0},{4,6},{6,4},{8,10},{10,8},{12,14},{14,12},{1,3},{3,1},... | collective-permute-start | bytes 786440 | tf_op jit(solution)/shard_map/ppermute | solution.py:322
  32.9 14.5 %collective-permute-start.7 = (bf16[32,4096]{1,0:T(8,128)(2,1)S(1)}, bf16[32,4096]{1,0:T(8,128)(2,1)S(1)}, u32[]{:S(2)}, u32[]{:S(2)}) collective-permute-start(bf16[32,4096]{1,0:T(8,128)(2,1)S(1)} %collective-permute-done.2.refs_3_), channel_id=1, source_target_pairs={{0,2},{2,0},{4,6},{6,4},{8,10},{10,8},{12,14},{14,12},{1,3},{3,1},... | collective-permute-start | bytes 786440 | tf_op jit(solution)/shard_map/ppermute | solution.py:322
  36.9 1.0 copy-start.4
  37.9 17.1 %collective-permute-start.3 = (bf16[128,4096]{1,0:T(8,128)(2,1)S(1)}, bf16[128,4096]{1,0:T(8,128)(2,1)S(1)}, u32[]{:S(2)}, u32[]{:S(2)}) collective-permute-start(bf16[128,4096]{1,0:T(8,128)(2,1)S(1)} %shard_map.96.refs_1_.refs_0_), channel_id=1, source_target_pairs={{0,1},{1,0},{2,3},{3,2},{4,5},{5,4},{6,7},{7,6},{8,9},{9,8},{10,11... | collective-permute-start | bytes 3145736 | tf_op jit(solution)/shard_map/ppermute | solution.py:324
  47.5 9.7 %collective-permute-start.8 = (bf16[128,4096]{1,0:T(8,128)(2,1)S(1)}, bf16[128,4096]{1,0:T(8,128)(2,1)S(1)}, u32[]{:S(2)}, u32[]{:S(2)}) collective-permute-start(bf16[128,4096]{1,0:T(8,128)(2,1)S(1)} %shard_map.97.refs_1_.refs_2_), channel_id=1, source_target_pairs={{0,1},{1,0},{2,3},{3,2},{4,5},{5,4},{6,7},{7,6},{8,9},{9,8},{10,11... | collective-permute-start | bytes 3145736 | tf_op jit(solution)/shard_map/ppermute | solution.py:326
  57.2 1.4 copy-start.3
  62.6 42.5 %all-to-all-start = ((bf16[4,8,192,256]{3,2,1,0:T(8,128)(2,1)}), bf16[4,8,192,256]{3,2,1,0:T(8,128)(2,1)}, u32[]{:S(2)}, u32[]{:S(2)}) async-start(bf16[4,8,192,256]{3,2,1,0:T(8,128)(2,1)} %bitcast.24), calls=%async_computation | async-start | bytes 6291456 | tf_op jit(solution)/shard_map/all_to_all | solution.py:333
  68.0 4.3 %collective-permute-start.10 = (bf16[128,2048]{1,0:T(8,128)(2,1)S(1)}, bf16[128,2048]{1,0:T(8,128)(2,1)S(1)}, u32[]{:S(2)}, u32[]{:S(2)}) collective-permute-start(bf16[128,2048]{1,0:T(8,128)(2,1)S(1)} %get-tuple-element.38), channel_id=1, source_target_pairs={{0,1},{1,0},{2,3},{3,2},{4,5},{5,4},{6,7},{7,6},{8,9},{9,8},{10,11... | collective-permute-start | bytes 1572872 | tf_op jit(solution)/shard_map/ppermute | solution.py:337
  69.9 4.6 %collective-permute-start.9 = (bf16[128,2048]{1,0:T(8,128)(2,1)S(1)}, bf16[128,2048]{1,0:T(8,128)(2,1)S(1)}, u32[]{:S(2)}, u32[]{:S(2)}) collective-permute-start(bf16[128,2048]{1,0:T(8,128)(2,1)S(1)} %get-tuple-element.34), channel_id=1, source_target_pairs={{0,1},{1,0},{2,3},{3,2},{4,5},{5,4},{6,7},{7,6},{8,9},{9,8},{10,11... | collective-permute-start | bytes 1572872 | tf_op jit(solution)/shard_map/ppermute | solution.py:328
  72.5 15.5 %collective-permute-start.11 = (bf16[128,2048]{1,0:T(8,128)(2,1)S(1)}, bf16[128,2048]{1,0:T(8,128)(2,1)S(1)}, u32[]{:S(2)}, u32[]{:S(2)}) collective-permute-start(bf16[128,2048]{1,0:T(8,128)(2,1)S(1)} %shard_map.103), channel_id=1, source_target_pairs={{0,2},{2,0},{4,6},{6,4},{8,10},{10,8},{12,14},{14,12},{1,3},{3,1},... | collective-permute-start | bytes 1572872 | tf_op jit(solution)/shard_map/ppermute | solution.py:339
  89.0 37.3 %copy-start.5 = (f32[128,128]{1,0:T(8,128)S(1)}, f32[128,128]{1,0:T(8,128)}, u32[]{:S(2)}) copy-start(f32[128,128]{1,0:T(8,128)} %get-tuple-element.46.refs_4_) | copy-start | bytes 196612
  89.0 37.3 %copy-start.6 = (bf16[128,128]{1,0:T(8,128)(2,1)S(1)}, bf16[128,128]{1,0:T(8,128)(2,1)}, u32[]{:S(2)}) copy-start(bf16[128,128]{1,0:T(8,128)(2,1)} %get-tuple-element.47.refs_5_) | copy-start | bytes 98308
  89.0 7.7 %collective-permute-start.12 = (bf16[32,2048]{1,0:T(8,128)(2,1)S(1)}, bf16[32,2048]{1,0:T(8,128)(2,1)S(1)}, u32[]{:S(2)}, u32[]{:S(2)}) collective-permute-start(bf16[32,2048]{1,0:T(8,128)(2,1)S(1)} %get-tuple-element.39), channel_id=1, source_target_pairs={{14,0},{4,2},{2,4},{8,6},{6,8},{12,10},{10,12},{0,14},{15,1},{5,3}... | collective-permute-start | bytes 393224 | tf_op jit(solution)/shard_map/ppermute | solution.py:345
  91.2 7.0 %collective-permute-start.13 = (bf16[32,2048]{1,0:T(8,128)(2,1)S(1)}, bf16[32,2048]{1,0:T(8,128)(2,1)S(1)}, u32[]{:S(2)}, u32[]{:S(2)}) collective-permute-start(bf16[32,2048]{1,0:T(8,128)(2,1)S(1)} %get-tuple-element.40), channel_id=1, source_target_pairs={{4,0},{14,2},{8,4},{2,6},{12,8},{6,10},{0,12},{10,14},{5,1},{15,3}... | collective-permute-start | bytes 393224 | tf_op jit(solution)/shard_map/ppermute | solution.py:345
  107.7 32.0 %all-to-all-start.1 = ((bf16[8,192,256]{2,1,0:T(8,128)(2,1)}), bf16[8,192,256]{2,1,0:T(8,128)(2,1)S(1)}, u32[]{:S(2)}, u32[]{:S(2)}) async-start(bf16[8,192,256]{2,1,0:T(8,128)(2,1)} %bitcast.25), calls=%async_computation.1 | async-start | bytes 1572864 | tf_op jit(solution)/shard_map/all_to_all | solution.py:348
  116.1 10.2 %collective-permute-start.14 = (bf16[32,2048]{1,0:T(8,128)(2,1)S(1)}, bf16[32,2048]{1,0:T(8,128)(2,1)S(1)}, u32[]{:S(2)}, u32[]{:S(2)}) collective-permute-start(bf16[32,2048]{1,0:T(8,128)(2,1)S(1)} %get-tuple-element.45), channel_id=1, source_target_pairs={{10,0},{8,2},{14,4},{12,6},{2,8},{0,10},{6,12},{4,14},{11,1},{9,3}... | collective-permute-start | bytes 393224 | tf_op jit(solution)/shard_map/ppermute | solution.py:345

commit v6 on v5

--- a/solution.py
+++ b/solution.py
@@ -200,6 +200,22 @@
     )
 
 
+def near_kernel(touched, a, b, c, d, wg, wu, wd, mine, grads, out):
+    join_kernel(a, b, c, d, mine)
+    layer_kernel(1, True, touched, mine, wg, wu, wd, grads, out)
+
+
+def join_layer(touched, parts, wg, wu, wd):
+    rows = 4 * CAP
+    return call(
+        near_kernel,
+        (shaped(rows, 2 * D), shaped(rows, 3 * HID), shaped(rows, D)),
+        (touched, *parts, wg, wu, wd),
+        2 * 4 * rows * D * HID, 2 * (3 * D * HID + rows * 5 * D),
+        "s" + "v" * 7, "vvh",
+    )
+
+
 def out_kernel(mine, mates, wd, out_mine, out_mates):
     out_mates.ref[...] = mm(mates[...], wd[...]).astype(bf16)
     out_mates.send()
@@ -213,8 +229,8 @@
 PAIRED = 2
 
 
-def delta_kernel(xa, xb, xc, xd, ga, gb, gc, *outs):
-    grads = jnp.concatenate([ga[...], gb[...], gc[...]], axis=0)
+def delta_kernel(xa, xb, xc, xd, ga, gb, gc, gd, *outs):
+    grads = jnp.concatenate([ga[...], gb[...], gc[...], gd[...]], axis=0)
     left_over = [PAIRED * SHARE] * len(outs)
     for base, lo, n in ((0, 0, 2), (D, 2 * HID, 1)):
         right = grads[:, lo:lo + n * HID]
@@ -238,7 +254,7 @@
 def delta(xs, grads):
     out = call(
         delta_kernel, shaped(X * Z // PAIRED, PAIRED * SHARE, HID), (*xs, *grads),
-        2 * 3 * 16 * CAP * D * HID, 2 * (16 * CAP * 2 * D + 3 * D * HID), "v" * 7, "p", limit=VMEM_WIDE,
+        2 * 3 * 16 * CAP * D * HID, 2 * (16 * CAP * 2 * D + 3 * D * HID), "v" * 8, "p", limit=VMEM_WIDE,
     )
     return out.reshape(X, Z, SHARE, HID)
 
@@ -320,16 +336,16 @@
     )
     near = [own, lax.ppermute(one, "y", PERM1), lax.ppermute(two, "y", PERM2), lax.ppermute(three, "y", PERM3)]
     far = [lax.ppermute(part, "y", PAIR) for part in near]
-    mine = join(near)
+    mine, ga, p_mine = join_layer(touched, near, wg, wu, wd)
     mates = lax.ppermute(mine, "c", SWAP)
     pair_mine = join(far)
     pair_mates = lax.ppermute(pair_mine, "c", SWAP)
-    ga, p_mine, p_mates = layer(touched, (mine, mates), wg, wu, wd, True)
+    gb, p_mates = layer(touched, (mates,), wg, wu, wd, True)
     p_got = lax.ppermute(p_mates, "c", SWAP)
     gc, act_mine = layer(touched, (pair_mine,), wg, wu, wd, False)
     gd, act_mates = layer(touched, (pair_mates,), wg, wu, wd, False)
 
-    deltas = delta((mine, mates, pair_mine, pair_mates), (ga, gc, gd))
+    deltas = delta((mine, mates, pair_mine, pair_mates), (ga, gb, gc, gd))
     over_x = lax.all_to_all(deltas, "x", split_axis=0, concat_axis=0, tiled=True)
     q_mine, q_mates = call(
         out_kernel, (shaped(4 * CAP, D),) * 2, (act_mine, act_mates, wd), 0, 0, "vvv", "hh"

time: 141 us -> 140 us (level)
  local copies, waits for them, and re-layouts: 0.98 us -> 5.29 us
  waiting for transfers between devices: 50.9 us -> 47.3 us
  starting transfers between devices: 69.5 us -> 67.1 us
    unnamed x16 -> x20, local copies, waits for them, and re-layouts: 0.98 us -> 5.29 us
    ppermute x4, waiting for transfers between devices: 3.6 us -> 0.01 us  [body(): far = [lax.ppermute(part, 'y', PAIR) for part in near]]
    ppermute x1, starting transfers between devices: 6.11 us -> 3.87 us  [body(): pair_mates = lax.ppermute(pair_mine, 'c', SWAP)]
  transfers between devices with their start and end apart: 17 -> 17, of which waited for: 8 -> 7; matrix products, arithmetic and copies ran while one was open for 0% -> 0% of each run, Pallas kernels for 5% -> 5%
where the time goes in v6:
time: 140 us
  starting transfers between devices  67.1 us (48%)
  waiting for transfers between devices  47.3 us (34%)
  Pallas kernels  18.9 us (13%)
  local copies, waits for them, and re-layouts  5.29 us (4%)
    pallas_call x11, Pallas kernels, call(): pl.pallas_call(run, out_shape=outs, in_specs=[kind[m] for m in space], ou...  15.5 us
    ppermute x1, waiting for transfers between devices, body(): from_pair = lax.ppermute(q_sum, 'y', PAIR)  13.6 us
    all_to_all x1, waiting for transfers between devices, body(): lax.all_to_all(fold(over_x, 8, 1.0, True), 'z', split_axis=0, concat_axis...  12.2 us
    ppermute x3, starting transfers between devices, body(): lax.ppermute(block, 'y', back_perm(perm))  12.1 us
    ppermute x4, starting transfers between devices, body(): far = [lax.ppermute(part, 'y', PAIR) for part in near]  11.2 us
    all_to_all x1, starting transfers between devices, body(): lax.all_to_all(fold(over_x, 8, 1.0, True), 'z', split_axis=0, concat_axis...  8.39 us
    ppermute x1, waiting for transfers between devices, body(): lax.ppermute(three, 'y', PERM3)  7.32 us
    ppermute x3, waiting for transfers between devices, body(): lax.ppermute(block, 'y', back_perm(perm))  7.3 us
  transfers between devices with their start and end apart: 17, of which 7 were waited for; matrix products, arithmetic and copies ran while one was open for 0% of the time, Pallas kernels for 5%

profile of v6, /device:TPU:1, one launch (start us, length us, event | category | flops | bytes accessed | tf_op | source)
XLA Modules:
  0.0 139.6 jit_solution(6492532064615236158)
XLA Ops:
  0.6 2.6 %shard_map.95 = (bf16[32,4096]{1,0:T(8,128)(2,1)}, bf16[32,4096]{1,0:T(8,128)(2,1)}, bf16[32,4096]{1,0:T(8,128)(2,1)}, bf16[32,4096]{1,0:T(8,128)(2,1)}, bf16[128,128]{1,0:T(8,128)(2,1)}, /*index=5*/f32[128,128]{1,0:T(8,128)}) custom-call(s32[1]{0:T(128)} %bitcast.refs_0_, s32[1,128]{1,0:T(1,128)} %bitcast.30, f32[1,128]{1,0:T(1,128)} %bitcast.31, ...), custom_call_target="tpu_custom_call" | custom-call | flops 134217728 | bytes 2097152 | tf_op jit(solution)/shard_map/pallas_call | solution.py:104
  3.3 5.9 %collective-permute-start = (bf16[32,4096]{1,0:T(8,128)(2,1)}, bf16[32,4096]{1,0:T(8,128)(2,1)S(1)}, u32[]{:S(2)}, u32[]{:S(2)}) collective-permute-start(bf16[32,4096]{1,0:T(8,128)(2,1)} %get-tuple-element.29), channel_id=1, source_target_pairs={{0,14},{2,4},{4,2},{6,8},{8,6},{10,12},{12,10},{14,0},{1,15},{3,5}... | collective-permute-start | bytes 786440 | tf_op jit(solution)/shard_map/ppermute | solution.py:337
  9.2 1.9 %collective-permute-start.1 = (bf16[32,4096]{1,0:T(8,128)(2,1)}, bf16[32,4096]{1,0:T(8,128)(2,1)S(1)}, u32[]{:S(2)}, u32[]{:S(2)}) collective-permute-start(bf16[32,4096]{1,0:T(8,128)(2,1)} %get-tuple-element.30), channel_id=1, source_target_pairs={{0,4},{2,14},{4,8},{6,2},{8,12},{10,6},{12,0},{14,10},{1,5},{3,15}... | collective-permute-start | bytes 786440 | tf_op jit(solution)/shard_map/ppermute | solution.py:337
  11.1 6.9 %collective-permute-start.2 = (bf16[32,4096]{1,0:T(8,128)(2,1)}, bf16[32,4096]{1,0:T(8,128)(2,1)S(1)}, u32[]{:S(2)}, u32[]{:S(2)}) collective-permute-start(bf16[32,4096]{1,0:T(8,128)(2,1)} %get-tuple-element.31), channel_id=1, source_target_pairs={{0,10},{2,8},{4,14},{6,12},{8,2},{10,0},{12,6},{14,4},{1,11},{3,9}... | collective-permute-start | bytes 786440 | tf_op jit(solution)/shard_map/ppermute | solution.py:337
  18.1 1.9 %collective-permute-start.4 = (bf16[32,4096]{1,0:T(8,128)(2,1)}, bf16[32,4096]{1,0:T(8,128)(2,1)S(1)}, u32[]{:S(2)}, u32[]{:S(2)}) collective-permute-start(bf16[32,4096]{1,0:T(8,128)(2,1)} %get-tuple-element.28.refs_1_), channel_id=1, source_target_pairs={{0,2},{2,0},{4,6},{6,4},{8,10},{10,8},{12,14},{14,12},{1,3},{3,1},... | collective-permute-start | bytes 786440 | tf_op jit(solution)/shard_map/ppermute | solution.py:338
  20.0 3.4 %collective-permute-start.5 = (bf16[32,4096]{1,0:T(8,128)(2,1)S(1)}, bf16[32,4096]{1,0:T(8,128)(2,1)S(1)}, u32[]{:S(2)}, u32[]{:S(2)}) collective-permute-start(bf16[32,4096]{1,0:T(8,128)(2,1)S(1)} %collective-permute-done.refs_2_), channel_id=1, source_target_pairs={{0,2},{2,0},{4,6},{6,4},{8,10},{10,8},{12,14},{14,12},{1,3},{3,1},... | collective-permute-start | bytes 786440 | tf_op jit(solution)/shard_map/ppermute | solution.py:338
  23.4 1.9 %collective-permute-start.6 = (bf16[32,4096]{1,0:T(8,128)(2,1)S(1)}, bf16[32,4096]{1,0:T(8,128)(2,1)S(1)}, u32[]{:S(2)}, u32[]{:S(2)}) collective-permute-start(bf16[32,4096]{1,0:T(8,128)(2,1)S(1)} %collective-permute-done.1.refs_3_), channel_id=1, source_target_pairs={{0,2},{2,0},{4,6},{6,4},{8,10},{10,8},{12,14},{14,12},{1,3},{3,1},... | collective-permute-start | bytes 786440 | tf_op jit(solution)/shard_map/ppermute | solution.py:338
  25.3 7.3 %collective-permute-done.2.refs_4_ = bf16[32,4096]{1,0:T(8,128)(2,1)S(1)} collective-permute-done((bf16[32,4096]{1,0:T(8,128)(2,1)}, bf16[32,4096]{1,0:T(8,128)(2,1)S(1)}, u32[]{:S(2)}, u32[]{:S(2)}) %collective-permute-start.2) | collective-permute-done | bytes 262176 | tf_op jit(solution)/shard_map/ppermute | solution.py:337
  32.6 4.0 %collective-permute-start.7 = (bf16[32,4096]{1,0:T(8,128)(2,1)S(1)}, bf16[32,4096]{1,0:T(8,128)(2,1)S(1)}, u32[]{:S(2)}, u32[]{:S(2)}) collective-permute-start(bf16[32,4096]{1,0:T(8,128)(2,1)S(1)} %collective-permute-done.2.refs_4_), channel_id=1, source_target_pairs={{0,2},{2,0},{4,6},{6,4},{8,10},{10,8},{12,14},{14,12},{1,3},{3,1},... | collective-permute-start | bytes 786440 | tf_op jit(solution)/shard_map/ppermute | solution.py:338
  37.8 1.2 copy-done.2
  39.1 1.2 copy-done.4
  41.9 1.6 %shard_map.96 = (bf16[128,4096]{1,0:T(8,128)(2,1)S(1)}, bf16[128,768]{1,0:T(8,128)(2,1)S(1)}, bf16[128,2048]{1,0:T(8,128)(2,1)S(1)}) custom-call(s32[1,16]{1,0:T(1,128)S(1)} %copy-done.9, bf16[32,4096]{1,0:T(8,128)(2,1)S(1)} %copy-done.6, bf16[32,4096]{1,0:T(8,128)(2,1)S(1)} %collective-permute-done.refs_2_, ...), custom_call_target="tpu_custom_call" | custom-call | flops 536870912 | bytes 5767168 | tf_op jit(solution)/shard_map/pallas_call | solution.py:104
  43.5 5.9 %collective-permute-start.3 = (bf16[128,4096]{1,0:T(8,128)(2,1)S(1)}, bf16[128,4096]{1,0:T(8,128)(2,1)S(1)}, u32[]{:S(2)}, u32[]{:S(2)}) collective-permute-start(bf16[128,4096]{1,0:T(8,128)(2,1)S(1)} %get-tuple-element.32.refs_0_), channel_id=1, source_target_pairs={{0,1},{1,0},{2,3},{3,2},{4,5},{5,4},{6,7},{7,6},{8,9},{9,8},{10,11... | collective-permute-start | bytes 3145736 | tf_op jit(solution)/shard_map/ppermute | solution.py:340
  49.5 3.9 %collective-permute-start.8 = (bf16[128,4096]{1,0:T(8,128)(2,1)S(1)}, bf16[128,4096]{1,0:T(8,128)(2,1)S(1)}, u32[]{:S(2)}, u32[]{:S(2)}) collective-permute-start(bf16[128,4096]{1,0:T(8,128)(2,1)S(1)} %shard_map.97.refs_1_.refs_2_), channel_id=1, source_target_pairs={{0,1},{1,0},{2,3},{3,2},{4,5},{5,4},{6,7},{7,6},{8,9},{9,8},{10,11... | collective-permute-start | bytes 3145736 | tf_op jit(solution)/shard_map/ppermute | solution.py:342
  53.4 1.3 shard_map.99
  54.7 1.6 %shard_map.98 = (bf16[128,768]{1,0:T(8,128)(2,1)S(1)}, bf16[128,2048]{1,0:T(8,128)(2,1)S(1)}) custom-call(s32[1,16]{1,0:T(1,128)S(1)} %copy-done.9, bf16[128,4096]{1,0:T(8,128)(2,1)S(1)} %collective-permute-done.3.refs_1_, bf16[2048,256]{1,0:T(8,128)(2,1)S(1)} %bitcast.20, bf16[2048,256]{1,0:T(8,128)(2,1)S(1)} %bitcast.24, bf16[256,2048]{1,0:T(8,128)(2,1)S(1)} %bitcast.15), custom_call_target="tpu_custom_call" | custom-call | flops 536870912 | bytes 4718592 | tf_op jit(solution)/shard_map/pallas_call | solution.py:104
  56.3 1.3 shard_map.100
  57.7 4.1 %shard_map.101 = bf16[16,384,256]{2,1,0:T(8,128)(2,1)} custom-call(bf16[128,4096]{1,0:T(8,128)(2,1)S(1)} %get-tuple-element.32.refs_0_, bf16[128,4096]{1,0:T(8,128)(2,1)S(1)} %collective-permute-done.3.refs_1_, bf16[128,4096]{1,0:T(8,128)(2,1)S(1)} %shard_map.97.refs_1_.refs_2_, bf16[128,4096]{1,0:T(8,128)(2,1)} %copy-done.5, ...), custom_call_target="tpu_custom_call" | custom-call | flops 1610612736 | bytes 7340032 | tf_op jit(solution)/shard_map/pallas_call | solution.py:104
  61.7 4.7 %all-to-all-start = ((bf16[4,8,192,256]{3,2,1,0:T(8,128)(2,1)}), bf16[4,8,192,256]{3,2,1,0:T(8,128)(2,1)}, u32[]{:S(2)}, u32[]{:S(2)}) async-start(bf16[4,8,192,256]{3,2,1,0:T(8,128)(2,1)} %bitcast.27), calls=%async_computation | async-start | bytes 6291456 | tf_op jit(solution)/shard_map/all_to_all | solution.py:349
  67.1 1.9 %collective-permute-start.10 = (bf16[128,2048]{1,0:T(8,128)(2,1)S(1)}, bf16[128,2048]{1,0:T(8,128)(2,1)S(1)}, u32[]{:S(2)}, u32[]{:S(2)}) collective-permute-start(bf16[128,2048]{1,0:T(8,128)(2,1)S(1)} %get-tuple-element.42), channel_id=1, source_target_pairs={{0,1},{1,0},{2,3},{3,2},{4,5},{5,4},{6,7},{7,6},{8,9},{9,8},{10,11... | collective-permute-start | bytes 1572872 | tf_op jit(solution)/shard_map/ppermute | solution.py:353
  69.1 2.4 %collective-permute-start.9 = (bf16[128,2048]{1,0:T(8,128)(2,1)S(1)}, bf16[128,2048]{1,0:T(8,128)(2,1)S(1)}, u32[]{:S(2)}, u32[]{:S(2)}) collective-permute-start(bf16[128,2048]{1,0:T(8,128)(2,1)S(1)} %get-tuple-element.38), channel_id=1, source_target_pairs={{0,1},{1,0},{2,3},{3,2},{4,5},{5,4},{6,7},{7,6},{8,9},{9,8},{10,11... | collective-permute-start | bytes 1572872 | tf_op jit(solution)/shard_map/ppermute | solution.py:344
  71.7 1.9 %collective-permute-start.11 = (bf16[128,2048]{1,0:T(8,128)(2,1)S(1)}, bf16[128,2048]{1,0:T(8,128)(2,1)S(1)}, u32[]{:S(2)}, u32[]{:S(2)}) collective-permute-start(bf16[128,2048]{1,0:T(8,128)(2,1)S(1)} %shard_map.103), channel_id=1, source_target_pairs={{0,2},{2,0},{4,6},{6,4},{8,10},{10,8},{12,14},{14,12},{1,3},{3,1},... | collective-permute-start | bytes 1572872 | tf_op jit(solution)/shard_map/ppermute | solution.py:355
  73.6 13.6 %collective-permute-done.11.refs_2_ = bf16[128,2048]{1,0:T(8,128)(2,1)S(1)} collective-permute-done((bf16[128,2048]{1,0:T(8,128)(2,1)S(1)}, bf16[128,2048]{1,0:T(8,128)(2,1)S(1)}, u32[]{:S(2)}, u32[]{:S(2)}) %collective-permute-start.11) | collective-permute-done | bytes 524320 | tf_op jit(solution)/shard_map/ppermute | solution.py:355
  88.2 2.2 %collective-permute-start.12 = (bf16[32,2048]{1,0:T(8,128)(2,1)S(1)}, bf16[32,2048]{1,0:T(8,128)(2,1)S(1)}, u32[]{:S(2)}, u32[]{:S(2)}) collective-permute-start(bf16[32,2048]{1,0:T(8,128)(2,1)S(1)} %get-tuple-element.43), channel_id=1, source_target_pairs={{14,0},{4,2},{2,4},{8,6},{6,8},{12,10},{10,12},{0,14},{15,1},{5,3}... | collective-permute-start | bytes 393224 | tf_op jit(solution)/shard_map/ppermute | solution.py:361
  90.4 4.9 %collective-permute-start.13 = (bf16[32,2048]{1,0:T(8,128)(2,1)S(1)}, bf16[32,2048]{1,0:T(8,128)(2,1)S(1)}, u32[]{:S(2)}, u32[]{:S(2)}) collective-permute-start(bf16[32,2048]{1,0:T(8,128)(2,1)S(1)} %get-tuple-element.44), channel_id=1, source_target_pairs={{4,0},{14,2},{8,4},{2,6},{12,8},{6,10},{0,12},{10,14},{5,1},{15,3}... | collective-permute-start | bytes 393224 | tf_op jit(solution)/shard_map/ppermute | solution.py:361
  95.9 1.5 %collective-permute-done.13.refs_2_ = bf16[32,2048]{1,0:T(8,128)(2,1)S(1)} collective-permute-done((bf16[32,2048]{1,0:T(8,128)(2,1)S(1)}, bf16[32,2048]{1,0:T(8,128)(2,1)S(1)}, u32[]{:S(2)}, u32[]{:S(2)}) %collective-permute-start.13) | collective-permute-done | bytes 131104 | tf_op jit(solution)/shard_map/ppermute | solution.py:361
  97.4 6.8 %all-to-all-done = bf16[4,8,192,256]{3,2,1,0:T(8,128)(2,1)} async-done(((bf16[4,8,192,256]{3,2,1,0:T(8,128)(2,1)}), bf16[4,8,192,256]{3,2,1,0:T(8,128)(2,1)}, u32[]{:S(2)}, u32[]{:S(2)}) %all-to-all-start) | async-done | bytes 3145760 | tf_op jit(solution)/shard_map/all_to_all | solution.py:349
  104.2 2.6 %shard_map.105 = bf16[24,64,256]{2,1,0:T(8,128)(2,1)} custom-call(bf16[4,24,64,256]{3,2,1,0:T(8,128)(2,1)} %bitcast.7.got), custom_call_target="tpu_custom_call" | custom-call | bytes 3145728 | tf_op jit(solution)/shard_map/pallas_call | solution.py:296
  106.9 8.4 %all-to-all-start.1 = ((bf16[8,192,256]{2,1,0:T(8,128)(2,1)}), bf16[8,192,256]{2,1,0:T(8,128)(2,1)S(1)}, u32[]{:S(2)}, u32[]{:S(2)}) async-start(bf16[8,192,256]{2,1,0:T(8,128)(2,1)} %bitcast.28), calls=%async_computation.1 | async-start | bytes 1572864 | tf_op jit(solution)/shard_map/all_to_all | solution.py:364
  115.2 4.9 %collective-permute-start.14 = (bf16[32,2048]{1,0:T(8,128)(2,1)S(1)}, bf16[32,2048]{1,0:T(8,128)(2,1)S(1)}, u32[]{:S(2)}, u32[]{:S(2)}) collective-permute-start(bf16[32,2048]{1,0:T(8,128)(2,1)S(1)} %get-tuple-element.49), channel_id=1, source_target_pairs={{10,0},{8,2},{14,4},{12,6},{2,8},{0,10},{6,12},{4,14},{11,1},{9,3}... | collective-permute-start | bytes 393224 | tf_op jit(solution)/shard_map/ppermute | solution.py:361
  120.2 5.2 %collective-permute-done.14.refs_3_ = bf16[32,2048]{1,0:T(8,128)(2,1)S(1)} collective-permute-done((bf16[32,2048]{1,0:T(8,128)(2,1)S(1)}, bf16[32,2048]{1,0:T(8,128)(2,1)S(1)}, u32[]{:S(2)}, u32[]{:S(2)}) %collective-permute-start.14) | collective-permute-done | bytes 131104 | tf_op jit(solution)/shard_map/ppermute | solution.py:361
  126.6 12.2 %all-to-all-done.1 = bf16[8,192,256]{2,1,0:T(8,128)(2,1)S(1)} async-done(((bf16[8,192,256]{2,1,0:T(8,128)(2,1)}), bf16[8,192,256]{2,1,0:T(8,128)(2,1)S(1)}, u32[]{:S(2)}, u32[]{:S(2)}) %all-to-all-start.1) | async-done | bytes 786464 | tf_op jit(solution)/shard_map/all_to_all | solution.py:364
  (35 shorter events, 7.2 us)
Async XLA Ops:
  3.3 16.7 %collective-permute-start = (bf16[32,4096]{1,0:T(8,128)(2,1)}, bf16[32,4096]{1,0:T(8,128)(2,1)S(1)}, u32[]{:S(2)}, u32[]{:S(2)}) collective-permute-start(bf16[32,4096]{1,0:T(8,128)(2,1)} %get-tuple-element.29), channel_id=1, source_target_pairs={{0,14},{2,4},{4,2},{6,8},{8,6},{10,12},{12,10},{14,0},{1,15},{3,5}... | collective-permute-start | bytes 786440 | tf_op jit(solution)/shard_map/ppermute | solution.py:337
  9.2 14.2 %collective-permute-start.1 = (bf16[32,4096]{1,0:T(8,128)(2,1)}, bf16[32,4096]{1,0:T(8,128)(2,1)S(1)}, u32[]{:S(2)}, u32[]{:S(2)}) collective-permute-start(bf16[32,4096]{1,0:T(8,128)(2,1)} %get-tuple-element.30), channel_id=1, source_target_pairs={{0,4},{2,14},{4,8},{6,2},{8,12},{10,6},{12,0},{14,10},{1,5},{3,15}... | collective-permute-start | bytes 786440 | tf_op jit(solution)/shard_map/ppermute | solution.py:337
  11.1 21.5 %collective-permute-start.2 = (bf16[32,4096]{1,0:T(8,128)(2,1)}, bf16[32,4096]{1,0:T(8,128)(2,1)S(1)}, u32[]{:S(2)}, u32[]{:S(2)}) collective-permute-start(bf16[32,4096]{1,0:T(8,128)(2,1)} %get-tuple-element.31), channel_id=1, source_target_pairs={{0,10},{2,8},{4,14},{6,12},{8,2},{10,0},{12,6},{14,4},{1,11},{3,9}... | collective-permute-start | bytes 786440 | tf_op jit(solution)/shard_map/ppermute | solution.py:337
  18.1 31.3 %collective-permute-start.4 = (bf16[32,4096]{1,0:T(8,128)(2,1)}, bf16[32,4096]{1,0:T(8,128)(2,1)S(1)}, u32[]{:S(2)}, u32[]{:S(2)}) collective-permute-start(bf16[32,4096]{1,0:T(8,128)(2,1)} %get-tuple-element.28.refs_1_), channel_id=1, source_target_pairs={{0,2},{2,0},{4,6},{6,4},{8,10},{10,8},{12,14},{14,12},{1,3},{3,1},... | collective-permute-start | bytes 786440 | tf_op jit(solution)/shard_map/ppermute | solution.py:338
  20.0 29.4 %collective-permute-start.5 = (bf16[32,4096]{1,0:T(8,128)(2,1)S(1)}, bf16[32,4096]{1,0:T(8,128)(2,1)S(1)}, u32[]{:S(2)}, u32[]{:S(2)}) collective-permute-start(bf16[32,4096]{1,0:T(8,128)(2,1)S(1)} %collective-permute-done.refs_2_), channel_id=1, source_target_pairs={{0,2},{2,0},{4,6},{6,4},{8,10},{10,8},{12,14},{14,12},{1,3},{3,1},... | collective-permute-start | bytes 786440 | tf_op jit(solution)/shard_map/ppermute | solution.py:338
  23.4 26.0 %collective-permute-start.6 = (bf16[32,4096]{1,0:T(8,128)(2,1)S(1)}, bf16[32,4096]{1,0:T(8,128)(2,1)S(1)}, u32[]{:S(2)}, u32[]{:S(2)}) collective-permute-start(bf16[32,4096]{1,0:T(8,128)(2,1)S(1)} %collective-permute-done.1.refs_3_), channel_id=1, source_target_pairs={{0,2},{2,0},{4,6},{6,4},{8,10},{10,8},{12,14},{14,12},{1,3},{3,1},... | collective-permute-start | bytes 786440 | tf_op jit(solution)/shard_map/ppermute | solution.py:338
  32.6 16.7 %collective-permute-start.7 = (bf16[32,4096]{1,0:T(8,128)(2,1)S(1)}, bf16[32,4096]{1,0:T(8,128)(2,1)S(1)}, u32[]{:S(2)}, u32[]{:S(2)}) collective-permute-start(bf16[32,4096]{1,0:T(8,128)(2,1)S(1)} %collective-permute-done.2.refs_4_), channel_id=1, source_target_pairs={{0,2},{2,0},{4,6},{6,4},{8,10},{10,8},{12,14},{14,12},{1,3},{3,1},... | collective-permute-start | bytes 786440 | tf_op jit(solution)/shard_map/ppermute | solution.py:338
  36.6 1.2 copy-start
  37.8 1.2 copy-start.2
  39.1 1.2 copy-start.4
  40.3 0.9 copy-start.6
  41.2 0.7 copy-start.9
  41.9 11.5 %copy-start.1 = (bf16[1,256,2048]{2,1,0:T(8,128)(2,1)S(1)}, bf16[1,256,2048]{2,1,0:T(8,128)(2,1)}, u32[]{:S(2)}) copy-start(bf16[1,256,2048]{2,1,0:T(8,128)(2,1)} %param.14) | copy-start | bytes 3145732
  41.9 11.5 %copy-start.3 = (bf16[1,2048,256]{2,1,0:T(8,128)(2,1)S(1)}, bf16[1,2048,256]{2,1,0:T(8,128)(2,1)}, u32[]{:S(2)}) copy-start(bf16[1,2048,256]{2,1,0:T(8,128)(2,1)} %param.12) | copy-start | bytes 3145732
  43.5 11.3 %collective-permute-start.3 = (bf16[128,4096]{1,0:T(8,128)(2,1)S(1)}, bf16[128,4096]{1,0:T(8,128)(2,1)S(1)}, u32[]{:S(2)}, u32[]{:S(2)}) collective-permute-start(bf16[128,4096]{1,0:T(8,128)(2,1)S(1)} %get-tuple-element.32.refs_0_), channel_id=1, source_target_pairs={{0,1},{1,0},{2,3},{3,2},{4,5},{5,4},{6,7},{7,6},{8,9},{9,8},{10,11... | collective-permute-start | bytes 3145736 | tf_op jit(solution)/shard_map/ppermute | solution.py:340
  49.5 6.8 %collective-permute-start.8 = (bf16[128,4096]{1,0:T(8,128)(2,1)S(1)}, bf16[128,4096]{1,0:T(8,128)(2,1)S(1)}, u32[]{:S(2)}, u32[]{:S(2)}) collective-permute-start(bf16[128,4096]{1,0:T(8,128)(2,1)S(1)} %shard_map.97.refs_1_.refs_2_), channel_id=1, source_target_pairs={{0,1},{1,0},{2,3},{3,2},{4,5},{5,4},{6,7},{7,6},{8,9},{9,8},{10,11... | collective-permute-start | bytes 3145736 | tf_op jit(solution)/shard_map/ppermute | solution.py:342
  56.3 1.4 copy-start.5
  61.7 42.5 %all-to-all-start = ((bf16[4,8,192,256]{3,2,1,0:T(8,128)(2,1)}), bf16[4,8,192,256]{3,2,1,0:T(8,128)(2,1)}, u32[]{:S(2)}, u32[]{:S(2)}) async-start(bf16[4,8,192,256]{3,2,1,0:T(8,128)(2,1)} %bitcast.27), calls=%async_computation | async-start | bytes 6291456 | tf_op jit(solution)/shard_map/all_to_all | solution.py:349
  67.1 4.3 %collective-permute-start.10 = (bf16[128,2048]{1,0:T(8,128)(2,1)S(1)}, bf16[128,2048]{1,0:T(8,128)(2,1)S(1)}, u32[]{:S(2)}, u32[]{:S(2)}) collective-permute-start(bf16[128,2048]{1,0:T(8,128)(2,1)S(1)} %get-tuple-element.42), channel_id=1, source_target_pairs={{0,1},{1,0},{2,3},{3,2},{4,5},{5,4},{6,7},{7,6},{8,9},{9,8},{10,11... | collective-permute-start | bytes 1572872 | tf_op jit(solution)/shard_map/ppermute | solution.py:353
  69.1 4.6 %collective-permute-start.9 = (bf16[128,2048]{1,0:T(8,128)(2,1)S(1)}, bf16[128,2048]{1,0:T(8,128)(2,1)S(1)}, u32[]{:S(2)}, u32[]{:S(2)}) collective-permute-start(bf16[128,2048]{1,0:T(8,128)(2,1)S(1)} %get-tuple-element.38), channel_id=1, source_target_pairs={{0,1},{1,0},{2,3},{3,2},{4,5},{5,4},{6,7},{7,6},{8,9},{9,8},{10,11... | collective-permute-start | bytes 1572872 | tf_op jit(solution)/shard_map/ppermute | solution.py:344
  71.7 15.5 %collective-permute-start.11 = (bf16[128,2048]{1,0:T(8,128)(2,1)S(1)}, bf16[128,2048]{1,0:T(8,128)(2,1)S(1)}, u32[]{:S(2)}, u32[]{:S(2)}) collective-permute-start(bf16[128,2048]{1,0:T(8,128)(2,1)S(1)} %shard_map.103), channel_id=1, source_target_pairs={{0,2},{2,0},{4,6},{6,4},{8,10},{10,8},{12,14},{14,12},{1,3},{3,1},... | collective-permute-start | bytes 1572872 | tf_op jit(solution)/shard_map/ppermute | solution.py:355
  88.1 37.3 %copy-start.7 = (f32[128,128]{1,0:T(8,128)S(1)}, f32[128,128]{1,0:T(8,128)}, u32[]{:S(2)}) copy-start(f32[128,128]{1,0:T(8,128)} %get-tuple-element.50.refs_4_) | copy-start | bytes 196612
  88.2 37.3 %copy-start.8 = (bf16[128,128]{1,0:T(8,128)(2,1)S(1)}, bf16[128,128]{1,0:T(8,128)(2,1)}, u32[]{:S(2)}) copy-start(bf16[128,128]{1,0:T(8,128)(2,1)} %get-tuple-element.51.refs_5_) | copy-start | bytes 98308
  88.2 7.7 %collective-permute-start.12 = (bf16[32,2048]{1,0:T(8,128)(2,1)S(1)}, bf16[32,2048]{1,0:T(8,128)(2,1)S(1)}, u32[]{:S(2)}, u32[]{:S(2)}) collective-permute-start(bf16[32,2048]{1,0:T(8,128)(2,1)S(1)} %get-tuple-element.43), channel_id=1, source_target_pairs={{14,0},{4,2},{2,4},{8,6},{6,8},{12,10},{10,12},{0,14},{15,1},{5,3}... | collective-permute-start | bytes 393224 | tf_op jit(solution)/shard_map/ppermute | solution.py:361
  90.4 7.0 %collective-permute-start.13 = (bf16[32,2048]{1,0:T(8,128)(2,1)S(1)}, bf16[32,2048]{1,0:T(8,128)(2,1)S(1)}, u32[]{:S(2)}, u32[]{:S(2)}) collective-permute-start(bf16[32,2048]{1,0:T(8,128)(2,1)S(1)} %get-tuple-element.44), channel_id=1, source_target_pairs={{4,0},{14,2},{8,4},{2,6},{12,8},{6,10},{0,12},{10,14},{5,1},{15,3}... | collective-permute-start | bytes 393224 | tf_op jit(solution)/shard_map/ppermute | solution.py:361
  106.9 32.0 %all-to-all-start.1 = ((bf16[8,192,256]{2,1,0:T(8,128)(2,1)}), bf16[8,192,256]{2,1,0:T(8,128)(2,1)S(1)}, u32[]{:S(2)}, u32[]{:S(2)}) async-start(bf16[8,192,256]{2,1,0:T(8,128)(2,1)} %bitcast.28), calls=%async_computation.1 | async-start | bytes 1572864 | tf_op jit(solution)/shard_map/all_to_all | solution.py:364
  115.2 10.2 %collective-permute-start.14 = (bf16[32,2048]{1,0:T(8,128)(2,1)S(1)}, bf16[32,2048]{1,0:T(8,128)(2,1)S(1)}, u32[]{:S(2)}, u32[]{:S(2)}) collective-permute-start(bf16[32,2048]{1,0:T(8,128)(2,1)S(1)} %get-tuple-element.49), channel_id=1, source_target_pairs={{10,0},{8,2},{14,4},{12,6},{2,8},{0,10},{6,12},{4,14},{11,1},{9,3}... | collective-permute-start | bytes 393224 | tf_op jit(solution)/shard_map/ppermute | solution.py:361
